TPU v7x, 32 devices: a whole 2x2x4 slice. The times are simulated.
32 devices in a mesh: rows: 8 (over z, x), cols: 4 (over y, core).
Axes of the slice: x: 2, y: 2, z: 4, core: 2. Of those that a mesh axis runs over, the one named last changes fastest.
Arguments:
- vectors: bfloat16 [32768, 1024], P('rows'), may hold values from -6 to 6
- near_tiles: bfloat16 [128, 16, 256, 256], P(('rows', 'cols')), may hold values from -0.09375 to 0.09375
- near_cols: int32 [128, 16], P(('rows', 'cols')), may hold values from 0 to 19, as said below
- left_one: bfloat16 [32768, 512], P('rows', 'cols'), may hold values from -0.25 to 0.25
- right_one: bfloat16 [32768, 512], P('rows', 'cols'), may hold values from -0.046875 to 0.046875
- left_two: bfloat16 [32768, 512], P('rows', 'cols'), may hold values from -0.25 to 0.25
- right_two: bfloat16 [32768, 512], P('rows', 'cols'), may hold values from -0.0625 to 0.0625
Outputs:
- product: bfloat16 [32768, 1024], P(('rows', 'cols'))
Inputs may be any that keep to these rules, and one draw needn't show every extreme that they name: `near_cols`: each row names 16 different column tiles of its window of 20.
All inputs are finite; a program needn't handle non-finite values.
Results may differ from a plain program's by a relative error of at most 0.014.
Values may be sent and summed in bfloat16 or wider, within the bound.
No kernel may reach another device: no remote copies, remote signals or barrier semaphores. Data moves between devices by JAX's collectives and lax.ppermute only.
A program may use at most 192 MiB of HBM per device.

v0:
```python
import jax
import jax.numpy as jnp
from jax import lax
from jax.sharding import PartitionSpec as P

B = 256
REACH = 2


def padded(x, sides, width):
    for axis, dim in sides:
        devices, length = (lax.axis_size(axis), x.shape[dim])
        up = [(i, (i + 1) % devices) for i in range(devices - 1)]
        down = [(j, i) for i, j in up]
        last = lax.slice_in_dim(x, length - width, length, axis=dim)
        initial = lax.slice_in_dim(x, 0, width, axis=dim)
        before = lax.ppermute(last, axis, up)
        after = lax.ppermute(initial, axis, down)
        x = jnp.concatenate([before, x, after], axis=dim)
    return x


def partner(value, axis, stride):
    mask = 2**stride
    pairs = [(source, source ^ mask) for source in range(lax.axis_size(axis))]
    return lax.ppermute(value, axis, pairs)


def per_device(vectors, near_tiles, near_cols, left_one, right_one, left_two, right_two):
    vector_count = vectors.shape[1]
    levels = lax.axis_size("rows").bit_length() - 1
    extended = padded(vectors, (("rows", 0),), REACH * B)
    blocks = extended.reshape(extended.shape[0] // B, B, vector_count)
    picked = blocks[near_cols]
    near_part = jnp.einsum("tkab,tkbn->tan", near_tiles, picked, preferred_element_type=jnp.float32)
    near_part = near_part.reshape(-1, vector_count)
    proj_one = jnp.einsum("mr,mn->rn", right_one, vectors, preferred_element_type=jnp.float32)
    proj_two = jnp.einsum("mr,mn->rn", right_two, vectors, preferred_element_type=jnp.float32)
    acc_one = proj_one
    for level_bit in range(levels - 1):
        acc_one = acc_one + partner(acc_one.astype(jnp.bfloat16), "rows", level_bit).astype(
            acc_one.dtype
        )
    far_one = partner(acc_one.astype(jnp.bfloat16), "rows", levels - 1).astype(acc_one.dtype)
    acc_two = proj_two
    for level_bit in range(levels - 2):
        acc_two = acc_two + partner(acc_two.astype(jnp.bfloat16), "rows", level_bit).astype(
            acc_two.dtype
        )
    far_two = partner(acc_two.astype(jnp.bfloat16), "rows", levels - 2).astype(acc_two.dtype)
    coeff_one = far_one.astype(jnp.bfloat16)
    second_coefficient = far_two.astype(jnp.bfloat16)
    panel_one, panel_two = (
        lax.all_to_all(left_one, "cols", split_axis=0, concat_axis=1, tiled=True),
        lax.all_to_all(left_two, "cols", split_axis=0, concat_axis=1, tiled=True),
    )
    whole_one, whole_two = (
        lax.all_gather(coeff_one, "cols", axis=0, tiled=True),
        lax.all_gather(second_coefficient, "cols", axis=0, tiled=True),
    )
    lowrank = jnp.dot(panel_one, whole_one, preferred_element_type=jnp.float32) + jnp.dot(
        panel_two, whole_two, preferred_element_type=jnp.float32
    )
    return (near_part + lowrank).astype(jnp.bfloat16)


def solution(mesh):
    placed = (
        P("rows", None),
        P(("rows", "cols"), None, None, None),
        P(("rows", "cols"), None),
        P("rows", "cols"),
        P("rows", "cols"),
        P("rows", "cols"),
        P("rows", "cols"),
    )
    return jax.shard_map(
        per_device, mesh=mesh, in_specs=placed, out_specs=P(("rows", "cols"), None), check_vma=False
    )
```

profile of v0, /device:TPU:0, one launch (start us, length us, event | category | flops | bytes accessed | tf_op | source)
XLA Modules:
  0.0 159.7 jit_solution(10019204013991232347)
XLA Ops:
  6.5 0.0 copy-start
  6.5 0.0 copy-start.2
  6.5 1.2 copy-done
  7.8 4.7 %fusion.3 = (bf16[128,1024]{1,0:T(8,128)(2,1)S(1)}, f32[128,1024]{1,0:T(8,128)S(1)}) fusion(bf16[4096,128]{1,0:T(8,128)(2,1)S(1)} %copy-done, bf16[4096,1024]{1,0:T(8,128)(2,1)} %param.7), kind=kOutput, calls=%fused_computation.11 | convolution fusion | flops 1073872896 | bytes 10223616 | tf_op jit(solution)/shard_map/mr,mn->rn/dot_general | solution.py:38
  12.4 3.0 %collective-permute-start.5 = (bf16[128,1024]{1,0:T(8,128)(2,1)S(1)}, bf16[128,1024]{1,0:T(8,128)(2,1)S(1)}, u32[]{:S(2)}, u32[]{:S(2)}) collective-permute-start(bf16[128,1024]{1,0:T(8,128)(2,1)S(1)} %get-tuple-element.7), channel_id=1, source_target_pairs={{0,4},{4,0},{8,12},{12,8},{16,20},{20,16},{24,28},{28,24},{1,5},{5... | collective-permute-start | bytes 786440 | tf_op jit(solution)/shard_map/ppermute | solution.py:26
  15.4 6.3 %collective-permute-done.5 = bf16[128,1024]{1,0:T(8,128)(2,1)S(1)} collective-permute-done((bf16[128,1024]{1,0:T(8,128)(2,1)S(1)}, bf16[128,1024]{1,0:T(8,128)(2,1)S(1)}, u32[]{:S(2)}, u32[]{:S(2)}) %collective-permute-start.5) | collective-permute-done | bytes 262176 | tf_op jit(solution)/shard_map/ppermute | solution.py:26
  21.7 0.1 add_convert_fusion
  21.8 1.9 %collective-permute-start.6 = (bf16[128,1024]{1,0:T(8,128)(2,1)S(1)}, bf16[128,1024]{1,0:T(8,128)(2,1)S(1)}, u32[]{:S(2)}, u32[]{:S(2)}) collective-permute-start(bf16[128,1024]{1,0:T(8,128)(2,1)S(1)} %add_convert_fusion), channel_id=1, source_target_pairs={{0,8},{4,12},{8,0},{12,4},{16,24},{20,28},{24,16},{28,20},{1,9},{5... | collective-permute-start | bytes 786440 | tf_op jit(solution)/shard_map/ppermute | solution.py:26
  23.7 3.5 %all-to-all-start.1 = ((bf16[4,1024,128]{2,1,0:T(8,128)(2,1)}), bf16[4,1024,128]{2,1,0:T(8,128)(2,1)S(1)}, u32[]{:S(2)}, u32[]{:S(2)}) async-start(bf16[4,1024,128]{2,1,0:T(8,128)(2,1)} %bitcast.35), calls=%async_computation.1 | async-start | bytes 2097152 | tf_op jit(solution)/shard_map/all_to_all | solution.py:55
  27.2 0.0 all-gather.5.cloned.1.call-start
  27.3 2.1 %collective-permute-done.6 = bf16[128,1024]{1,0:T(8,128)(2,1)S(1)} collective-permute-done((bf16[128,1024]{1,0:T(8,128)(2,1)S(1)}, bf16[128,1024]{1,0:T(8,128)(2,1)S(1)}, u32[]{:S(2)}, u32[]{:S(2)}) %collective-permute-start.6) | collective-permute-done | bytes 262176 | tf_op jit(solution)/shard_map/ppermute | solution.py:26
  29.4 0.0 copy-start.3
  29.4 0.7 copy-done.3
  30.1 0.0 all-gather.5.cloned.1.call-update
  30.1 0.0 copy-done.2
  30.1 4.7 %fusion.4 = (bf16[128,1024]{1,0:T(8,128)(2,1)S(1)}, f32[128,1024]{1,0:T(8,128)S(1)}) fusion(bf16[4096,128]{1,0:T(8,128)(2,1)S(1)} %copy-done.2, bf16[4096,1024]{1,0:T(8,128)(2,1)} %param.7), kind=kOutput, calls=%fused_computation.12 | convolution fusion | flops 1073872896 | bytes 10223616 | tf_op jit(solution)/shard_map/mr,mn->rn/dot_general | solution.py:37
  34.8 0.0 copy-start.5
  34.8 1.5 collective-permute-start.2
  36.3 3.1 %fusion.2 = (bf16[512,1024]{1,0:T(8,128)(2,1)}, bf16[512,1024]{1,0:T(8,128)(2,1)}) fusion(bf16[4096,1024]{1,0:T(8,128)(2,1)} %param.7), kind=kLoop, calls=%fused_computation.10 | loop fusion | bytes 4194304 | tf_op jit(solution)/shard_map/slice | solution.py:15
  39.4 1.3 collective-permute-start.1
  40.7 5.5 %collective-permute-start = (bf16[512,1024]{1,0:T(8,128)(2,1)}, bf16[512,1024]{1,0:T(8,128)(2,1)}, u32[]{:S(2)}, u32[]{:S(2)}) collective-permute-start(bf16[512,1024]{1,0:T(8,128)(2,1)} %get-tuple-element.5), channel_id=1, source_target_pairs={{0,4},{4,8},{8,12},{12,16},{16,20},{20,24},{24,28},{1,5},{5,9},{9,... | collective-permute-start | bytes 3145736 | tf_op jit(solution)/shard_map/ppermute | solution.py:17
  46.2 0.0 collective-permute-done.2
  46.2 0.1 fusion.1
  46.3 0.7 collective-permute-start.3
  46.9 0.0 all-to-all-done.1
  46.9 3.5 %all-to-all-start = ((bf16[4,1024,128]{2,1,0:T(8,128)(2,1)}), bf16[4,1024,128]{2,1,0:T(8,128)(2,1)S(1)}, u32[]{:S(2)}, u32[]{:S(2)}) async-start(bf16[4,1024,128]{2,1,0:T(8,128)(2,1)} %bitcast.36), calls=%async_computation | async-start | bytes 2097152 | tf_op jit(solution)/shard_map/all_to_all | solution.py:54
  50.5 0.2 all-gather.3.cloned.1.call-start
  50.7 19.6 %collective-permute-done.3 = bf16[128,1024]{1,0:T(8,128)(2,1)S(1)} collective-permute-done((bf16[128,1024]{1,0:T(8,128)(2,1)S(1)}, bf16[128,1024]{1,0:T(8,128)(2,1)S(1)}, u32[]{:S(2)}, u32[]{:S(2)}) %collective-permute-start.3) | collective-permute-done | bytes 262176 | tf_op jit(solution)/shard_map/ppermute | solution.py:26
  70.3 0.1 add_convert_fusion.1
  70.4 4.7 %collective-permute-start.4 = (bf16[128,1024]{1,0:T(8,128)(2,1)S(1)}, bf16[128,1024]{1,0:T(8,128)(2,1)S(1)}, u32[]{:S(2)}, u32[]{:S(2)}) collective-permute-start(bf16[128,1024]{1,0:T(8,128)(2,1)S(1)} %add_convert_fusion.1), channel_id=1, source_target_pairs={{0,16},{4,20},{8,24},{12,28},{16,0},{20,4},{24,8},{28,12},{1,17},{... | collective-permute-start | bytes 786440 | tf_op jit(solution)/shard_map/ppermute | solution.py:26
  75.1 0.0 copy-done.5
  75.1 0.1 reshape.16
  75.2 6.7 %collective-permute-done.4 = bf16[128,1024]{1,0:T(8,128)(2,1)S(1)} collective-permute-done((bf16[128,1024]{1,0:T(8,128)(2,1)S(1)}, bf16[128,1024]{1,0:T(8,128)(2,1)S(1)}, u32[]{:S(2)}, u32[]{:S(2)}) %collective-permute-start.4) | collective-permute-done | bytes 262176 | tf_op jit(solution)/shard_map/ppermute | solution.py:26
  81.9 0.0 copy-start.4
  81.9 0.7 copy-done.4
  82.6 0.0 all-gather.3.cloned.1.call-update
  82.6 0.5 copy.13
  83.2 0.0 all-to-all-done
  83.2 1.3 copy.12
  84.5 0.0 collective-permute-done.1
  84.5 1.7 %collective-permute-done = bf16[512,1024]{1,0:T(8,128)(2,1)} collective-permute-done((bf16[512,1024]{1,0:T(8,128)(2,1)}, bf16[512,1024]{1,0:T(8,128)(2,1)}, u32[]{:S(2)}, u32[]{:S(2)}) %collective-permute-start) | collective-permute-done | bytes 1048608 | tf_op jit(solution)/shard_map/ppermute | solution.py:17
  86.2 13.6 %pad_maximum_fusion = bf16[5120,1024]{1,0:T(8,128)(2,1)} fusion(bf16[512,1024]{1,0:T(8,128)(2,1)} %collective-permute-done.1, bf16[4096,1024]{1,0:T(8,128)(2,1)} %param.7, bf16[512,1024]{1,0:T(8,128)(2,1)} %collective-permute-done), kind=kLoop, calls=%fused_computation.1 | loop fusion | flops 31457280 | bytes 20971520 | tf_op jit(solution)/shard_map/concatenate | solution.py:19
  99.7 16.4 %gather_fusion = bf16[64,256,1024]{2,1,0:T(8,128)(2,1)} fusion(bf16[20,256,1024]{2,1,0:T(8,128)(2,1)} %bitcast.28, s32[1024]{0:T(1024)S(1)} %pad_clamp_fusion), kind=kCustom, calls=%fused_computation | custom fusion | bytes 67109120 | tf_op jit(solution)/shard_map/gather | solution.py:34
  116.2 18.8 %fusion.6 = f32[4,1024,256,1]{1,2,3,0:T(8,128)} fusion(bf16[4,16,256,256]{3,2,1,0:T(8,128)(2,1)} %param.8, bf16[4,16,256,1024]{3,2,1,0:T(8,128)(2,1)} %bitcast.29), kind=kOutput, calls=%fused_computation.14 | convolution fusion | flops 8589934592 | bytes 46137344 | tf_op jit(solution)/shard_map/tkab,tkbn->tan/dot_general | solution.py:35
  135.0 5.3 %copy.14 = f32[1024,1024]{0,1:T(8,128)} copy(f32[1024,1024]{1,0:T(8,128)} %bitcast.31) | data formatting | bytes 8388608 | tf_op jit(solution)/shard_map/reshape | solution.py:36
  140.3 0.0 all-gather.5.cloned.1.call-done
  140.3 4.5 %fusion.5 = f32[1024,1024]{1,0:T(8,128)} fusion(bf16[512,1024]{1,0:T(8,128)(2,1)} %all-gather.5.cloned.1.call-done, bf16[1024,512]{0,1:T(8,128)(2,1)S(1)} %bitcast.34), kind=kOutput, calls=%fused_computation.13 | convolution fusion | flops 1073741824 | bytes 6291456 | tf_op jit(solution)/shard_map/dot_general | solution.py:61
  144.8 0.0 all-gather.3.cloned.1.call-done
  144.8 0.0 copy-start.1
  144.8 5.4 %fusion = bf16[1024,1024]{0,1:T(8,128)(2,1)S(1)} fusion(f32[1024,1024]{0,1:T(8,128)} %copy.14, f32[1024,1024]{1,0:T(8,128)} %fusion.5, bf16[512,1024]{1,0:T(8,128)(2,1)} %all-gather.3.cloned.1.call-done, bf16[1024,512]{0,1:T(8,128)(2,1)} %bitcast.30), kind=kOutput, calls=%fused_computation.3 | convolution fusion | flops 1076887552 | bytes 12582912 | tf_op jit(solution)/shard_map/dot_general | solution.py:61
  150.3 2.6 %copy.15 = bf16[1024,1024]{1,0:T(8,128)(2,1)} copy(bf16[1024,1024]{0,1:T(8,128)(2,1)S(1)} %fusion) | data formatting | bytes 4194304 | tf_op jit(solution)/shard_map/convert_element_type | solution.py:64
  152.8 0.0 copy-done.1
  (2 shorter events, 0.0 us)
Async XLA Ops:
  6.5 1.2 copy-start
  6.5 23.6 %copy-start.2 = (bf16[4096,128]{1,0:T(8,128)(2,1)S(1)}, bf16[4096,128]{1,0:T(8,128)(2,1)}, u32[]{:S(2)}) copy-start(bf16[4096,128]{1,0:T(8,128)(2,1)} %param.11) | copy-start | bytes 3145732
  12.4 9.3 %collective-permute-start.5 = (bf16[128,1024]{1,0:T(8,128)(2,1)S(1)}, bf16[128,1024]{1,0:T(8,128)(2,1)S(1)}, u32[]{:S(2)}, u32[]{:S(2)}) collective-permute-start(bf16[128,1024]{1,0:T(8,128)(2,1)S(1)} %get-tuple-element.7), channel_id=1, source_target_pairs={{0,4},{4,0},{8,12},{12,8},{16,20},{20,16},{24,28},{28,24},{1,5},{5... | collective-permute-start | bytes 786440 | tf_op jit(solution)/shard_map/ppermute | solution.py:26
  21.8 7.6 %collective-permute-start.6 = (bf16[128,1024]{1,0:T(8,128)(2,1)S(1)}, bf16[128,1024]{1,0:T(8,128)(2,1)S(1)}, u32[]{:S(2)}, u32[]{:S(2)}) collective-permute-start(bf16[128,1024]{1,0:T(8,128)(2,1)S(1)} %add_convert_fusion), channel_id=1, source_target_pairs={{0,8},{4,12},{8,0},{12,4},{16,24},{20,28},{24,16},{28,20},{1,9},{5... | collective-permute-start | bytes 786440 | tf_op jit(solution)/shard_map/ppermute | solution.py:26
  23.7 23.2 %all-to-all-start.1 = ((bf16[4,1024,128]{2,1,0:T(8,128)(2,1)}), bf16[4,1024,128]{2,1,0:T(8,128)(2,1)S(1)}, u32[]{:S(2)}, u32[]{:S(2)}) async-start(bf16[4,1024,128]{2,1,0:T(8,128)(2,1)} %bitcast.35), calls=%async_computation.1 | async-start | bytes 2097152 | tf_op jit(solution)/shard_map/all_to_all | solution.py:55
  27.2 113.1 %all-gather.5.cloned.1.call-start = ((), (), s32[]{:S(2)}) async-start(), calls=%async_computation.3 | async-start | bytes 1310720 | tf_op jit(solution)/shard_map/all_gather | solution.py:59
  29.4 0.7 copy-start.3
  34.8 40.3 %copy-start.5 = (s32[4,16]{1,0:T(4,128)S(1)}, s32[4,16]{1,0:T(4,128)}, u32[]{:S(2)}) copy-start(s32[4,16]{1,0:T(4,128)} %param.9) | copy-start | bytes 772
  34.8 11.4 %collective-permute-start.2 = (bf16[128,1024]{1,0:T(8,128)(2,1)S(1)}, bf16[128,1024]{1,0:T(8,128)(2,1)S(1)}, u32[]{:S(2)}, u32[]{:S(2)}) collective-permute-start(bf16[128,1024]{1,0:T(8,128)(2,1)S(1)} %get-tuple-element.9), channel_id=1, source_target_pairs={{0,4},{4,0},{8,12},{12,8},{16,20},{20,16},{24,28},{28,24},{1,5},{5... | collective-permute-start | bytes 786440 | tf_op jit(solution)/shard_map/ppermute | solution.py:26
  39.4 45.1 %collective-permute-start.1 = (bf16[512,1024]{1,0:T(8,128)(2,1)}, bf16[512,1024]{1,0:T(8,128)(2,1)}, u32[]{:S(2)}, u32[]{:S(2)}) collective-permute-start(bf16[512,1024]{1,0:T(8,128)(2,1)} %get-tuple-element.6), channel_id=1, source_target_pairs={{4,0},{8,4},{12,8},{16,12},{20,16},{24,20},{28,24},{5,1},{9,5},{13... | collective-permute-start | bytes 3145736 | tf_op jit(solution)/shard_map/ppermute | solution.py:18
  40.7 45.5 %collective-permute-start = (bf16[512,1024]{1,0:T(8,128)(2,1)}, bf16[512,1024]{1,0:T(8,128)(2,1)}, u32[]{:S(2)}, u32[]{:S(2)}) collective-permute-start(bf16[512,1024]{1,0:T(8,128)(2,1)} %get-tuple-element.5), channel_id=1, source_target_pairs={{0,4},{4,8},{8,12},{12,16},{16,20},{20,24},{24,28},{1,5},{5,9},{9,... | collective-permute-start | bytes 3145736 | tf_op jit(solution)/shard_map/ppermute | solution.py:17
  46.3 24.0 %collective-permute-start.3 = (bf16[128,1024]{1,0:T(8,128)(2,1)S(1)}, bf16[128,1024]{1,0:T(8,128)(2,1)S(1)}, u32[]{:S(2)}, u32[]{:S(2)}) collective-permute-start(bf16[128,1024]{1,0:T(8,128)(2,1)S(1)} %fusion.1), channel_id=1, source_target_pairs={{0,8},{4,12},{8,0},{12,4},{16,24},{20,28},{24,16},{28,20},{1,9},{5... | collective-permute-start | bytes 786440 | tf_op jit(solution)/shard_map/ppermute | solution.py:26
  46.9 36.2 %all-to-all-start = ((bf16[4,1024,128]{2,1,0:T(8,128)(2,1)}), bf16[4,1024,128]{2,1,0:T(8,128)(2,1)S(1)}, u32[]{:S(2)}, u32[]{:S(2)}) async-start(bf16[4,1024,128]{2,1,0:T(8,128)(2,1)} %bitcast.36), calls=%async_computation | async-start | bytes 2097152 | tf_op jit(solution)/shard_map/all_to_all | solution.py:54
  50.5 94.4 %all-gather.3.cloned.1.call-start = ((), (), s32[]{:S(2)}) async-start(), calls=%async_computation.2 | async-start | bytes 1310720 | tf_op jit(solution)/shard_map/all_gather | solution.py:58
  70.4 11.5 %collective-permute-start.4 = (bf16[128,1024]{1,0:T(8,128)(2,1)S(1)}, bf16[128,1024]{1,0:T(8,128)(2,1)S(1)}, u32[]{:S(2)}, u32[]{:S(2)}) collective-permute-start(bf16[128,1024]{1,0:T(8,128)(2,1)S(1)} %add_convert_fusion.1), channel_id=1, source_target_pairs={{0,16},{4,20},{8,24},{12,28},{16,0},{20,4},{24,8},{28,12},{1,17},{... | collective-permute-start | bytes 786440 | tf_op jit(solution)/shard_map/ppermute | solution.py:26
  81.9 0.7 copy-start.4
  144.8 8.0 %copy-start.1 = (bf16[4096,128]{1,0:T(8,128)(2,1)S(1)}, bf16[4096,128]{1,0:T(8,128)(2,1)}, u32[]{:S(2)}) copy-start(bf16[4096,128]{1,0:T(8,128)(2,1)} %param.13) | copy-start | bytes 3145732
Sparse Core Ops, SparseCore 0:
  30.2 18.4 all-gather.4
  82.7 19.5 all-gather.2
where the time goes:
time: 160 us
  matrix products  38.1 us (24%)
  waiting for transfers between devices  36.4 us (23%)
  local copies, waits for them, and re-layouts  32 us (20%)
  starting transfers between devices  25.9 us (16%)
  other arithmetic  13.8 us (9%)
  between operations  13.5 us (8%)
    ppermute x5, waiting for transfers between devices, partner(): return lax.ppermute(value, axis, pairs)  34.7 us
    dot_general x1, matrix products, per_device(): jnp.einsum('tkab,tkbn->tan', near_tiles, picked, preferred_element_type=j...  18.8 us
    gather x1, local copies, waits for them, and re-layouts, per_device(): picked = blocks[near_cols]  16.4 us
    concatenate x1, other arithmetic, padded(): x = jnp.concatenate([before, x, after], axis=dim)  13.6 us
    ppermute x5, starting transfers between devices, partner(): return lax.ppermute(value, axis, pairs)  11.8 us
    ppermute x1, starting transfers between devices, padded(): before = lax.ppermute(last, axis, up)  5.52 us
    dot_general x1, matrix products, per_device(): jnp.dot(panel_one, whole_one, preferred_element_type=jnp.float32)  5.43 us
    reshape x1, local copies, waits for them, and re-layouts, per_device(): near_part = near_part.reshape(-1, vector_count)  5.33 us
  transfers between devices with their start and end apart: 11, of which 5 were waited for; matrix products, arithmetic and copies ran while one was open for 43% of the time, Pallas kernels for 0%

commit v1 on v0

v1 whole, which is shorter than its diff:
```python
import jax
import jax.numpy as jnp
from jax import lax
from jax.experimental import pallas as pl
from jax.experimental.pallas import tpu as pltpu
from jax.sharding import PartitionSpec as P

B = 256
REACH = 2
AXES = ("rows", "cols")
VMEM = 56 * 1024 * 1024


def moved(value, target):
    n_rows, n_cols = lax.axis_size("rows"), lax.axis_size("cols")
    pairs = []
    for row in range(n_rows):
        for col in range(n_cols):
            other = target(row, col)
            if 0 <= other[0] < n_rows:
                pairs.append((row * n_cols + col, other[0] * n_cols + other[1]))
    return lax.ppermute(value, AXES, pairs)


def flipped(value, row_bits, col_bits):
    return moved(value, lambda row, col: (row ^ row_bits, col ^ col_bits))


def project(half, right_one, right_two, vectors):
    depth, rank = right_one.shape
    width = vectors.shape[1] // 2
    step = min(512, depth)
    steps = depth // step

    def kernel(half_ref, one_ref, two_ref, vectors_ref, out_ref, acc_ref):
        k = pl.program_id(0)
        both = jnp.concatenate([one_ref[...], two_ref[...]], axis=1)
        part = lax.dot_general(
            both, vectors_ref[...], (((0,), (0,)), ((), ())), preferred_element_type=jnp.float32
        )

        @pl.when(k == 0)
        def _():
            acc_ref[...] = part

        @pl.when(k > 0)
        def _():
            acc_ref[...] += part

        @pl.when(k == steps - 1)
        def _():
            out_ref[...] = acc_ref[...].astype(jnp.bfloat16)

    return pl.pallas_call(
        kernel,
        out_shape=jax.ShapeDtypeStruct((2 * rank, width), jnp.bfloat16),
        grid_spec=pltpu.PrefetchScalarGridSpec(
            num_scalar_prefetch=1,
            grid=(steps,),
            in_specs=[
                pl.BlockSpec((step, rank), lambda k, half: (k, 0)),
                pl.BlockSpec((step, rank), lambda k, half: (k, 0)),
                pl.BlockSpec((step, width), lambda k, half: (k, half[0])),
            ],
            out_specs=pl.BlockSpec((2 * rank, width), lambda k, half: (0, 0)),
            scratch_shapes=[pltpu.VMEM((2 * rank, width), jnp.float32)],
        ),
        compiler_params=pltpu.CompilerParams(vmem_limit_bytes=VMEM),
        cost_estimate=pl.CostEstimate(
            flops=4 * rank * width * depth, bytes_accessed=2 * depth * (2 * rank + width), transcendentals=0
        ),
        name="project",
    )(half, right_one, right_two, vectors)


def near_inside(slots, near_tiles, vectors, first, count):
    _, nnz, _, _ = near_tiles.shape
    depth, width = vectors.shape
    inside = depth // B

    def kernel(slots_ref, tiles_ref, vectors_ref, out_ref, row_ref):
        t = pl.program_id(0) + first
        for col in range(inside):
            slot = slots_ref[t, col + REACH]
            tile = tiles_ref[0, jnp.maximum(slot, 0)]
            row_ref[:, col * B : (col + 1) * B] = jnp.where(slot >= 0, tile, jnp.zeros_like(tile))
        out_ref[...] = jnp.dot(row_ref[...], vectors_ref[...], preferred_element_type=jnp.float32)

    return pl.pallas_call(
        kernel,
        out_shape=jax.ShapeDtypeStruct((count * B, width), jnp.float32),
        grid_spec=pltpu.PrefetchScalarGridSpec(
            num_scalar_prefetch=1,
            grid=(count,),
            in_specs=[
                pl.BlockSpec((1, nnz, B, B), lambda t, slots: (t + first, 0, 0, 0)),
                pl.BlockSpec((depth, width), lambda t, slots: (0, 0)),
            ],
            out_specs=pl.BlockSpec((B, width), lambda t, slots: (t, 0)),
            scratch_shapes=[pltpu.VMEM((B, depth), jnp.bfloat16)],
        ),
        compiler_params=pltpu.CompilerParams(vmem_limit_bytes=VMEM),
        cost_estimate=pl.CostEstimate(
            flops=2 * count * B * depth * width,
            bytes_accessed=count * nnz * B * B * 2 + depth * width * 2 + count * B * width * 4,
            transcendentals=0,
        ),
        name="near_inside",
    )(slots, near_tiles, vectors)


def finish(where, halo_slots, near, near_tiles, halos, left_own, left_other, coeffs):
    tiles = near_tiles.shape[0]
    rows, width = near.shape
    half_width = width // 2
    rank = left_own[0].shape[1]
    outside = halo_slots.shape[1]
    per_half = len(coeffs) // 2
    others = len(left_other)

    def kernel(where_ref, slots_ref, near_ref, *refs):
        tile_refs, refs = refs[:outside], refs[outside:]
        halo_refs, refs = refs[:2], refs[2:]
        own_refs, refs = refs[:2], refs[2:]
        other_refs, refs = refs[:others], refs[others:]
        mine_refs, theirs_refs, out_ref = refs[:per_half], refs[per_half : 2 * per_half], refs[-1]
        j, t = pl.program_id(0), pl.program_id(1)
        wide = []
        for i in range(outside):
            tile = tile_refs[i][0, 0]
            wide.append(jnp.where(slots_ref[t, i] >= 0, tile, jnp.zeros_like(tile)))
        for level in range(2):
            wide.append(own_refs[level][...])
            wide += [ref[level] for ref in other_refs]
        wide = jnp.concatenate(wide, axis=1)

        def put(coeff_refs):
            tall = [ref[...] for ref in halo_refs]
            for level in range(2):
                tall += [ref[level * rank : (level + 1) * rank] for ref in coeff_refs]
            tall = jnp.concatenate(tall, axis=0)
            out_ref[...] = (
                near_ref[...] + jnp.dot(wide, tall, preferred_element_type=jnp.float32)
            ).astype(jnp.bfloat16)

        pl.when(j == 0)(lambda: put(mine_refs))
        pl.when(j == 1)(lambda: put(theirs_refs))

    def tile_spec(i):
        return pl.BlockSpec(
            (1, 1, B, B), lambda j, t, where, slots: (t, jnp.maximum(slots[t, i], 0), 0, 0)
        )

    def by_half(j, where):
        return jnp.bitwise_xor(j, where[0])

    return pl.pallas_call(
        kernel,
        out_shape=jax.ShapeDtypeStruct((rows, width), jnp.bfloat16),
        grid_spec=pltpu.PrefetchScalarGridSpec(
            num_scalar_prefetch=2,
            grid=(2, tiles),
            in_specs=[pl.BlockSpec((B, half_width), lambda j, t, where, slots: (t, by_half(j, where)))]
            + [tile_spec(i) for i in range(outside)]
            + [
                pl.BlockSpec((REACH * B, half_width), lambda j, t, where, slots: (0, by_half(j, where)))
                for _ in range(2)
            ]
            + [
                pl.BlockSpec((B, rank), lambda j, t, where, slots: (where[1] * tiles + t, 0))
                for _ in range(2)
            ]
            + [pl.BlockSpec((2, B, rank), lambda j, t, where, slots: (0, t, 0)) for _ in range(others)]
            + [
                pl.BlockSpec((2 * rank, half_width), lambda j, t, where, slots: (0, 0))
                for _ in range(2 * per_half)
            ],
            out_specs=pl.BlockSpec((B, half_width), lambda j, t, where, slots: (t, by_half(j, where))),
        ),
        compiler_params=pltpu.CompilerParams(vmem_limit_bytes=VMEM),
        cost_estimate=pl.CostEstimate(
            flops=2 * rows * width * (outside * B + 2 * per_half * rank),
            bytes_accessed=rows * width * 6 + 16 * 2**20,
            transcendentals=0,
        ),
        name="finish",
    )(where, halo_slots, near, *([near_tiles] * outside), *halos, *left_own, *left_other, *coeffs)


def per_device(vectors, near_tiles, near_cols, left_one, right_one, left_two, right_two):
    n_rows, n_cols = lax.axis_size("rows"), lax.axis_size("cols")
    bits = n_rows.bit_length() - 1
    row, col = lax.axis_index("rows"), lax.axis_index("cols")
    half, core = row % 2, col % 2
    depth, width = vectors.shape
    rank = right_one.shape[1]
    inside = depth // B
    window = inside + 2 * REACH

    nnz = near_cols.shape[1]
    names = near_cols[:, :, None] == jnp.arange(window, dtype=jnp.int32)
    slots = jnp.max(jnp.where(names, jnp.arange(nnz, dtype=jnp.int32)[None, :, None], -1), axis=1)

    send = project((1 - half).reshape(1), right_one, right_two, vectors)
    arrived = flipped(send, 1, 0)
    keep = project(half.reshape(1), right_one, right_two, vectors)

    edge = lax.dynamic_slice_in_dim(
        vectors, jnp.where(core == 0, depth - REACH * B, 0), REACH * B, axis=0
    )
    halo_mine = moved(edge, lambda r, c: (r + 1 if c % 2 == 0 else r - 1, c))

    share = depth // n_cols
    left_other = []
    for offset in range(1, n_cols):
        begin = (col ^ offset) * share
        piece = jnp.stack(
            [lax.dynamic_slice_in_dim(left, begin, share, axis=0) for left in (left_one, left_two)]
        )
        left_other.append(flipped(piece, 0, offset))

    near = near_inside(slots, near_tiles, vectors, 0, near_tiles.shape[0])

    def summed(a, b):
        return (a.astype(jnp.float32) + b.astype(jnp.float32)).astype(jnp.bfloat16)

    both = summed(keep, arrived)
    for bit in range(1, bits - 2):
        both = summed(both, flipped(both, 2**bit, 0))
    arrived = flipped(both, 2 ** (bits - 2), 0)
    one = summed(both[:rank], arrived[:rank])
    one = flipped(one, 2 ** (bits - 1), 0)
    both = jnp.concatenate([one, arrived[rank:]], axis=0)

    coeffs = []
    for other in range(2):
        for offset in range(0, n_cols, 2):
            there = both if (other, offset) == (0, 0) else flipped(both, other, offset)
            coeffs += [there, flipped(there, 0, 1)]

    halo_other = flipped(halo_mine, 0, 1)
    before, after = slots[:, :REACH], slots[:, window - REACH :]
    halo_slots = jnp.where(
        core == 0,
        jnp.concatenate([before, after], axis=1),
        jnp.concatenate([after, before], axis=1),
    )
    return finish(
        jnp.stack([half, col]),
        halo_slots,
        near,
        near_tiles,
        (halo_mine, halo_other),
        (left_one, left_two),
        left_other,
        coeffs,
    )


def solution(mesh):
    placed = (
        P("rows", None),
        P(("rows", "cols"), None, None, None),
        P(("rows", "cols"), None),
        P("rows", "cols"),
        P("rows", "cols"),
        P("rows", "cols"),
        P("rows", "cols"),
    )
    return jax.shard_map(
        per_device, mesh=mesh, in_specs=placed, out_specs=P(("rows", "cols"), None), check_vma=False
    )
```

time: 160 us -> 84.8 us (0.53)
  the two profiles are of different devices: /device:TPU:0 before, /device:TPU:3 now
where the time goes in v1:
time: 84.8 us; the launch traced here: 84.1 us
  Pallas kernels  42.7 us (50%)
  starting transfers between devices  27.3 us (32%)
  waiting for transfers between devices  6.4 us (8%)
  local copies, waits for them, and re-layouts  4.33 us (5%)
  other arithmetic  3.11 us (4%)
    ppermute x15, starting transfers between devices, moved(): return lax.ppermute(value, AXES, pairs)  27.3 us
    pallas_call x1, Pallas kernels, near_inside(): pl.pallas_call(kernel, out_shape=jax.ShapeDtypeStruct((count * B, width),...  15.1 us
    pallas_call x2, Pallas kernels, project(): pl.pallas_call(kernel, out_shape=jax.ShapeDtypeStruct((2 * rank, width),...  14.7 us
    pallas_call x1, Pallas kernels, finish(): pl.pallas_call(kernel, out_shape=jax.ShapeDtypeStruct((rows, width), jnp....  12.9 us
    ppermute x15, waiting for transfers between devices, moved(): return lax.ppermute(value, AXES, pairs)  6.4 us
    dynamic_slice x1, local copies, waits for them, and re-layouts, per_device(): lax.dynamic_slice_in_dim(vectors, jnp.where(core == 0, depth - REACH * B,...  2.41 us
    unnamed x34, local copies, waits for them, and re-layouts  1.72 us
  transfers between devices with their start and end apart: 15, of which 2 were waited for; matrix products, arithmetic and copies ran while one was open for 7% of the time, Pallas kernels for 27%

profile of v1, /device:TPU:3, one launch (start us, length us, event | category | flops | bytes accessed | tf_op | source)
XLA Modules:
  0.0 84.1 jit_solution(7418750609807814189)
XLA Ops:
  0.0 7.3 %project.3 = bf16[256,512]{1,0:T(8,128)(2,1)} custom-call(s32[1]{0:T(128)} %bitcast.8.half_ref, bf16[4096,128]{1,0:T(8,128)(2,1)} %one_ref.3, bf16[4096,128]{1,0:T(8,128)(2,1)} %two_ref.3, bf16[4096,1024]{1,0:T(8,128)(2,1)} %vectors_ref.5), custom_call_target="tpu_custom_call" | custom-call | flops 1073741824 | bytes 6291456 | tf_op jit(solution)/shard_map/project/pallas_call | solution.py:54
  7.4 0.0 collective-permute-start.5
  7.4 2.4 %constant_dynamic-slice_fusion = bf16[512,1024]{1,0:T(8,128)(2,1)} fusion(bf16[4096,1024]{1,0:T(8,128)(2,1)} %vectors_ref.5, s32[]{:T(128)S(6)} %select_n.45), kind=kLoop, calls=%fused_computation.15 | loop fusion | bytes 2097156 | tf_op jit(solution)/shard_map/dynamic_slice | solution.py:208
  9.8 3.2 %collective-permute-start = (bf16[512,1024]{1,0:T(8,128)(2,1)}, bf16[512,1024]{1,0:T(8,128)(2,1)S(1)}, u32[]{:S(2)}, u32[]{:S(2)}) collective-permute-start(bf16[512,1024]{1,0:T(8,128)(2,1)} %constant_dynamic-slice_fusion), channel_id=1, source_target_pairs={{0,4},{2,6},{4,8},{5,1},{6,10},{7,3},{8,12},{9,5},{10,14},{11,7},{... | collective-permute-start | bytes 3145736 | tf_op jit(solution)/shard_map/ppermute | solution.py:22
  13.0 0.0 copy-start.16
  13.0 7.4 %project.2 = bf16[256,512]{1,0:T(8,128)(2,1)} custom-call(s32[1]{0:T(128)} %bitcast.half_ref, bf16[4096,128]{1,0:T(8,128)(2,1)} %one_ref.3, bf16[4096,128]{1,0:T(8,128)(2,1)} %two_ref.3, bf16[4096,1024]{1,0:T(8,128)(2,1)} %vectors_ref.5), custom_call_target="tpu_custom_call" | custom-call | flops 1073741824 | bytes 6291456 | tf_op jit(solution)/shard_map/project/pallas_call | solution.py:54
  20.4 0.0 collective-permute-done.5
  20.4 1.0 %add_convert_fusion = bf16[256,512]{1,0:T(8,128)(2,1)S(1)} fusion(bf16[256,512]{1,0:T(8,128)(2,1)S(1)} %collective-permute-done.5, bf16[256,512]{1,0:T(8,128)(2,1)} %project.2), kind=kLoop, calls=%fused_computation.3 | loop fusion | flops 524288 | bytes 786432 | tf_op jit(solution)/shard_map/convert_element_type | solution.py:225
  21.4 1.4 %collective-permute-start.6 = (bf16[256,512]{1,0:T(8,128)(2,1)S(1)}, bf16[256,512]{1,0:T(8,128)(2,1)S(1)}, u32[]{:S(2)}, u32[]{:S(2)}) collective-permute-start(bf16[256,512]{1,0:T(8,128)(2,1)S(1)} %add_convert_fusion), channel_id=1, source_target_pairs={{0,8},{1,9},{2,10},{3,11},{4,12},{5,13},{6,14},{7,15},{8,0},{9,1},... | collective-permute-start | bytes 786440 | tf_op jit(solution)/shard_map/ppermute | solution.py:22
  22.8 0.0 copy-done
  22.8 0.0 copy-done.1
  22.8 0.1 dynamic-slice_bitcast_fusion
  22.9 0.1 pad_maximum_fusion
  23.0 7.5 %collective-permute-start.2 = (bf16[2,1024,128]{2,1,0:T(8,128)(2,1)S(1)}, bf16[2,1024,128]{2,1,0:T(8,128)(2,1)S(1)}, u32[]{:S(2)}, u32[]{:S(2)}) collective-permute-start(bf16[2,1024,128]{2,1,0:T(8,128)(2,1)S(1)} %pad_maximum_fusion), channel_id=1, source_target_pairs={{0,1},{1,0},{2,3},{3,2},{4,5},{5,4},{6,7},{7,6},{8,9},{9,8},{10,11... | collective-permute-start | bytes 1572872 | tf_op jit(solution)/shard_map/ppermute | solution.py:22
  30.4 0.1 pad_maximum_fusion.1
  30.5 1.3 %collective-permute-start.3 = (bf16[2,1024,128]{2,1,0:T(8,128)(2,1)S(1)}, bf16[2,1024,128]{2,1,0:T(8,128)(2,1)S(1)}, u32[]{:S(2)}, u32[]{:S(2)}) collective-permute-start(bf16[2,1024,128]{2,1,0:T(8,128)(2,1)S(1)} %pad_maximum_fusion.1), channel_id=1, source_target_pairs={{0,2},{1,3},{2,0},{3,1},{4,6},{5,7},{6,4},{7,5},{8,10},{9,11},{10,... | collective-permute-start | bytes 1572872 | tf_op jit(solution)/shard_map/ppermute | solution.py:22
  31.8 0.0 collective-permute-done.6
  31.8 0.1 collective-permute-start.7
  31.9 0.1 pad_maximum_fusion.2
  32.0 7.2 %collective-permute-start.4 = (bf16[2,1024,128]{2,1,0:T(8,128)(2,1)S(1)}, bf16[2,1024,128]{2,1,0:T(8,128)(2,1)S(1)}, u32[]{:S(2)}, u32[]{:S(2)}) collective-permute-start(bf16[2,1024,128]{2,1,0:T(8,128)(2,1)S(1)} %pad_maximum_fusion.2), channel_id=1, source_target_pairs={{0,3},{1,2},{2,1},{3,0},{4,7},{5,6},{6,5},{7,4},{8,11},{9,10},{10,... | collective-permute-start | bytes 1572872 | tf_op jit(solution)/shard_map/ppermute | solution.py:22
  39.2 0.0 copy-done.16
  39.2 0.7 select_reduce_fusion.slots_ref
  39.9 0.0 collective-permute-done.7
  40.0 0.0 copy-start.2
  40.0 0.0 copy-start.15
  40.0 2.3 %collective-permute-start.13 = (bf16[256,512]{1,0:T(8,128)(2,1)S(1)}, bf16[256,512]{1,0:T(8,128)(2,1)S(1)}, u32[]{:S(2)}, u32[]{:S(2)}) collective-permute-start(bf16[256,512]{1,0:T(8,128)(2,1)S(1)} %pad_maximum_fusion.3.refs_11_), channel_id=1, source_target_pairs={{0,6},{1,7},{2,4},{3,5},{4,2},{5,3},{6,0},{7,1},{8,14},{9,15},{10,... | collective-permute-start | bytes 786440 | tf_op jit(solution)/shard_map/ppermute | solution.py:22
  42.2 0.0 collective-permute-done.2.refs_8_
  42.2 0.0 collective-permute-start.11
  42.3 6.1 %collective-permute-done.3.refs_9_ = bf16[2,1024,128]{2,1,0:T(8,128)(2,1)S(1)} collective-permute-done((bf16[2,1024,128]{2,1,0:T(8,128)(2,1)S(1)}, bf16[2,1024,128]{2,1,0:T(8,128)(2,1)S(1)}, u32[]{:S(2)}, u32[]{:S(2)}) %collective-permute-start.3) | collective-permute-done | bytes 524320 | tf_op jit(solution)/shard_map/ppermute | solution.py:22
  48.3 1.0 %collective-permute-start.9 = (bf16[256,512]{1,0:T(8,128)(2,1)S(1)}, bf16[256,512]{1,0:T(8,128)(2,1)S(1)}, u32[]{:S(2)}, u32[]{:S(2)}) collective-permute-start(bf16[256,512]{1,0:T(8,128)(2,1)S(1)} %pad_maximum_fusion.3.refs_11_), channel_id=1, source_target_pairs={{0,2},{1,3},{2,0},{3,1},{4,6},{5,7},{6,4},{7,5},{8,10},{9,11},{10,... | collective-permute-start | bytes 786440 | tf_op jit(solution)/shard_map/ppermute | solution.py:22
  49.4 0.0 collective-permute-done.refs_4_
  49.4 2.3 %collective-permute-start.1 = (bf16[512,1024]{1,0:T(8,128)(2,1)S(1)}, bf16[512,1024]{1,0:T(8,128)(2,1)S(1)}, u32[]{:S(2)}, u32[]{:S(2)}) collective-permute-start(bf16[512,1024]{1,0:T(8,128)(2,1)S(1)} %collective-permute-done.refs_4_), channel_id=1, source_target_pairs={{0,1},{1,0},{2,3},{3,2},{4,5},{5,4},{6,7},{7,6},{8,9},{9,8},{10,11... | collective-permute-start | bytes 3145736 | tf_op jit(solution)/shard_map/ppermute | solution.py:22
  51.6 15.1 %near_inside.1.near_ref = f32[1024,1024]{1,0:T(8,128)} custom-call(s32[4,20]{1,0:T(4,128)} %select_reduce_fusion.slots_ref, bf16[4,16,256,256]{3,2,1,0:T(8,128)(2,1)} %refs_3_.1, bf16[4096,1024]{1,0:T(8,128)(2,1)} %vectors_ref.5), custom_call_target="tpu_custom_call" | custom-call | flops 8589934592 | bytes 20971520 | tf_op jit(solution)/shard_map/near_inside/pallas_call | solution.py:89
  66.7 0.0 copy-done.5
  66.7 0.0 copy-done.6
  66.7 0.0 copy-done.3
  66.7 0.0 collective-permute-done.4.refs_10_
  66.7 0.0 copy-done.2
  66.7 0.0 copy-start.7
  66.7 0.1 collective-permute-start.8
  66.8 0.0 collective-permute-done.13.refs_17_
  66.8 0.0 copy-start.8
  66.8 0.5 collective-permute-start.14
  67.3 0.0 collective-permute-done.11.refs_15_
  67.3 0.1 collective-permute-start.12
  67.4 0.0 collective-permute-done.9.refs_13_
  67.4 0.4 collective-permute-start.10
  67.9 0.0 copy-done.15
  67.9 0.1 fusion
  67.9 0.6 pad_add_fusion.where_ref
  68.5 0.6 add_select_fusion.slots_ref
  69.1 0.0 collective-permute-done.8.refs_12_
  69.1 0.0 collective-permute-done.14.refs_18_
  69.1 0.0 copy-start.12
  69.2 0.0 collective-permute-done.12.refs_16_
  69.2 0.0 copy-start.13
  69.2 0.3 collective-permute-done.10.refs_14_
  69.5 0.0 collective-permute-done.1.refs_5_
  69.5 0.3 copy-done.11
  69.8 0.1 copy-done.12
  69.9 0.1 copy-done.13
  70.0 0.2 copy-done.14
  70.2 1.0 %copy-done.4 = bf16[512,1024]{1,0:T(8,128)(2,1)} copy-done((bf16[512,1024]{1,0:T(8,128)(2,1)}, bf16[512,1024]{1,0:T(8,128)(2,1)S(1)}, u32[]{:S(2)}) %copy-start.4) | copy-done | bytes 1048600
  71.2 12.9 %finish.1 = bf16[1024,1024]{1,0:T(8,128)(2,1)} custom-call(s32[2]{0:T(128)} %pad_add_fusion.where_ref, s32[4,4]{1,0:T(4,128)} %add_select_fusion.slots_ref, f32[1024,1024]{1,0:T(8,128)} %near_inside.1.near_ref, bf16[4,16,256,256]{3,2,1,0:T(8,128)(2,1)} %refs_3_.1, bf16[4,16,256,256]{3,2,1,0:T(8,128)(2,1)} %refs_3_.1, bf16[4,16,256,256]{3,2,1,0:T(8,128)(2,1)} %refs_3_.1, ...), custom_call_target="tpu_custom_call" | custom-call | flops 4294967296 | bytes 23068672 | tf_op jit(solution)/shard_map/finish/pallas_call | solution.py:157
  (17 shorter events, 0.1 us)
Async XLA Ops:
  7.3 15.4 %copy-start = (bf16[4096,128]{1,0:T(8,128)(2,1)S(1)}, bf16[4096,128]{1,0:T(8,128)(2,1)}, u32[]{:S(2)}) copy-start(bf16[4096,128]{1,0:T(8,128)(2,1)} %refs_6_.1) | copy-start | bytes 3145732
  7.3 15.4 %copy-start.1 = (bf16[4096,128]{1,0:T(8,128)(2,1)S(1)}, bf16[4096,128]{1,0:T(8,128)(2,1)}, u32[]{:S(2)}) copy-start(bf16[4096,128]{1,0:T(8,128)(2,1)} %refs_7_.1) | copy-start | bytes 3145732
  7.4 13.0 %collective-permute-start.5 = (bf16[256,512]{1,0:T(8,128)(2,1)}, bf16[256,512]{1,0:T(8,128)(2,1)S(1)}, u32[]{:S(2)}, u32[]{:S(2)}) collective-permute-start(bf16[256,512]{1,0:T(8,128)(2,1)} %project.3), channel_id=1, source_target_pairs={{0,4},{1,5},{2,6},{3,7},{4,0},{5,1},{6,2},{7,3},{8,12},{9,13},{10,... | collective-permute-start | bytes 786440 | tf_op jit(solution)/shard_map/ppermute | solution.py:22
  9.8 39.6 %collective-permute-start = (bf16[512,1024]{1,0:T(8,128)(2,1)}, bf16[512,1024]{1,0:T(8,128)(2,1)S(1)}, u32[]{:S(2)}, u32[]{:S(2)}) collective-permute-start(bf16[512,1024]{1,0:T(8,128)(2,1)} %constant_dynamic-slice_fusion), channel_id=1, source_target_pairs={{0,4},{2,6},{4,8},{5,1},{6,10},{7,3},{8,12},{9,5},{10,14},{11,7},{... | collective-permute-start | bytes 3145736 | tf_op jit(solution)/shard_map/ppermute | solution.py:22
  13.0 26.2 %copy-start.16 = (s32[4,16]{1,0:T(4,128)S(1)}, s32[4,16]{1,0:T(4,128)}, u32[]{:S(2)}) copy-start(s32[4,16]{1,0:T(4,128)} %param.9) | copy-start | bytes 772
  21.4 10.4 %collective-permute-start.6 = (bf16[256,512]{1,0:T(8,128)(2,1)S(1)}, bf16[256,512]{1,0:T(8,128)(2,1)S(1)}, u32[]{:S(2)}, u32[]{:S(2)}) collective-permute-start(bf16[256,512]{1,0:T(8,128)(2,1)S(1)} %add_convert_fusion), channel_id=1, source_target_pairs={{0,8},{1,9},{2,10},{3,11},{4,12},{5,13},{6,14},{7,15},{8,0},{9,1},... | collective-permute-start | bytes 786440 | tf_op jit(solution)/shard_map/ppermute | solution.py:22
  23.0 19.3 %collective-permute-start.2 = (bf16[2,1024,128]{2,1,0:T(8,128)(2,1)S(1)}, bf16[2,1024,128]{2,1,0:T(8,128)(2,1)S(1)}, u32[]{:S(2)}, u32[]{:S(2)}) collective-permute-start(bf16[2,1024,128]{2,1,0:T(8,128)(2,1)S(1)} %pad_maximum_fusion), channel_id=1, source_target_pairs={{0,1},{1,0},{2,3},{3,2},{4,5},{5,4},{6,7},{7,6},{8,9},{9,8},{10,11... | collective-permute-start | bytes 1572872 | tf_op jit(solution)/shard_map/ppermute | solution.py:22
  30.5 17.8 %collective-permute-start.3 = (bf16[2,1024,128]{2,1,0:T(8,128)(2,1)S(1)}, bf16[2,1024,128]{2,1,0:T(8,128)(2,1)S(1)}, u32[]{:S(2)}, u32[]{:S(2)}) collective-permute-start(bf16[2,1024,128]{2,1,0:T(8,128)(2,1)S(1)} %pad_maximum_fusion.1), channel_id=1, source_target_pairs={{0,2},{1,3},{2,0},{3,1},{4,6},{5,7},{6,4},{7,5},{8,10},{9,11},{10,... | collective-permute-start | bytes 1572872 | tf_op jit(solution)/shard_map/ppermute | solution.py:22
  31.8 8.1 %collective-permute-start.7 = (bf16[128,512]{1,0:T(8,128)(2,1)S(1)}, bf16[128,512]{1,0:T(8,128)(2,1)S(1)}, u32[]{:S(2)}, u32[]{:S(2)}) collective-permute-start(bf16[128,512]{1,0:T(8,128)(2,1)S(1)} %add_convert_fusion.1), channel_id=1, source_target_pairs={{0,16},{1,17},{2,18},{3,19},{4,20},{5,21},{6,22},{7,23},{8,24},{9,... | collective-permute-start | bytes 393224 | tf_op jit(solution)/shard_map/ppermute | solution.py:22
  32.0 34.8 %collective-permute-start.4 = (bf16[2,1024,128]{2,1,0:T(8,128)(2,1)S(1)}, bf16[2,1024,128]{2,1,0:T(8,128)(2,1)S(1)}, u32[]{:S(2)}, u32[]{:S(2)}) collective-permute-start(bf16[2,1024,128]{2,1,0:T(8,128)(2,1)S(1)} %pad_maximum_fusion.2), channel_id=1, source_target_pairs={{0,3},{1,2},{2,1},{3,0},{4,7},{5,6},{6,5},{7,4},{8,11},{9,10},{10,... | collective-permute-start | bytes 1572872 | tf_op jit(solution)/shard_map/ppermute | solution.py:22
  40.0 26.8 %copy-start.2 = (bf16[256,512]{1,0:T(8,128)(2,1)}, bf16[256,512]{1,0:T(8,128)(2,1)S(1)}, u32[]{:S(2)}) copy-start(bf16[256,512]{1,0:T(8,128)(2,1)S(1)} %pad_maximum_fusion.3.refs_11_) | copy-start | bytes 786436
  40.0 27.9 %copy-start.15 = (s32[4,20]{1,0:T(4,128)S(1)}, s32[4,20]{1,0:T(4,128)}, u32[]{:S(2)}) copy-start(s32[4,20]{1,0:T(4,128)} %select_reduce_fusion.slots_ref) | copy-start | bytes 964
  40.0 26.9 %collective-permute-start.13 = (bf16[256,512]{1,0:T(8,128)(2,1)S(1)}, bf16[256,512]{1,0:T(8,128)(2,1)S(1)}, u32[]{:S(2)}, u32[]{:S(2)}) collective-permute-start(bf16[256,512]{1,0:T(8,128)(2,1)S(1)} %pad_maximum_fusion.3.refs_11_), channel_id=1, source_target_pairs={{0,6},{1,7},{2,4},{3,5},{4,2},{5,3},{6,0},{7,1},{8,14},{9,15},{10,... | collective-permute-start | bytes 786440 | tf_op jit(solution)/shard_map/ppermute | solution.py:22
  42.2 24.5 %copy-start.5 = (bf16[2,1024,128]{2,1,0:T(8,128)(2,1)}, bf16[2,1024,128]{2,1,0:T(8,128)(2,1)S(1)}, u32[]{:S(2)}) copy-start(bf16[2,1024,128]{2,1,0:T(8,128)(2,1)S(1)} %collective-permute-done.2.refs_8_) | copy-start | bytes 1572868
  42.2 25.1 %collective-permute-start.11 = (bf16[256,512]{1,0:T(8,128)(2,1)S(1)}, bf16[256,512]{1,0:T(8,128)(2,1)S(1)}, u32[]{:S(2)}, u32[]{:S(2)}) collective-permute-start(bf16[256,512]{1,0:T(8,128)(2,1)S(1)} %pad_maximum_fusion.3.refs_11_), channel_id=1, source_target_pairs={{0,4},{1,5},{2,6},{3,7},{4,0},{5,1},{6,2},{7,3},{8,12},{9,13},{10,... | collective-permute-start | bytes 786440 | tf_op jit(solution)/shard_map/ppermute | solution.py:22
  48.3 18.4 %copy-start.6 = (bf16[2,1024,128]{2,1,0:T(8,128)(2,1)}, bf16[2,1024,128]{2,1,0:T(8,128)(2,1)S(1)}, u32[]{:S(2)}) copy-start(bf16[2,1024,128]{2,1,0:T(8,128)(2,1)S(1)} %collective-permute-done.3.refs_9_) | copy-start | bytes 1572868
  48.3 19.1 %collective-permute-start.9 = (bf16[256,512]{1,0:T(8,128)(2,1)S(1)}, bf16[256,512]{1,0:T(8,128)(2,1)S(1)}, u32[]{:S(2)}, u32[]{:S(2)}) collective-permute-start(bf16[256,512]{1,0:T(8,128)(2,1)S(1)} %pad_maximum_fusion.3.refs_11_), channel_id=1, source_target_pairs={{0,2},{1,3},{2,0},{3,1},{4,6},{5,7},{6,4},{7,5},{8,10},{9,11},{10,... | collective-permute-start | bytes 786440 | tf_op jit(solution)/shard_map/ppermute | solution.py:22
  49.4 17.4 %copy-start.3 = (bf16[512,1024]{1,0:T(8,128)(2,1)}, bf16[512,1024]{1,0:T(8,128)(2,1)S(1)}, u32[]{:S(2)}) copy-start(bf16[512,1024]{1,0:T(8,128)(2,1)S(1)} %collective-permute-done.refs_4_) | copy-start | bytes 3145732
  49.4 20.1 %collective-permute-start.1 = (bf16[512,1024]{1,0:T(8,128)(2,1)S(1)}, bf16[512,1024]{1,0:T(8,128)(2,1)S(1)}, u32[]{:S(2)}, u32[]{:S(2)}) collective-permute-start(bf16[512,1024]{1,0:T(8,128)(2,1)S(1)} %collective-permute-done.refs_4_), channel_id=1, source_target_pairs={{0,1},{1,0},{2,3},{3,2},{4,5},{5,4},{6,7},{7,6},{8,9},{9,8},{10,11... | collective-permute-start | bytes 3145736 | tf_op jit(solution)/shard_map/ppermute | solution.py:22
  66.7 2.7 %copy-start.7 = (bf16[2,1024,128]{2,1,0:T(8,128)(2,1)}, bf16[2,1024,128]{2,1,0:T(8,128)(2,1)S(1)}, u32[]{:S(2)}) copy-start(bf16[2,1024,128]{2,1,0:T(8,128)(2,1)S(1)} %collective-permute-done.4.refs_10_) | copy-start | bytes 1572868
  66.7 2.4 %collective-permute-start.8 = (bf16[256,512]{1,0:T(8,128)(2,1)S(1)}, bf16[256,512]{1,0:T(8,128)(2,1)S(1)}, u32[]{:S(2)}, u32[]{:S(2)}) collective-permute-start(bf16[256,512]{1,0:T(8,128)(2,1)S(1)} %pad_maximum_fusion.3.refs_11_), channel_id=1, source_target_pairs={{0,1},{1,0},{2,3},{3,2},{4,5},{5,4},{6,7},{7,6},{8,9},{9,8},{10,11... | collective-permute-start | bytes 786440 | tf_op jit(solution)/shard_map/ppermute | solution.py:22
  66.8 2.6 %copy-start.8 = (bf16[256,512]{1,0:T(8,128)(2,1)}, bf16[256,512]{1,0:T(8,128)(2,1)S(1)}, u32[]{:S(2)}) copy-start(bf16[256,512]{1,0:T(8,128)(2,1)S(1)} %collective-permute-done.13.refs_17_) | copy-start | bytes 786436
  66.8 2.3 %collective-permute-start.14 = (bf16[256,512]{1,0:T(8,128)(2,1)S(1)}, bf16[256,512]{1,0:T(8,128)(2,1)S(1)}, u32[]{:S(2)}, u32[]{:S(2)}) collective-permute-start(bf16[256,512]{1,0:T(8,128)(2,1)S(1)} %collective-permute-done.13.refs_17_), channel_id=1, source_target_pairs={{0,1},{1,0},{2,3},{3,2},{4,5},{5,4},{6,7},{7,6},{8,9},{9,8},{10,11... | collective-permute-start | bytes 786440 | tf_op jit(solution)/shard_map/ppermute | solution.py:22
  67.3 2.2 %copy-start.9 = (bf16[256,512]{1,0:T(8,128)(2,1)}, bf16[256,512]{1,0:T(8,128)(2,1)S(1)}, u32[]{:S(2)}) copy-start(bf16[256,512]{1,0:T(8,128)(2,1)S(1)} %collective-permute-done.11.refs_15_) | copy-start | bytes 786436
  67.3 1.8 %collective-permute-start.12 = (bf16[256,512]{1,0:T(8,128)(2,1)S(1)}, bf16[256,512]{1,0:T(8,128)(2,1)S(1)}, u32[]{:S(2)}, u32[]{:S(2)}) collective-permute-start(bf16[256,512]{1,0:T(8,128)(2,1)S(1)} %collective-permute-done.11.refs_15_), channel_id=1, source_target_pairs={{0,1},{1,0},{2,3},{3,2},{4,5},{5,4},{6,7},{7,6},{8,9},{9,8},{10,11... | collective-permute-start | bytes 786440 | tf_op jit(solution)/shard_map/ppermute | solution.py:22
  67.4 2.1 %copy-start.10 = (bf16[256,512]{1,0:T(8,128)(2,1)}, bf16[256,512]{1,0:T(8,128)(2,1)S(1)}, u32[]{:S(2)}) copy-start(bf16[256,512]{1,0:T(8,128)(2,1)S(1)} %collective-permute-done.9.refs_13_) | copy-start | bytes 786436
  67.4 2.0 %collective-permute-start.10 = (bf16[256,512]{1,0:T(8,128)(2,1)S(1)}, bf16[256,512]{1,0:T(8,128)(2,1)S(1)}, u32[]{:S(2)}, u32[]{:S(2)}) collective-permute-start(bf16[256,512]{1,0:T(8,128)(2,1)S(1)} %collective-permute-done.9.refs_13_), channel_id=1, source_target_pairs={{0,1},{1,0},{2,3},{3,2},{4,5},{5,4},{6,7},{7,6},{8,9},{9,8},{10,11... | collective-permute-start | bytes 786440 | tf_op jit(solution)/shard_map/ppermute | solution.py:22
  69.1 0.7 copy-start.11
  69.1 0.8 copy-start.12
  69.2 0.9 %copy-start.13 = (bf16[256,512]{1,0:T(8,128)(2,1)}, bf16[256,512]{1,0:T(8,128)(2,1)S(1)}, u32[]{:S(2)}) copy-start(bf16[256,512]{1,0:T(8,128)(2,1)S(1)} %collective-permute-done.12.refs_16_) | copy-start | bytes 786436
  69.5 0.7 copy-start.14
  70.2 1.0 %copy-start.4 = (bf16[512,1024]{1,0:T(8,128)(2,1)}, bf16[512,1024]{1,0:T(8,128)(2,1)S(1)}, u32[]{:S(2)}) copy-start(bf16[512,1024]{1,0:T(8,128)(2,1)S(1)} %collective-permute-done.1.refs_5_) | copy-start | bytes 3145732

commit v2 on v0

v2 whole, which is shorter than its diff:
```python
import jax
import jax.numpy as jnp
from jax import lax
from jax.experimental import pallas as pl
from jax.experimental.pallas import tpu as pltpu
from jax.sharding import PartitionSpec as P

B = 256
REACH = 2
AXES = ("rows", "cols")
VMEM = 32 * 1024 * 1024
ANY = pl.BlockSpec(memory_space=pl.ANY)
SMEM = pl.BlockSpec(memory_space=pltpu.SMEM)


def moved(value, target):
    n_rows, n_cols = lax.axis_size("rows"), lax.axis_size("cols")
    pairs = []
    for row in range(n_rows):
        for col in range(n_cols):
            other = target(row, col)
            if 0 <= other[0] < n_rows:
                pairs.append((row * n_cols + col, other[0] * n_cols + other[1]))
    return lax.ppermute(value, AXES, pairs)


def flipped(value, row_bits, col_bits):
    return moved(value, lambda row, col: (row ^ row_bits, col ^ col_bits))


def span(index, size):
    return pl.ds(pl.multiple_of(index * size, size), size)


def called(kernel, name, smem, hbm, after, out_shape, scratch, flops, moved_bytes):
    return pl.pallas_call(
        kernel,
        out_shape=out_shape,
        in_specs=[SMEM] * len(smem) + [ANY] * (len(hbm) + len(after)),
        out_specs=jax.tree.map(lambda _: ANY, out_shape),
        scratch_shapes=scratch,
        compiler_params=pltpu.CompilerParams(vmem_limit_bytes=VMEM),
        cost_estimate=pl.CostEstimate(flops=flops, bytes_accessed=moved_bytes, transcendentals=0),
        name=name,
    )(*smem, *hbm, *after)


def project(where, right_one, right_two, vectors, other, with_edge, after=()):
    depth, rank = right_one.shape
    width = vectors.shape[1] // 2
    parts = 8
    step = depth // parts
    edge = REACH * B

    def kernel(where_ref, one_ref, two_ref, vectors_ref, *refs):
        refs = refs[len(after) :]
        outs, refs = refs[: 1 + with_edge], refs[1 + with_edge :]
        rights, block, total, result, right_sems, block_sems, out_sems = refs
        half = where_ref[0] ^ 1 if other else where_ref[0]
        copies = []
        for i in range(parts):
            rows = pl.ds(i * step, step)
            copies.append(
                [
                    pltpu.make_async_copy(
                        ref.at[rows], rights.at[rows, pl.ds(level * rank, rank)], right_sems.at[level, i]
                    )
                    for level, ref in enumerate((one_ref, two_ref))
                ]
                + [
                    pltpu.make_async_copy(
                        vectors_ref.at[rows, span(half, width)], block.at[rows], block_sems.at[i]
                    )
                ]
            )
            for copy in copies[-1]:
                copy.start()
        if with_edge:
            begin = pl.multiple_of(jnp.where(where_ref[1] % 2 == 0, depth - edge, 0), edge)
            edge_copy = pltpu.make_async_copy(vectors_ref.at[pl.ds(begin, edge)], outs[1], out_sems.at[1])
            edge_copy.start()
        for i in range(parts):
            for copy in copies[i]:
                copy.wait()
            rows = pl.ds(i * step, step)
            part = lax.dot_general(
                rights[rows], block[rows], (((0,), (0,)), ((), ())), preferred_element_type=jnp.float32
            )
            if i == 0:
                total[...] = part
            elif i < parts - 1:
                total[...] += part
            else:
                result[...] = (total[...] + part).astype(jnp.bfloat16)
        out_copy = pltpu.make_async_copy(result, outs[0], out_sems.at[0])
        out_copy.start()
        out_copy.wait()
        if with_edge:
            edge_copy.wait()

    out = [jax.ShapeDtypeStruct((2 * rank, width), jnp.bfloat16)]
    if with_edge:
        out.append(jax.ShapeDtypeStruct((edge, vectors.shape[1]), jnp.bfloat16))
    return called(
        kernel,
        "project",
        [where],
        [right_one, right_two, vectors],
        after,
        out,
        [
            pltpu.VMEM((depth, 2 * rank), jnp.bfloat16),
            pltpu.VMEM((depth, width), jnp.bfloat16),
            pltpu.VMEM((2 * rank, width), jnp.float32),
            pltpu.VMEM((2 * rank, width), jnp.bfloat16),
            pltpu.SemaphoreType.DMA((2, parts)),
            pltpu.SemaphoreType.DMA((parts,)),
            pltpu.SemaphoreType.DMA((2,)),
        ],
        4 * rank * width * depth,
        2 * depth * (2 * rank + width),
    )


def near_inside(slots, near_tiles, vectors, first, count, sofar, after=()):
    tiles = near_tiles.shape[0]
    rows, width = tiles * B, vectors.shape[1]
    group = min(2, count)
    groups = count // group
    half = width // 2
    given = 0 if sofar is None else 1

    def kernel(slots_ref, tiles_ref, vectors_ref, *refs):
        sofar_refs, refs = refs[:given], refs[given + len(after) :]
        out_ref, wide, tall, total, result, tile_sems, vector_sems, sofar_sem, out_sems = refs

        def tile_copy(t, c):
            slot = slots_ref[t, first + c + REACH]
            copy = pltpu.make_async_copy(
                tiles_ref.at[t, jnp.maximum(slot, 0)],
                wide.at[pl.ds(t * B, B), pl.ds(c * B, B)],
                tile_sems.at[t, c],
            )
            return slot >= 0, copy

        def vector_copy(c):
            return pltpu.make_async_copy(
                vectors_ref.at[pl.ds((first + c) * B, B)], tall.at[pl.ds(c * B, B)], vector_sems.at[c]
            )

        if given:
            sofar_copy = pltpu.make_async_copy(sofar_refs[0], result, sofar_sem)
        for c in range(count):
            vector_copy(c).start()
            for t in range(tiles):
                there, copy = tile_copy(t, c)
                pl.when(there)(copy.start)

                @pl.when(jnp.logical_not(there))
                def _():
                    wide[t * B : (t + 1) * B, c * B : (c + 1) * B] = jnp.zeros((B, B), jnp.bfloat16)

            if given and c == group - 1:
                sofar_copy.start()
        out_copies = []
        for g in range(groups):
            for c in range(g * group, (g + 1) * group):
                vector_copy(c).wait()
                for t in range(tiles):
                    there, copy = tile_copy(t, c)
                    pl.when(there)(copy.wait)
            chosen = pl.ds(g * group * B, group * B)
            if given and g == groups - 1:
                sofar_copy.wait()
            for n in range(2):
                columns = pl.ds(n * half, half)
                part = jnp.dot(wide[:, chosen], tall[chosen, columns], preferred_element_type=jnp.float32)
                if g > 0:
                    part = total[:, columns] + part
                if g < groups - 1:
                    total[:, columns] = part
                else:
                    if given:
                        part = part + result[:, columns].astype(jnp.float32)
                    result[:, columns] = part.astype(jnp.bfloat16)
                    out_copies.append(
                        pltpu.make_async_copy(result.at[:, columns], out_ref.at[:, columns], out_sems.at[n])
                    )
                    out_copies[-1].start()
        for copy in out_copies:
            copy.wait()

    return called(
        kernel,
        "near_inside",
        [slots],
        [near_tiles, vectors] + ([sofar] if given else []),
        after,
        jax.ShapeDtypeStruct((rows, width), jnp.bfloat16),
        [
            pltpu.VMEM((rows, count * B), jnp.bfloat16),
            pltpu.VMEM((count * B, width), jnp.bfloat16),
            pltpu.VMEM((rows, width), jnp.float32),
            pltpu.VMEM((rows, width), jnp.bfloat16),
            pltpu.SemaphoreType.DMA((tiles, count)),
            pltpu.SemaphoreType.DMA((count,)),
            pltpu.SemaphoreType.DMA,
            pltpu.SemaphoreType.DMA((2,)),
        ],
        2 * rows * count * B * width,
        2 * count * B * (rows + width) + 2 * rows * width,
    )


def add_level(where, slots, sofar, near_tiles, halos, level, left, left_other, coeffs, after=()):
    rows, width = sofar.shape
    tiles = rows // B
    half = width // 2
    rank = left.shape[1]
    outside = 2 * REACH if halos else 0
    window = slots.shape[1]
    others = len(left_other)
    offsets = others + 1
    depth = outside * B + offsets * rank

    def kernel(where_ref, slots_ref, sofar_ref, tiles_ref, left_ref, *refs):
        other_refs, refs = refs[:others], refs[others:]
        coeff_refs, refs = refs[: 2 * offsets], refs[2 * offsets :]
        halo_refs, refs = refs[: len(halos)], refs[len(halos) + len(after) :]
        out_ref, wide, tall, result, tile_sems, halo_sems, left_sems, coeff_sems, sofar_sem, out_sems = refs
        mine, core = where_ref[0], where_ref[1] % 2

        def tile_copy(t, i):
            before = (i < REACH) == (core == 0)
            slot = slots_ref[t, jnp.where(before, i % REACH, window - REACH + i % REACH)]
            copy = pltpu.make_async_copy(
                tiles_ref.at[t, jnp.maximum(slot, 0)],
                wide.at[pl.ds(t * B, B), pl.ds(i * B, B)],
                tile_sems.at[t, i],
            )
            return slot >= 0, copy

        copies = []
        for i in range(outside):
            for t in range(tiles):
                there, copy = tile_copy(t, i)
                pl.when(there)(copy.start)

                @pl.when(jnp.logical_not(there))
                def _():
                    wide[t * B : (t + 1) * B, i * B : (i + 1) * B] = jnp.zeros((B, B), jnp.bfloat16)

        for i in range(len(halos)):
            copies.append(
                pltpu.make_async_copy(
                    halo_refs[i], tall.at[pl.ds(i * REACH * B, REACH * B)], halo_sems.at[i]
                )
            )
        for d in range(offsets):
            source = left_ref.at[span(where_ref[1], rows)] if d == 0 else other_refs[d - 1].at[level]
            place = outside * B + d * rank
            copies.append(
                pltpu.make_async_copy(source, wide.at[:, pl.ds(place, rank)], left_sems.at[d])
            )
            for other in range(2):
                copies.append(
                    pltpu.make_async_copy(
                        coeff_refs[other * offsets + d],
                        tall.at[pl.ds(place, rank), span(mine ^ other, half)],
                        coeff_sems.at[other, d],
                    )
                )
        copies.append(pltpu.make_async_copy(sofar_ref, result, sofar_sem))
        for copy in copies:
            copy.start()
        for copy in copies:
            copy.wait()
        for i in range(outside):
            for t in range(tiles):
                there, copy = tile_copy(t, i)
                pl.when(there)(copy.wait)
        out_copies = []
        for n in range(2):
            columns = pl.ds(n * half, half)
            part = jnp.dot(wide[...], tall[:, columns], preferred_element_type=jnp.float32)
            result[:, columns] = (result[:, columns].astype(jnp.float32) + part).astype(jnp.bfloat16)
            out_copies.append(
                pltpu.make_async_copy(result.at[:, columns], out_ref.at[:, columns], out_sems.at[n])
            )
            out_copies[-1].start()
        for copy in out_copies:
            copy.wait()

    return called(
        kernel,
        "add_level",
        [where, slots],
        [sofar, near_tiles, left, *left_other, *coeffs, *halos],
        after,
        jax.ShapeDtypeStruct((rows, width), jnp.bfloat16),
        [
            pltpu.VMEM((rows, depth), jnp.bfloat16),
            pltpu.VMEM((depth, width), jnp.bfloat16),
            pltpu.VMEM((rows, width), jnp.bfloat16),
            pltpu.SemaphoreType.DMA((tiles, max(outside, 1))),
            pltpu.SemaphoreType.DMA((2,)),
            pltpu.SemaphoreType.DMA((offsets,)),
            pltpu.SemaphoreType.DMA((2, offsets)),
            pltpu.SemaphoreType.DMA,
            pltpu.SemaphoreType.DMA((2,)),
        ],
        2 * rows * depth * width,
        2 * depth * (rows + width) + 4 * rows * width,
    )


def per_device(vectors, near_tiles, near_cols, left_one, right_one, left_two, right_two):
    n_rows, n_cols = lax.axis_size("rows"), lax.axis_size("cols")
    bits = n_rows.bit_length() - 1
    row, col = lax.axis_index("rows"), lax.axis_index("cols")
    depth = vectors.shape[0]
    rank = right_one.shape[1]
    inside = depth // B
    where = jnp.stack([row % 2, col])

    (send,) = project(where, right_one, right_two, vectors, True, False)
    arrived = flipped(send, 1, 0)
    keep, edge = project(where, right_one, right_two, vectors, False, True, after=(send,))

    nnz = near_cols.shape[1]
    names = near_cols[:, :, None] == jnp.arange(inside + 2 * REACH, dtype=jnp.int32)
    slots = jnp.max(jnp.where(names, jnp.arange(nnz, dtype=jnp.int32)[None, :, None], -1), axis=1)

    share = depth // n_cols
    left_other = []
    for offset in range(1, n_cols):
        begin = (col ^ offset) * share
        piece = jnp.stack(
            [lax.dynamic_slice_in_dim(left, begin, share, axis=0) for left in (left_one, left_two)]
        )
        left_other.append(flipped(piece, 0, offset))

    def summed(a, b):
        return (a.astype(jnp.float32) + b.astype(jnp.float32)).astype(jnp.bfloat16)

    near = near_inside(slots, near_tiles, vectors, 0, inside // 2, None, after=(keep,))
    both = summed(keep, arrived)

    halo_mine = moved(edge, lambda r, c: (r + 1 if c % 2 == 0 else r - 1, c))

    for bit in range(1, bits - 2):
        both = summed(both, flipped(both, 2**bit, 0))
    arrived = flipped(both, 2 ** (bits - 2), 0)
    near = near_inside(slots, near_tiles, vectors, inside // 2, inside // 2, near, after=(both,))
    one = flipped(summed(both[:rank], arrived[:rank]), 2 ** (bits - 1), 0)
    two = arrived[rank:]

    def gathered(value):
        found = []
        for other in range(2):
            for offset in range(0, n_cols, 2):
                there = value if (other, offset) == (0, 0) else flipped(value, other, offset)
                found += [there, flipped(there, 0, 1)]
        return found

    coeffs_two = gathered(two)
    halos = (halo_mine, flipped(halo_mine, 0, 1))
    coeffs_one = gathered(one)
    near = add_level(where, slots, near, near_tiles, halos, 1, left_two, left_other, coeffs_two)
    return add_level(where, slots, near, near_tiles, (), 0, left_one, left_other, coeffs_one)


def solution(mesh):
    placed = (
        P("rows", None),
        P(("rows", "cols"), None, None, None),
        P(("rows", "cols"), None),
        P("rows", "cols"),
        P("rows", "cols"),
        P("rows", "cols"),
        P("rows", "cols"),
    )
    return jax.shard_map(
        per_device, mesh=mesh, in_specs=placed, out_specs=P(("rows", "cols"), None), check_vma=False
    )
```

time: 160 us -> 109 us (0.68)
  matrix products: 38.1 us -> 0 us
  Pallas kernels: 0 us -> 32.3 us
  local copies, waits for them, and re-layouts: 32 us -> 18.8 us
  between operations: 13.5 us -> 0.43 us
  other arithmetic: 13.8 us -> 1.37 us
  starting transfers between devices: 25.9 us -> 22.2 us
  waiting for transfers between devices: 36.4 us -> 33 us
    dot_general x5 -> x0, matrix products: 38.1 us -> none  [the longest x1 18.8 us: per_device(): jnp.einsum('tkab,tkbn->tan', near_tiles, picked, preferred_element_type=j...]
    pallas_call x0 -> x6, Pallas kernels: none -> 32.3 us  [called(): pl.pallas_call(kernel, out_shape=out_shape, in_specs=[SMEM] * len(smem) +...]
    gather x1 -> x0, local copies, waits for them, and re-layouts: 16.4 us -> none  [per_device(): picked = blocks[near_cols]]
    unnamed x12 -> x44, local copies, waits for them, and re-layouts: 2.64 us -> 18.7 us
    concatenate x1 -> x0, other arithmetic: 13.6 us -> none  [padded(): x = jnp.concatenate([before, x, after], axis=dim)]
    all_to_all x2 -> x0, starting transfers between devices: 7.04 us -> none  [the longest x1 3.52 us: per_device(): lax.all_to_all(left_one, 'cols', split_axis=0, concat_axis=1, tiled=True)]
    reshape x1 -> x0, local copies, waits for them, and re-layouts: 5.33 us -> none  [per_device(): near_part = near_part.reshape(-1, vector_count)]
    ppermute x7 -> x22, starting transfers between devices: 18.6 us -> 22.2 us  [moved(): return lax.ppermute(value, AXES, pairs)]
  transfers between devices with their start and end apart: 11 -> 22, of which waited for: 5 -> 3; matrix products, arithmetic and copies ran while one was open for 43% -> 1% of each run, Pallas kernels for 0% -> 20%
where the time goes in v2:
time: 109 us; the launch traced here: 108 us
  waiting for transfers between devices  33 us (30%)
  Pallas kernels  32.3 us (30%)
  starting transfers between devices  22.2 us (20%)
  local copies, waits for them, and re-layouts  18.8 us (17%)
  other arithmetic  1.37 us (1%)
    ppermute x22, waiting for transfers between devices, moved(): return lax.ppermute(value, AXES, pairs)  33 us
    pallas_call x6, Pallas kernels, called(): pl.pallas_call(kernel, out_shape=out_shape, in_specs=[SMEM] * len(smem) +...  32.3 us
    ppermute x22, starting transfers between devices, moved(): return lax.ppermute(value, AXES, pairs)  22.2 us
    unnamed x44, local copies, waits for them, and re-layouts  18.7 us
  transfers between devices with their start and end apart: 22, of which 3 were waited for; matrix products, arithmetic and copies ran while one was open for 1% of the time, Pallas kernels for 20%

profile of v2, /device:TPU:0, one launch (start us, length us, event | category | flops | bytes accessed | tf_op | source)
XLA Modules:
  0.0 108.1 jit_solution(6237628827849341153)
XLA Ops:
  0.0 0.1 pad_add_fusion.where_ref
  0.1 3.4 %copy-done = bf16[4096,1024]{1,0:T(8,128)(2,1)S(1)} copy-done((bf16[4096,1024]{1,0:T(8,128)(2,1)S(1)}, bf16[4096,1024]{1,0:T(8,128)(2,1)}, u32[]{:S(2)}) %copy-start) | copy-done | bytes 8388632
  3.5 1.2 %copy-done.4 = bf16[4096,128]{1,0:T(8,128)(2,1)S(1)} copy-done((bf16[4096,128]{1,0:T(8,128)(2,1)S(1)}, bf16[4096,128]{1,0:T(8,128)(2,1)}, u32[]{:S(2)}) %copy-start.4) | copy-done | bytes 1048600
  4.7 1.2 %copy-done.5 = bf16[4096,128]{1,0:T(8,128)(2,1)S(1)} copy-done((bf16[4096,128]{1,0:T(8,128)(2,1)S(1)}, bf16[4096,128]{1,0:T(8,128)(2,1)}, u32[]{:S(2)}) %copy-start.5) | copy-done | bytes 1048600
  5.9 3.5 %project.2.refs_0_ = bf16[256,512]{1,0:T(8,128)(2,1)S(1)} custom-call(s32[2]{0:T(128)S(1)} %pad_add_fusion.where_ref, bf16[4096,128]{1,0:T(8,128)(2,1)S(1)} %copy-done.4, bf16[4096,128]{1,0:T(8,128)(2,1)S(1)} %copy-done.5, bf16[4096,1024]{1,0:T(8,128)(2,1)S(1)} %copy-done), custom_call_target="tpu_custom_call" | custom-call | flops 1073741824 | bytes 6291456 | tf_op jit(solution)/shard_map/project/pallas_call | solution.py:36
  9.4 0.0 copy-start.6
  9.5 0.0 copy-start.7
  9.5 3.5 %project.3 = (bf16[256,512]{1,0:T(8,128)(2,1)S(1)}, bf16[512,1024]{1,0:T(8,128)(2,1)}) custom-call(s32[2]{0:T(128)S(1)} %pad_add_fusion.where_ref, bf16[4096,128]{1,0:T(8,128)(2,1)S(1)} %copy-done.4, bf16[4096,128]{1,0:T(8,128)(2,1)S(1)} %copy-done.5, bf16[4096,1024]{1,0:T(8,128)(2,1)S(1)} %copy-done, bf16[256,512]{1,0:T(8,128)(2,1)S(1)} %project.2.refs_0_), custom_call_target="tpu_custom_call" | custom-call | flops 1073741824 | bytes 6291456 | tf_op jit(solution)/shard_map/project/pallas_call | solution.py:36
  13.0 5.8 %collective-permute-start.12 = (bf16[512,1024]{1,0:T(8,128)(2,1)}, bf16[512,1024]{1,0:T(8,128)(2,1)}, u32[]{:S(2)}, u32[]{:S(2)}) collective-permute-start(bf16[512,1024]{1,0:T(8,128)(2,1)} %get-tuple-element.8), channel_id=1, source_target_pairs={{0,4},{2,6},{4,8},{5,1},{6,10},{7,3},{8,12},{9,5},{10,14},{11,7},{... | collective-permute-start | bytes 3145736 | tf_op jit(solution)/shard_map/ppermute | solution.py:24
  18.9 0.6 collective-permute-start
  19.5 0.1 dynamic-slice_bitcast_fusion
  19.6 0.0 copy-start.21
  19.6 0.1 pad_maximum_fusion
  19.7 0.1 collective-permute-start.1
  19.8 0.1 pad_maximum_fusion.1
  19.8 1.6 %collective-permute-start.2 = (bf16[2,1024,128]{2,1,0:T(8,128)(2,1)S(1)}, bf16[2,1024,128]{2,1,0:T(8,128)(2,1)S(1)}, u32[]{:S(2)}, u32[]{:S(2)}) collective-permute-start(bf16[2,1024,128]{2,1,0:T(8,128)(2,1)S(1)} %pad_maximum_fusion.1), channel_id=1, source_target_pairs={{0,2},{1,3},{2,0},{3,1},{4,6},{5,7},{6,4},{7,5},{8,10},{9,11},{10,... | collective-permute-start | bytes 1572872 | tf_op jit(solution)/shard_map/ppermute | solution.py:24
  21.4 0.1 pad_maximum_fusion.2
  21.5 0.4 collective-permute-start.3
  21.8 24.2 %collective-permute-done = bf16[256,512]{1,0:T(8,128)(2,1)} collective-permute-done((bf16[256,512]{1,0:T(8,128)(2,1)S(1)}, bf16[256,512]{1,0:T(8,128)(2,1)}, u32[]{:S(2)}, u32[]{:S(2)}) %collective-permute-start) | collective-permute-done | bytes 262176 | tf_op jit(solution)/shard_map/ppermute | solution.py:24
  46.0 1.0 add_convert_fusion.refs_1_
  47.0 1.9 %collective-permute-start.4 = (bf16[256,512]{1,0:T(8,128)(2,1)S(1)}, bf16[256,512]{1,0:T(8,128)(2,1)S(1)}, u32[]{:S(2)}, u32[]{:S(2)}) collective-permute-start(bf16[256,512]{1,0:T(8,128)(2,1)S(1)} %add_convert_fusion.refs_1_), channel_id=1, source_target_pairs={{0,8},{1,9},{2,10},{3,11},{4,12},{5,13},{6,14},{7,15},{8,0},{9,1},... | collective-permute-start | bytes 786440 | tf_op jit(solution)/shard_map/ppermute | solution.py:24
  48.9 0.0 collective-permute-done.12.refs_11_
  48.9 0.5 collective-permute-start.13
  49.4 0.1 select_reduce_fusion.slots_ref
  49.5 6.7 %collective-permute-done.4 = bf16[256,512]{1,0:T(8,128)(2,1)S(1)} collective-permute-done((bf16[256,512]{1,0:T(8,128)(2,1)S(1)}, bf16[256,512]{1,0:T(8,128)(2,1)S(1)}, u32[]{:S(2)}, u32[]{:S(2)}) %collective-permute-start.4) | collective-permute-done | bytes 262176 | tf_op jit(solution)/shard_map/ppermute | solution.py:24
  56.2 1.1 %collective-permute-start.10 = (bf16[128,512]{1,0:T(8,128)(2,1)S(1)}, bf16[128,512]{1,0:T(8,128)(2,1)S(1)}, u32[]{:S(2)}, u32[]{:S(2)}) collective-permute-start(bf16[128,512]{1,0:T(8,128)(2,1)S(1)} %slice.12.refs_3_), channel_id=1, source_target_pairs={{0,6},{1,7},{2,4},{3,5},{4,2},{5,3},{6,0},{7,1},{8,14},{9,15},{10,... | collective-permute-start | bytes 393224 | tf_op jit(solution)/shard_map/ppermute | solution.py:24
  57.3 0.5 collective-permute-start.6
  57.9 0.8 copy-done.9
  58.6 1.9 %collective-permute-start.8 = (bf16[128,512]{1,0:T(8,128)(2,1)S(1)}, bf16[128,512]{1,0:T(8,128)(2,1)S(1)}, u32[]{:S(2)}, u32[]{:S(2)}) collective-permute-start(bf16[128,512]{1,0:T(8,128)(2,1)S(1)} %slice.12.refs_3_), channel_id=1, source_target_pairs={{0,4},{1,5},{2,6},{3,7},{4,0},{5,1},{6,2},{7,3},{8,12},{9,13},{10,... | collective-permute-start | bytes 393224 | tf_op jit(solution)/shard_map/ppermute | solution.py:24
  60.6 0.8 copy-done.11
  61.4 2.2 %collective-permute-done.10.refs_9_ = bf16[128,512]{1,0:T(8,128)(2,1)S(1)} collective-permute-done((bf16[128,512]{1,0:T(8,128)(2,1)S(1)}, bf16[128,512]{1,0:T(8,128)(2,1)S(1)}, u32[]{:S(2)}, u32[]{:S(2)}) %collective-permute-start.10) | collective-permute-done | bytes 131104 | tf_op jit(solution)/shard_map/ppermute | solution.py:24
  63.6 2.5 %collective-permute-start.14 = (bf16[128,512]{1,0:T(8,128)(2,1)S(1)}, bf16[128,512]{1,0:T(8,128)(2,1)S(1)}, u32[]{:S(2)}, u32[]{:S(2)}) collective-permute-start(bf16[128,512]{1,0:T(8,128)(2,1)S(1)} %add_convert_fusion.1), channel_id=1, source_target_pairs={{0,16},{1,17},{2,18},{3,19},{4,20},{5,21},{6,22},{7,23},{8,24},{9,... | collective-permute-start | bytes 393224 | tf_op jit(solution)/shard_map/ppermute | solution.py:24
  66.1 0.0 collective-permute-start.11
  66.1 0.0 collective-permute-done.8.refs_7_
  66.1 0.5 collective-permute-start.7
  66.6 3.4 %copy-done.1 = bf16[4096,1024]{1,0:T(8,128)(2,1)S(1)} copy-done((bf16[4096,1024]{1,0:T(8,128)(2,1)S(1)}, bf16[4096,1024]{1,0:T(8,128)(2,1)}, u32[]{:S(2)}) %copy-start.1) | copy-done | bytes 8388632
  70.0 3.4 %copy-done.2 = bf16[4,16,256,256]{3,2,1,0:T(8,128)(2,1)S(1)} copy-done((bf16[4,16,256,256]{3,2,1,0:T(8,128)(2,1)S(1)}, bf16[4,16,256,256]{3,2,1,0:T(8,128)(2,1)}, u32[]{:S(2)}) %copy-start.2) | copy-done | bytes 8388632
  73.4 0.9 copy-done.14
  74.3 7.5 %near_inside.2.refs_0_ = bf16[1024,1024]{1,0:T(8,128)(2,1)S(1)} custom-call(s32[4,20]{1,0:T(4,128)S(1)} %select_reduce_fusion.slots_ref, bf16[4,16,256,256]{3,2,1,0:T(8,128)(2,1)S(1)} %copy-done.2, bf16[4096,1024]{1,0:T(8,128)(2,1)S(1)} %copy-done.1, bf16[256,512]{1,0:T(8,128)(2,1)S(1)} %copy-done.14), custom_call_target="tpu_custom_call" | custom-call | flops 4294967296 | bytes 10485760 | tf_op jit(solution)/shard_map/near_inside/pallas_call | solution.py:36
  81.8 0.0 collective-permute-done.14.refs_3_
  81.9 1.8 %collective-permute-start.16 = (bf16[128,512]{1,0:T(8,128)(2,1)S(1)}, bf16[128,512]{1,0:T(8,128)(2,1)S(1)}, u32[]{:S(2)}, u32[]{:S(2)}) collective-permute-start(bf16[128,512]{1,0:T(8,128)(2,1)S(1)} %collective-permute-done.14.refs_3_), channel_id=1, source_target_pairs={{0,2},{1,3},{2,0},{3,1},{4,6},{5,7},{6,4},{7,5},{8,10},{9,11},{10,... | collective-permute-start | bytes 393224 | tf_op jit(solution)/shard_map/ppermute | solution.py:24
  83.6 0.0 collective-permute-done.5.refs_4_
  83.6 0.0 collective-permute-start.18
  83.6 0.0 collective-permute-done.11.refs_10_
  83.6 0.6 copy-done.17
  84.3 1.8 %collective-permute-start.20 = (bf16[128,512]{1,0:T(8,128)(2,1)S(1)}, bf16[128,512]{1,0:T(8,128)(2,1)S(1)}, u32[]{:S(2)}, u32[]{:S(2)}) collective-permute-start(bf16[128,512]{1,0:T(8,128)(2,1)S(1)} %collective-permute-done.14.refs_3_), channel_id=1, source_target_pairs={{0,6},{1,7},{2,4},{3,5},{4,2},{5,3},{6,0},{7,1},{8,14},{9,15},{10,... | collective-permute-start | bytes 393224 | tf_op jit(solution)/shard_map/ppermute | solution.py:24
  86.1 0.0 collective-permute-done.7.refs_6_
  86.1 0.7 copy-done.19
  86.7 0.0 collective-permute-start.9
  86.7 7.8 %near_inside.3.sofar_ref = bf16[1024,1024]{1,0:T(8,128)(2,1)S(1)} custom-call(s32[4,20]{1,0:T(4,128)S(1)} %select_reduce_fusion.slots_ref, bf16[4,16,256,256]{3,2,1,0:T(8,128)(2,1)S(1)} %copy-done.3, bf16[4096,1024]{1,0:T(8,128)(2,1)S(1)} %copy-done.1, bf16[1024,1024]{1,0:T(8,128)(2,1)S(1)} %near_inside.2.refs_0_, bf16[256,512]{1,0:T(8,128)(2,1)S(1)} %add_convert_fusion.refs_1_), custom_call_target="tpu_custom_call" | custom-call | flops 4294967296 | bytes 10485760 | tf_op jit(solution)/shard_map/near_inside/pallas_call | solution.py:36
  94.6 0.0 copy-start.8
  94.6 0.0 collective-permute-done.9.refs_8_
  94.6 0.6 collective-permute-start.15
  95.2 0.0 collective-permute-done.16.refs_5_
  95.2 0.1 collective-permute-start.17
  95.3 0.0 collective-permute-done.18.refs_7_
  95.3 0.4 collective-permute-start.19
  95.7 0.0 collective-permute-done.20.refs_9_
  95.7 0.1 collective-permute-start.21
  95.8 1.0 copy-done.15
  96.8 0.0 copy-start.16
  96.8 1.2 %copy-done.16 = bf16[512,1024]{1,0:T(8,128)(2,1)S(1)} copy-done((bf16[512,1024]{1,0:T(8,128)(2,1)S(1)}, bf16[512,1024]{1,0:T(8,128)(2,1)}, u32[]{:S(2)}) %copy-start.16) | copy-done | bytes 1048600
  98.0 6.4 %add_level.2.sofar_ref = bf16[1024,1024]{1,0:T(8,128)(2,1)S(1)} custom-call(s32[2]{0:T(128)S(1)} %pad_add_fusion.where_ref, s32[4,20]{1,0:T(4,128)S(1)} %select_reduce_fusion.slots_ref, bf16[1024,1024]{1,0:T(8,128)(2,1)S(1)} %near_inside.3.sofar_ref, bf16[4,16,256,256]{3,2,1,0:T(8,128)(2,1)S(1)} %copy-done.3, bf16[4096,128]{1,0:T(8,128)(2,1)S(1)} %copy-done.6, ...), custom_call_target="tpu_custom_call" | custom-call | flops 3221225472 | bytes 10485760 | tf_op jit(solution)/shard_map/add_level/pallas_call | solution.py:36
  104.5 3.5 %add_level.3 = bf16[1024,1024]{1,0:T(8,128)(2,1)} custom-call(s32[2]{0:T(128)S(1)} %pad_add_fusion.where_ref, s32[4,20]{1,0:T(4,128)S(1)} %select_reduce_fusion.slots_ref, bf16[1024,1024]{1,0:T(8,128)(2,1)S(1)} %add_level.2.sofar_ref, bf16[4,16,256,256]{3,2,1,0:T(8,128)(2,1)S(1)} %copy-done.3, bf16[4096,128]{1,0:T(8,128)(2,1)S(1)} %copy-done.8, ...), custom_call_target="tpu_custom_call" | custom-call | flops 1073741824 | bytes 6291456 | tf_op jit(solution)/shard_map/add_level/pallas_call | solution.py:36
  (39 shorter events, 0.1 us)
Async XLA Ops:
  0.1 3.4 %copy-start = (bf16[4096,1024]{1,0:T(8,128)(2,1)S(1)}, bf16[4096,1024]{1,0:T(8,128)(2,1)}, u32[]{:S(2)}) copy-start(bf16[4096,1024]{1,0:T(8,128)(2,1)} %vectors_ref.7) | copy-start | bytes 25165828
  3.5 1.2 %copy-start.4 = (bf16[4096,128]{1,0:T(8,128)(2,1)S(1)}, bf16[4096,128]{1,0:T(8,128)(2,1)}, u32[]{:S(2)}) copy-start(bf16[4096,128]{1,0:T(8,128)(2,1)} %one_ref.3) | copy-start | bytes 3145732
  4.7 1.2 %copy-start.5 = (bf16[4096,128]{1,0:T(8,128)(2,1)S(1)}, bf16[4096,128]{1,0:T(8,128)(2,1)}, u32[]{:S(2)}) copy-start(bf16[4096,128]{1,0:T(8,128)(2,1)} %two_ref.3) | copy-start | bytes 3145732
  9.4 10.1 %copy-start.6 = (bf16[4096,128]{1,0:T(8,128)(2,1)S(1)}, bf16[4096,128]{1,0:T(8,128)(2,1)}, u32[]{:S(2)}) copy-start(bf16[4096,128]{1,0:T(8,128)(2,1)} %left_ref.2) | copy-start | bytes 3145732
  9.5 10.0 %copy-start.7 = (bf16[4096,128]{1,0:T(8,128)(2,1)S(1)}, bf16[4096,128]{1,0:T(8,128)(2,1)}, u32[]{:S(2)}) copy-start(bf16[4096,128]{1,0:T(8,128)(2,1)} %left_ref.3) | copy-start | bytes 3145732
  13.0 33.0 %copy-start.13 = (bf16[256,512]{1,0:T(8,128)(2,1)}, bf16[256,512]{1,0:T(8,128)(2,1)S(1)}, u32[]{:S(2)}) copy-start(bf16[256,512]{1,0:T(8,128)(2,1)S(1)} %get-tuple-element.7.refs_0_) | copy-start | bytes 786436
  13.0 35.9 %collective-permute-start.12 = (bf16[512,1024]{1,0:T(8,128)(2,1)}, bf16[512,1024]{1,0:T(8,128)(2,1)}, u32[]{:S(2)}, u32[]{:S(2)}) collective-permute-start(bf16[512,1024]{1,0:T(8,128)(2,1)} %get-tuple-element.8), channel_id=1, source_target_pairs={{0,4},{2,6},{4,8},{5,1},{6,10},{7,3},{8,12},{9,5},{10,14},{11,7},{... | collective-permute-start | bytes 3145736 | tf_op jit(solution)/shard_map/ppermute | solution.py:24
  18.9 27.1 %collective-permute-start = (bf16[256,512]{1,0:T(8,128)(2,1)S(1)}, bf16[256,512]{1,0:T(8,128)(2,1)}, u32[]{:S(2)}, u32[]{:S(2)}) collective-permute-start(bf16[256,512]{1,0:T(8,128)(2,1)S(1)} %project.2.refs_0_), channel_id=1, source_target_pairs={{0,4},{1,5},{2,6},{3,7},{4,0},{5,1},{6,2},{7,3},{8,12},{9,13},{10,... | collective-permute-start | bytes 786440 | tf_op jit(solution)/shard_map/ppermute | solution.py:24
  19.6 29.8 %copy-start.21 = (s32[4,16]{1,0:T(4,128)S(1)}, s32[4,16]{1,0:T(4,128)}, u32[]{:S(2)}) copy-start(s32[4,16]{1,0:T(4,128)} %param.9) | copy-start | bytes 772
  19.7 37.6 %collective-permute-start.1 = (bf16[2,1024,128]{2,1,0:T(8,128)(2,1)S(1)}, bf16[2,1024,128]{2,1,0:T(8,128)(2,1)S(1)}, u32[]{:S(2)}, u32[]{:S(2)}) collective-permute-start(bf16[2,1024,128]{2,1,0:T(8,128)(2,1)S(1)} %pad_maximum_fusion), channel_id=1, source_target_pairs={{0,1},{1,0},{2,3},{3,2},{4,5},{5,4},{6,7},{7,6},{8,9},{9,8},{10,11... | collective-permute-start | bytes 1572872 | tf_op jit(solution)/shard_map/ppermute | solution.py:24
  19.8 38.0 %collective-permute-start.2 = (bf16[2,1024,128]{2,1,0:T(8,128)(2,1)S(1)}, bf16[2,1024,128]{2,1,0:T(8,128)(2,1)S(1)}, u32[]{:S(2)}, u32[]{:S(2)}) collective-permute-start(bf16[2,1024,128]{2,1,0:T(8,128)(2,1)S(1)} %pad_maximum_fusion.1), channel_id=1, source_target_pairs={{0,2},{1,3},{2,0},{3,1},{4,6},{5,7},{6,4},{7,5},{8,10},{9,11},{10,... | collective-permute-start | bytes 1572872 | tf_op jit(solution)/shard_map/ppermute | solution.py:24
  21.5 39.1 %collective-permute-start.3 = (bf16[2,1024,128]{2,1,0:T(8,128)(2,1)S(1)}, bf16[2,1024,128]{2,1,0:T(8,128)(2,1)S(1)}, u32[]{:S(2)}, u32[]{:S(2)}) collective-permute-start(bf16[2,1024,128]{2,1,0:T(8,128)(2,1)S(1)} %pad_maximum_fusion.2), channel_id=1, source_target_pairs={{0,3},{1,2},{2,1},{3,0},{4,7},{5,6},{6,5},{7,4},{8,11},{9,10},{10,... | collective-permute-start | bytes 1572872 | tf_op jit(solution)/shard_map/ppermute | solution.py:24
  47.0 9.1 %collective-permute-start.4 = (bf16[256,512]{1,0:T(8,128)(2,1)S(1)}, bf16[256,512]{1,0:T(8,128)(2,1)S(1)}, u32[]{:S(2)}, u32[]{:S(2)}) collective-permute-start(bf16[256,512]{1,0:T(8,128)(2,1)S(1)} %add_convert_fusion.refs_1_), channel_id=1, source_target_pairs={{0,8},{1,9},{2,10},{3,11},{4,12},{5,13},{6,14},{7,15},{8,0},{9,1},... | collective-permute-start | bytes 786440 | tf_op jit(solution)/shard_map/ppermute | solution.py:24
  48.9 46.9 %collective-permute-start.13 = (bf16[512,1024]{1,0:T(8,128)(2,1)}, bf16[512,1024]{1,0:T(8,128)(2,1)S(1)}, u32[]{:S(2)}, u32[]{:S(2)}) collective-permute-start(bf16[512,1024]{1,0:T(8,128)(2,1)} %collective-permute-done.12.refs_11_), channel_id=1, source_target_pairs={{0,1},{1,0},{2,3},{3,2},{4,5},{5,4},{6,7},{7,6},{8,9},{9,8},{10,11... | collective-permute-start | bytes 3145736 | tf_op jit(solution)/shard_map/ppermute | solution.py:24
  56.2 7.4 %collective-permute-start.10 = (bf16[128,512]{1,0:T(8,128)(2,1)S(1)}, bf16[128,512]{1,0:T(8,128)(2,1)S(1)}, u32[]{:S(2)}, u32[]{:S(2)}) collective-permute-start(bf16[128,512]{1,0:T(8,128)(2,1)S(1)} %slice.12.refs_3_), channel_id=1, source_target_pairs={{0,6},{1,7},{2,4},{3,5},{4,2},{5,3},{6,0},{7,1},{8,14},{9,15},{10,... | collective-permute-start | bytes 393224 | tf_op jit(solution)/shard_map/ppermute | solution.py:24
  57.3 8.8 %collective-permute-start.6 = (bf16[128,512]{1,0:T(8,128)(2,1)S(1)}, bf16[128,512]{1,0:T(8,128)(2,1)S(1)}, u32[]{:S(2)}, u32[]{:S(2)}) collective-permute-start(bf16[128,512]{1,0:T(8,128)(2,1)S(1)} %slice.12.refs_3_), channel_id=1, source_target_pairs={{0,2},{1,3},{2,0},{3,1},{4,6},{5,7},{6,4},{7,5},{8,10},{9,11},{10,... | collective-permute-start | bytes 393224 | tf_op jit(solution)/shard_map/ppermute | solution.py:24
  57.8 0.8 copy-start.9
  58.6 7.4 %collective-permute-start.8 = (bf16[128,512]{1,0:T(8,128)(2,1)S(1)}, bf16[128,512]{1,0:T(8,128)(2,1)S(1)}, u32[]{:S(2)}, u32[]{:S(2)}) collective-permute-start(bf16[128,512]{1,0:T(8,128)(2,1)S(1)} %slice.12.refs_3_), channel_id=1, source_target_pairs={{0,4},{1,5},{2,6},{3,7},{4,0},{5,1},{6,2},{7,3},{8,12},{9,13},{10,... | collective-permute-start | bytes 393224 | tf_op jit(solution)/shard_map/ppermute | solution.py:24
  60.6 0.8 copy-start.11
  61.4 22.3 %collective-permute-start.5 = (bf16[128,512]{1,0:T(8,128)(2,1)S(1)}, bf16[128,512]{1,0:T(8,128)(2,1)S(1)}, u32[]{:S(2)}, u32[]{:S(2)}) collective-permute-start(bf16[128,512]{1,0:T(8,128)(2,1)S(1)} %slice.12.refs_3_), channel_id=1, source_target_pairs={{0,1},{1,0},{2,3},{3,2},{4,5},{5,4},{6,7},{7,6},{8,9},{9,8},{10,11... | collective-permute-start | bytes 393224 | tf_op jit(solution)/shard_map/ppermute | solution.py:24
  63.6 18.3 %collective-permute-start.14 = (bf16[128,512]{1,0:T(8,128)(2,1)S(1)}, bf16[128,512]{1,0:T(8,128)(2,1)S(1)}, u32[]{:S(2)}, u32[]{:S(2)}) collective-permute-start(bf16[128,512]{1,0:T(8,128)(2,1)S(1)} %add_convert_fusion.1), channel_id=1, source_target_pairs={{0,16},{1,17},{2,18},{3,19},{4,20},{5,21},{6,22},{7,23},{8,24},{9,... | collective-permute-start | bytes 393224 | tf_op jit(solution)/shard_map/ppermute | solution.py:24
  66.1 17.6 %collective-permute-start.11 = (bf16[128,512]{1,0:T(8,128)(2,1)S(1)}, bf16[128,512]{1,0:T(8,128)(2,1)S(1)}, u32[]{:S(2)}, u32[]{:S(2)}) collective-permute-start(bf16[128,512]{1,0:T(8,128)(2,1)S(1)} %collective-permute-done.10.refs_9_), channel_id=1, source_target_pairs={{0,1},{1,0},{2,3},{3,2},{4,5},{5,4},{6,7},{7,6},{8,9},{9,8},{10,11... | collective-permute-start | bytes 393224 | tf_op jit(solution)/shard_map/ppermute | solution.py:24
  66.1 20.0 %collective-permute-start.7 = (bf16[128,512]{1,0:T(8,128)(2,1)S(1)}, bf16[128,512]{1,0:T(8,128)(2,1)S(1)}, u32[]{:S(2)}, u32[]{:S(2)}) collective-permute-start(bf16[128,512]{1,0:T(8,128)(2,1)S(1)} %collective-permute-done.6.refs_5_), channel_id=1, source_target_pairs={{0,1},{1,0},{2,3},{3,2},{4,5},{5,4},{6,7},{7,6},{8,9},{9,8},{10,11... | collective-permute-start | bytes 393224 | tf_op jit(solution)/shard_map/ppermute | solution.py:24
  66.6 3.4 %copy-start.1 = (bf16[4096,1024]{1,0:T(8,128)(2,1)S(1)}, bf16[4096,1024]{1,0:T(8,128)(2,1)}, u32[]{:S(2)}) copy-start(bf16[4096,1024]{1,0:T(8,128)(2,1)} %vectors_ref.7) | copy-start | bytes 25165828
  70.0 3.4 %copy-start.2 = (bf16[4,16,256,256]{3,2,1,0:T(8,128)(2,1)S(1)}, bf16[4,16,256,256]{3,2,1,0:T(8,128)(2,1)}, u32[]{:S(2)}) copy-start(bf16[4,16,256,256]{3,2,1,0:T(8,128)(2,1)} %tiles_ref.7) | copy-start | bytes 25165828
  73.4 0.9 copy-start.14
  74.3 12.4 %copy-start.3 = (bf16[4,16,256,256]{3,2,1,0:T(8,128)(2,1)S(1)}, bf16[4,16,256,256]{3,2,1,0:T(8,128)(2,1)}, u32[]{:S(2)}) copy-start(bf16[4,16,256,256]{3,2,1,0:T(8,128)(2,1)} %tiles_ref.7) | copy-start | bytes 25165828
  81.8 14.9 %copy-start.10 = (bf16[2,1024,128]{2,1,0:T(8,128)(2,1)S(1)}, bf16[2,1024,128]{2,1,0:T(8,128)(2,1)}, u32[]{:S(2)}) copy-start(bf16[2,1024,128]{2,1,0:T(8,128)(2,1)} %copy-done.9) | copy-start | bytes 1572868
  81.8 14.9 %copy-start.12 = (bf16[2,1024,128]{2,1,0:T(8,128)(2,1)S(1)}, bf16[2,1024,128]{2,1,0:T(8,128)(2,1)}, u32[]{:S(2)}) copy-start(bf16[2,1024,128]{2,1,0:T(8,128)(2,1)} %copy-done.11) | copy-start | bytes 1572868
  81.9 13.3 %collective-permute-start.16 = (bf16[128,512]{1,0:T(8,128)(2,1)S(1)}, bf16[128,512]{1,0:T(8,128)(2,1)S(1)}, u32[]{:S(2)}, u32[]{:S(2)}) collective-permute-start(bf16[128,512]{1,0:T(8,128)(2,1)S(1)} %collective-permute-done.14.refs_3_), channel_id=1, source_target_pairs={{0,2},{1,3},{2,0},{3,1},{4,6},{5,7},{6,4},{7,5},{8,10},{9,11},{10,... | collective-permute-start | bytes 393224 | tf_op jit(solution)/shard_map/ppermute | solution.py:24
  83.6 11.6 %collective-permute-start.18 = (bf16[128,512]{1,0:T(8,128)(2,1)S(1)}, bf16[128,512]{1,0:T(8,128)(2,1)S(1)}, u32[]{:S(2)}, u32[]{:S(2)}) collective-permute-start(bf16[128,512]{1,0:T(8,128)(2,1)S(1)} %collective-permute-done.14.refs_3_), channel_id=1, source_target_pairs={{0,4},{1,5},{2,6},{3,7},{4,0},{5,1},{6,2},{7,3},{8,12},{9,13},{10,... | collective-permute-start | bytes 393224 | tf_op jit(solution)/shard_map/ppermute | solution.py:24
  83.6 0.7 copy-start.17
  84.3 11.4 %collective-permute-start.20 = (bf16[128,512]{1,0:T(8,128)(2,1)S(1)}, bf16[128,512]{1,0:T(8,128)(2,1)S(1)}, u32[]{:S(2)}, u32[]{:S(2)}) collective-permute-start(bf16[128,512]{1,0:T(8,128)(2,1)S(1)} %collective-permute-done.14.refs_3_), channel_id=1, source_target_pairs={{0,6},{1,7},{2,4},{3,5},{4,2},{5,3},{6,0},{7,1},{8,14},{9,15},{10,... | collective-permute-start | bytes 393224 | tf_op jit(solution)/shard_map/ppermute | solution.py:24
  86.1 10.7 %copy-start.18 = (bf16[128,512]{1,0:T(8,128)(2,1)S(1)}, bf16[128,512]{1,0:T(8,128)(2,1)}, u32[]{:S(2)}) copy-start(bf16[128,512]{1,0:T(8,128)(2,1)} %copy-done.17) | copy-start | bytes 393220
  86.1 0.7 copy-start.19
  86.7 7.9 %collective-permute-start.9 = (bf16[128,512]{1,0:T(8,128)(2,1)S(1)}, bf16[128,512]{1,0:T(8,128)(2,1)S(1)}, u32[]{:S(2)}, u32[]{:S(2)}) collective-permute-start(bf16[128,512]{1,0:T(8,128)(2,1)S(1)} %collective-permute-done.8.refs_7_), channel_id=1, source_target_pairs={{0,1},{1,0},{2,3},{3,2},{4,5},{5,4},{6,7},{7,6},{8,9},{9,8},{10,11... | collective-permute-start | bytes 393224 | tf_op jit(solution)/shard_map/ppermute | solution.py:24
  86.7 10.0 %copy-start.20 = (bf16[128,512]{1,0:T(8,128)(2,1)S(1)}, bf16[128,512]{1,0:T(8,128)(2,1)}, u32[]{:S(2)}) copy-start(bf16[128,512]{1,0:T(8,128)(2,1)} %copy-done.19) | copy-start | bytes 393220
  94.6 9.9 %copy-start.8 = (bf16[4096,128]{1,0:T(8,128)(2,1)S(1)}, bf16[4096,128]{1,0:T(8,128)(2,1)}, u32[]{:S(2)}) copy-start(bf16[4096,128]{1,0:T(8,128)(2,1)} %left_ref.3) | copy-start | bytes 3145732
  94.6 9.9 %collective-permute-start.15 = (bf16[128,512]{1,0:T(8,128)(2,1)S(1)}, bf16[128,512]{1,0:T(8,128)(2,1)S(1)}, u32[]{:S(2)}, u32[]{:S(2)}) collective-permute-start(bf16[128,512]{1,0:T(8,128)(2,1)S(1)} %collective-permute-done.14.refs_3_), channel_id=1, source_target_pairs={{0,1},{1,0},{2,3},{3,2},{4,5},{5,4},{6,7},{7,6},{8,9},{9,8},{10,11... | collective-permute-start | bytes 393224 | tf_op jit(solution)/shard_map/ppermute | solution.py:24
  95.2 9.3 %collective-permute-start.17 = (bf16[128,512]{1,0:T(8,128)(2,1)S(1)}, bf16[128,512]{1,0:T(8,128)(2,1)S(1)}, u32[]{:S(2)}, u32[]{:S(2)}) collective-permute-start(bf16[128,512]{1,0:T(8,128)(2,1)S(1)} %collective-permute-done.16.refs_5_), channel_id=1, source_target_pairs={{0,1},{1,0},{2,3},{3,2},{4,5},{5,4},{6,7},{7,6},{8,9},{9,8},{10,11... | collective-permute-start | bytes 393224 | tf_op jit(solution)/shard_map/ppermute | solution.py:24
  95.3 9.2 %collective-permute-start.19 = (bf16[128,512]{1,0:T(8,128)(2,1)S(1)}, bf16[128,512]{1,0:T(8,128)(2,1)S(1)}, u32[]{:S(2)}, u32[]{:S(2)}) collective-permute-start(bf16[128,512]{1,0:T(8,128)(2,1)S(1)} %collective-permute-done.18.refs_7_), channel_id=1, source_target_pairs={{0,1},{1,0},{2,3},{3,2},{4,5},{5,4},{6,7},{7,6},{8,9},{9,8},{10,11... | collective-permute-start | bytes 393224 | tf_op jit(solution)/shard_map/ppermute | solution.py:24
  95.7 8.8 %collective-permute-start.21 = (bf16[128,512]{1,0:T(8,128)(2,1)S(1)}, bf16[128,512]{1,0:T(8,128)(2,1)S(1)}, u32[]{:S(2)}, u32[]{:S(2)}) collective-permute-start(bf16[128,512]{1,0:T(8,128)(2,1)S(1)} %collective-permute-done.20.refs_9_), channel_id=1, source_target_pairs={{0,1},{1,0},{2,3},{3,2},{4,5},{5,4},{6,7},{7,6},{8,9},{9,8},{10,11... | collective-permute-start | bytes 393224 | tf_op jit(solution)/shard_map/ppermute | solution.py:24
  95.8 1.0 copy-start.15
  96.8 1.2 %copy-start.16 = (bf16[512,1024]{1,0:T(8,128)(2,1)S(1)}, bf16[512,1024]{1,0:T(8,128)(2,1)}, u32[]{:S(2)}) copy-start(bf16[512,1024]{1,0:T(8,128)(2,1)} %copy-done.15) | copy-start | bytes 3145732

commit v3 on v2

v3 whole, which is shorter than its diff:
```python
import jax
import jax.numpy as jnp
from jax import lax
from jax.experimental import pallas as pl
from jax.experimental.pallas import tpu as pltpu
from jax.sharding import PartitionSpec as P

B = 256
REACH = 2
AXES = ("rows", "cols")
VMEM = 64 * 1024 * 1024
COST_A = 1
COST_B = 10**10
COST_C = 1
HBM = pl.BlockSpec(memory_space=pltpu.HBM)
SMEM = pl.BlockSpec(memory_space=pltpu.SMEM)


def moved(value, target):
    n_rows, n_cols = lax.axis_size("rows"), lax.axis_size("cols")
    pairs = []
    for row in range(n_rows):
        for col in range(n_cols):
            other = target(row, col)
            if other is not None and 0 <= other[0] < n_rows:
                pairs.append((row * n_cols + col, other[0] * n_cols + other[1]))
    return lax.ppermute(value, AXES, pairs)


def flipped(value, row_bits, col_bits):
    return moved(value, lambda row, col: (row ^ row_bits, col ^ col_bits))


def span(index, size):
    return pl.ds(pl.multiple_of(index * size, size), size)


def called(kernel, name, smem, hbm, after, out_shape, scratch, aliases={}, flops=1):
    return pl.pallas_call(
        kernel,
        out_shape=out_shape,
        in_specs=[SMEM] * len(smem) + [HBM] * (len(hbm) + len(after)),
        out_specs=jax.tree.map(lambda _: HBM, out_shape),
        scratch_shapes=scratch,
        input_output_aliases=aliases,
        compiler_params=pltpu.CompilerParams(vmem_limit_bytes=VMEM),
        cost_estimate=pl.CostEstimate(flops=flops, bytes_accessed=1, transcendentals=0),
        name=name,
    )(*smem, *hbm, *after)


def project(right_one, right_two, vectors):
    depth, rank = right_one.shape
    width = vectors.shape[1]
    half = width // 2
    step = REACH * B
    parts = depth // step

    def kernel(one_ref, two_ref, vectors_ref, send_ref, keep_ref, token_ref, edge_ref, *scratch):
        rights, block, total, result, right_sems, block_sems, out_sems, edge_sems = scratch
        mine, last_first = lax.axis_index("rows") % 2, lax.axis_index("cols") % 2 == 0
        copies, places = [], []
        for i in range(parts):
            place = span(jnp.where(last_first, parts - 1 - i, i), step)
            places.append(place)
            copies.append(
                [
                    pltpu.make_async_copy(
                        ref.at[place], rights.at[place, pl.ds(level * rank, rank)], right_sems.at[level, i]
                    )
                    for level, ref in enumerate((one_ref, two_ref))
                ]
                + [pltpu.make_async_copy(vectors_ref.at[place], block.at[place], block_sems.at[i])]
            )
            for copy in copies[-1]:
                copy.start()
        edge_copy = pltpu.make_async_copy(block.at[places[0]], edge_ref, edge_sems.at[0])
        for i in range(parts):
            for copy in copies[i]:
                copy.wait()
            if i == 0:
                edge_copy.start()
            part = lax.dot_general(
                rights[places[i]], block[places[i]], (((0,), (0,)), ((), ())), preferred_element_type=jnp.float32
            )
            if i == 0:
                total[...] = part
            elif i < parts - 1:
                total[...] += part
            else:
                result[...] = (total[...] + part).astype(jnp.bfloat16)
        outs = [pltpu.make_async_copy(result.at[pl.ds(0, 16), pl.ds(0, 128)], token_ref, edge_sems.at[1])]
        for k, (ref, chosen) in enumerate(((send_ref, mine ^ 1), (keep_ref, mine))):
            outs.append(
                pltpu.make_async_copy(
                    result.at[pl.ds(0, rank), span(chosen, half)], ref.at[pl.ds(0, rank)], out_sems.at[k, 0]
                )
            )
            for n in range(2):
                outs.append(
                    pltpu.make_async_copy(
                        result.at[pl.ds(rank, rank), pl.ds(n * half, half)],
                        ref.at[pl.ds((1 + n) * rank, rank)],
                        out_sems.at[k, 1 + n],
                    )
                )
        for copy in outs:
            copy.start()
        for copy in outs:
            copy.wait()
        edge_copy.wait()

    return called(
        kernel,
        "project",
        [],
        [right_one, right_two, vectors],
        (),
        [
            jax.ShapeDtypeStruct((3 * rank, half), jnp.bfloat16),
            jax.ShapeDtypeStruct((3 * rank, half), jnp.bfloat16),
            jax.ShapeDtypeStruct((16, 128), jnp.bfloat16),
            jax.ShapeDtypeStruct((step, width), jnp.bfloat16),
        ],
        [
            pltpu.VMEM((depth, 2 * rank), jnp.bfloat16),
            pltpu.VMEM((depth, width), jnp.bfloat16),
            pltpu.VMEM((2 * rank, width), jnp.float32),
            pltpu.VMEM((2 * rank, width), jnp.bfloat16),
            pltpu.SemaphoreType.DMA((2, parts)),
            pltpu.SemaphoreType.DMA((parts,)),
            pltpu.SemaphoreType.DMA((2, 3)),
            pltpu.SemaphoreType.DMA((2,)),
        ],
    )


def near_inside(slots, near_tiles, vectors, first, count, sofar, lefts, flops, after=()):
    tiles = near_tiles.shape[0]
    rows, width = tiles * B, vectors.shape[1]
    group = 2
    groups = count // group
    half = width // 2
    given = 0 if sofar is None else 1
    shares = lefts[0].shape[0] // rows if lefts else 0
    more = 1 if lefts else 0
    rank = lefts[0].shape[1] if lefts else 0

    def kernel(slots_ref, tiles_ref, vectors_ref, *refs):
        sofar_refs, refs = refs[:given], refs[given:]
        left_refs, refs = refs[: len(lefts)], refs[len(lefts) + len(after) :]
        out_ref, pack_refs, refs = refs[0], refs[1 : 1 + more], refs[1 + more :]
        wide, tall, total, result, tile_sems, vector_sems, sofar_sem, out_sems = refs[:8]

        def tile_copy(t, c):
            slot = slots_ref[t, first + c + REACH]
            copy = pltpu.make_async_copy(
                tiles_ref.at[t, jnp.maximum(slot, 0)],
                wide.at[pl.ds(t * B, B), pl.ds(c * B, B)],
                tile_sems.at[t, c],
            )
            return slot >= 0, copy

        def vector_copy(c):
            return pltpu.make_async_copy(
                vectors_ref.at[pl.ds((first + c) * B, B)], tall.at[pl.ds(c * B, B)], vector_sems.at[c]
            )

        if given:
            sofar_copy = pltpu.make_async_copy(sofar_refs[0], result, sofar_sem)
        for c in range(count):
            vector_copy(c).start()
            for t in range(tiles):
                there, copy = tile_copy(t, c)
                pl.when(there)(copy.start)

                @pl.when(jnp.logical_not(there))
                def _():
                    wide[t * B : (t + 1) * B, c * B : (c + 1) * B] = jnp.zeros((B, B), jnp.bfloat16)

            if given and c == group - 1:
                sofar_copy.start()
        ins, outs = [], []
        if lefts:
            packed, in_sems, pack_sem = refs[8:]
            for d in range(shares):
                for level, ref in enumerate(left_refs):
                    ins.append(
                        pltpu.make_async_copy(
                            ref.at[pl.ds(d * rows, rows)], packed.at[d, level], in_sems.at[d, level]
                        )
                    )
            outs.append(pltpu.make_async_copy(packed, pack_refs[0], pack_sem))
            for copy in ins:
                copy.start()
        for g in range(groups):
            for c in range(g * group, (g + 1) * group):
                vector_copy(c).wait()
                for t in range(tiles):
                    there, copy = tile_copy(t, c)
                    pl.when(there)(copy.wait)
            chosen = pl.ds(g * group * B, group * B)
            if g == groups - 1:
                if given:
                    sofar_copy.wait()
                for copy in ins:
                    copy.wait()
                for copy in outs:
                    copy.start()
            for n in range(2):
                columns = pl.ds(n * half, half)
                part = jnp.dot(wide[:, chosen], tall[chosen, columns], preferred_element_type=jnp.float32)
                if g > 0:
                    part = total[:, columns] + part
                if g < groups - 1:
                    total[:, columns] = part
                else:
                    if given:
                        part = part + result[:, columns].astype(jnp.float32)
                    result[:, columns] = part.astype(jnp.bfloat16)
                    outs.append(
                        pltpu.make_async_copy(result.at[:, columns], out_ref.at[:, columns], out_sems.at[n])
                    )
                    outs[-1].start()
        for copy in outs:
            copy.wait()

    scratch = [
        pltpu.VMEM((rows, count * B), jnp.bfloat16),
        pltpu.VMEM((count * B, width), jnp.bfloat16),
        pltpu.VMEM((rows, width), jnp.float32),
        pltpu.VMEM((rows, width), jnp.bfloat16),
        pltpu.SemaphoreType.DMA((tiles, count)),
        pltpu.SemaphoreType.DMA((count,)),
        pltpu.SemaphoreType.DMA,
        pltpu.SemaphoreType.DMA((2,)),
    ]
    if lefts:
        scratch += [
            pltpu.VMEM((shares, 2, rows, rank), jnp.bfloat16),
            pltpu.SemaphoreType.DMA((shares, 2)),
            pltpu.SemaphoreType.DMA,
        ]
    return called(
        kernel,
        "near_inside",
        [slots],
        [near_tiles, vectors] + ([sofar] if given else []) + [*lefts],
        after,
        [jax.ShapeDtypeStruct((rows, width), jnp.bfloat16)]
        + [jax.ShapeDtypeStruct((shares, 2, rows, rank), jnp.bfloat16)] * more,
        scratch,
        flops=flops,
    )


def add_halos(slots, sofar, near_tiles, halos, after=()):
    rows, width = sofar.shape
    tiles = rows // B
    half = width // 2
    outside = 2 * REACH
    window = slots.shape[1]

    def kernel(slots_ref, sofar_ref, tiles_ref, *refs):
        halo_refs, refs = refs[:2], refs[2 + len(after) :]
        out_ref, wide, tall, total, result, tile_sems, halo_sems, sofar_sem, out_sems = refs
        core = lax.axis_index("cols") % 2

        def tile_copy(t, i):
            before = (i < REACH) == (core == 0)
            slot = slots_ref[t, jnp.where(before, i % REACH, window - REACH + i % REACH)]
            copy = pltpu.make_async_copy(
                tiles_ref.at[t, jnp.maximum(slot, 0)],
                wide.at[pl.ds(t * B, B), pl.ds(i * B, B)],
                tile_sems.at[t, i],
            )
            return slot >= 0, copy

        copies = [
            pltpu.make_async_copy(ref, tall.at[pl.ds(i * REACH * B, REACH * B)], halo_sems.at[i])
            for i, ref in enumerate(halo_refs)
        ]
        sofar_copy = pltpu.make_async_copy(sofar_ref, result, sofar_sem)
        for i in range(outside):
            if i % REACH == 0:
                copies[i // REACH].start()
            for t in range(tiles):
                there, copy = tile_copy(t, i)
                pl.when(there)(copy.start)

                @pl.when(jnp.logical_not(there))
                def _():
                    wide[t * B : (t + 1) * B, i * B : (i + 1) * B] = jnp.zeros((B, B), jnp.bfloat16)

        sofar_copy.start()
        out_copies = []
        for side in range(2):
            copies[side].wait()
            for i in range(side * REACH, (side + 1) * REACH):
                for t in range(tiles):
                    there, copy = tile_copy(t, i)
                    pl.when(there)(copy.wait)
            chosen = pl.ds(side * REACH * B, REACH * B)
            if side == 1:
                sofar_copy.wait()
            for n in range(2):
                columns = pl.ds(n * half, half)
                part = jnp.dot(wide[:, chosen], tall[chosen, columns], preferred_element_type=jnp.float32)
                if side == 0:
                    total[:, columns] = part
                else:
                    part = total[:, columns] + part + result[:, columns].astype(jnp.float32)
                    result[:, columns] = part.astype(jnp.bfloat16)
                    out_copies.append(
                        pltpu.make_async_copy(result.at[:, columns], out_ref.at[:, columns], out_sems.at[n])
                    )
                    out_copies[-1].start()
        for copy in out_copies:
            copy.wait()

    return called(
        kernel,
        "add_halos",
        [slots],
        [sofar, near_tiles, *halos],
        after,
        jax.ShapeDtypeStruct((rows, width), jnp.bfloat16),
        [
            pltpu.VMEM((rows, outside * B), jnp.bfloat16),
            pltpu.VMEM((outside * B, width), jnp.bfloat16),
            pltpu.VMEM((rows, width), jnp.float32),
            pltpu.VMEM((rows, width), jnp.bfloat16),
            pltpu.SemaphoreType.DMA((tiles, outside)),
            pltpu.SemaphoreType.DMA((2,)),
            pltpu.SemaphoreType.DMA,
            pltpu.SemaphoreType.DMA((2,)),
        ],
        flops=COST_C,
    )


def add_level(sofar, level, panels, coeffs):
    rows, width = sofar.shape
    half = width // 2
    offsets, _, _, rank = panels.shape
    whole = len(coeffs) == offsets
    inner = offsets * rank

    def kernel(sofar_ref, panels_ref, *refs):
        coeff_refs, refs = refs[: len(coeffs)], refs[len(coeffs) :]
        out_ref, lefts, ranks, result, left_sems, coeff_sems, sofar_sems, out_sems = refs
        mine, col = lax.axis_index("rows") % 2, lax.axis_index("cols")
        first, later = [], []
        for d in range(offsets):
            first.append(
                pltpu.make_async_copy(
                    panels_ref.at[col ^ d, level], lefts.at[:, pl.ds(d * rank, rank)], left_sems.at[d]
                )
            )
            for n in range(2):
                source = coeff_refs[d].at[pl.ds(n * rank, rank)] if whole else coeff_refs[n * offsets + d]
                (later if n else first).append(
                    pltpu.make_async_copy(source, ranks.at[n, pl.ds(d * rank, rank)], coeff_sems.at[n, d])
                )
        places = [pl.ds(n * half, half) if whole else span(mine ^ n, half) for n in range(2)]
        for n, copies in enumerate((first, later)):
            copies.append(
                pltpu.make_async_copy(sofar_ref.at[:, places[n]], result.at[n], sofar_sems.at[n])
            )
            for copy in copies:
                copy.start()
        out_copies = []
        for n, copies in enumerate((first, later)):
            for copy in copies:
                copy.wait()
            part = jnp.dot(lefts[...], ranks[n], preferred_element_type=jnp.float32)
            result[n] = (result[n].astype(jnp.float32) + part).astype(jnp.bfloat16)
            out_copies.append(
                pltpu.make_async_copy(result.at[n], out_ref.at[:, places[n]], out_sems.at[n])
            )
            out_copies[-1].start()
        for copy in out_copies:
            copy.wait()

    return called(
        kernel,
        "add_level",
        [],
        [sofar, panels, *coeffs],
        (),
        jax.ShapeDtypeStruct((rows, width), jnp.bfloat16),
        [
            pltpu.VMEM((rows, inner), jnp.bfloat16),
            pltpu.VMEM((2, inner, half), jnp.bfloat16),
            pltpu.VMEM((2, rows, half), jnp.bfloat16),
            pltpu.SemaphoreType.DMA((offsets,)),
            pltpu.SemaphoreType.DMA((2, offsets)),
            pltpu.SemaphoreType.DMA((2,)),
            pltpu.SemaphoreType.DMA((2,)),
        ],
    )


def summed(a, b, rank, swapped, passed=(), after=()):
    rows, width = a.shape
    outs = [(rank, width), (rows - rank, width)] if swapped else [(rows, width), (16, 128)]
    top = outs[0][0]

    def kernel(a_ref, b_ref, *refs):
        refs = refs[len(passed) + len(after) :]
        out_refs, (mine, theirs, total, in_sems, out_sems) = refs[: len(outs)], refs[-5:]
        ins = [
            pltpu.make_async_copy(a_ref.at[pl.ds(0, top)], mine, in_sems.at[0]),
            pltpu.make_async_copy(b_ref, theirs, in_sems.at[1]),
        ]
        for copy in ins:
            copy.start()
        for copy in ins:
            copy.wait()
        total[...] = (mine[...].astype(jnp.float32) + theirs[:top].astype(jnp.float32)).astype(jnp.bfloat16)
        results = [pltpu.make_async_copy(total, out_refs[0], out_sems.at[0])]
        other = theirs.at[pl.ds(top, rows - top)] if swapped else total.at[pl.ds(0, 16), pl.ds(0, 128)]
        results.append(pltpu.make_async_copy(other, out_refs[1], out_sems.at[1]))
        for copy in results:
            copy.start()
        for copy in results:
            copy.wait()

    return called(
        kernel,
        "summed",
        [],
        [a, b, *passed],
        after,
        [jax.ShapeDtypeStruct(shape, jnp.bfloat16) for shape in outs]
        + [jax.ShapeDtypeStruct(x.shape, x.dtype) for x in passed],
        [
            pltpu.VMEM((top, width), jnp.bfloat16),
            pltpu.VMEM((rows, width), jnp.bfloat16),
            pltpu.VMEM((top, width), jnp.bfloat16),
            pltpu.SemaphoreType.DMA((2,)),
            pltpu.SemaphoreType.DMA((2,)),
        ],
        {2 + i: len(outs) + i for i in range(len(passed))},
    )


def held(passed, after):
    def kernel(*refs):
        pass

    return called(
        kernel,
        "held",
        [],
        passed,
        after,
        [jax.ShapeDtypeStruct(x.shape, x.dtype) for x in passed],
        [],
        {i: i for i in range(len(passed))},
    )


def per_device(vectors, near_tiles, near_cols, left_one, right_one, left_two, right_two):
    n_rows, n_cols = lax.axis_size("rows"), lax.axis_size("cols")
    bits = n_rows.bit_length() - 1
    col = lax.axis_index("cols")
    depth = vectors.shape[0]
    rank = right_one.shape[1]
    inside = depth // B

    nnz = near_cols.shape[1]
    names = near_cols[:, :, None] == jnp.arange(inside + 2 * REACH, dtype=jnp.int32)
    slots = jnp.max(jnp.where(names, jnp.arange(nnz, dtype=jnp.int32)[None, :, None], -1), axis=1)

    cuts = [0, inside // 2, inside]

    def near_part(part, sofar, lefts=(), after=()):
        first, last = cuts[part : part + 2]
        return near_inside(slots, near_tiles, vectors, first, last - first, sofar, lefts, COST_B if last == inside else COST_A, after)

    send, keep, token, edge = project(right_one, right_two, vectors)
    arrived = flipped(send, 1, 0)

    (edge,) = held([edge], [flipped(token, 0, 1)])
    halo = moved(edge, lambda r, c: (r + 1 if c % 2 == 0 else r - 1, c))

    near, panels = near_part(0, None, (left_one, left_two), after=(keep,))
    both, _ = summed(keep, arrived, rank, False, after=(near,))
    for bit in range(1, bits - 2):
        both, _ = summed(both, flipped(both, 2**bit, 0), rank, False)
    arrived = flipped(both, 2 ** (bits - 2), 0)
    panels = lax.all_to_all(panels, "cols", split_axis=0, concat_axis=0, tiled=True)
    (near,) = near_part(1, near, after=(both,))
    one, two, halo = summed(both, arrived, rank, True, passed=(halo,), after=(near,))
    one = flipped(one, 2 ** (bits - 1), 0)
    near = add_halos(slots, near, near_tiles, (halo, flipped(halo, 0, 1)), after=(two,))

    offsets = range(0, n_cols, 2)
    twos = [two] + [flipped(two, 0, offset) for offset in offsets[1:]]
    one, *rest = held([one, *twos[1:]], [near])
    twos = [two] + rest
    ones = [
        one if (other, offset) == (0, 0) else flipped(one, other, offset)
        for other in range(2)
        for offset in offsets
    ]
    coeffs_two = [x for there in twos for x in (there, flipped(there, 0, 1))]
    near = add_level(near, 1, panels, coeffs_two)
    ones = [one, *held(ones[1:], [near])]
    coeffs_one = [x for there in ones for x in (there, flipped(there, 0, 1))]
    return add_level(near, 0, panels, coeffs_one)


def solution(mesh):
    placed = (
        P("rows", None),
        P(("rows", "cols"), None, None, None),
        P(("rows", "cols"), None),
        P("rows", "cols"),
        P("rows", "cols"),
        P("rows", "cols"),
        P("rows", "cols"),
    )
    return jax.shard_map(
        per_device, mesh=mesh, in_specs=placed, out_specs=P(("rows", "cols"), None), check_vma=False
    )
```

time: 109 us -> 77.2 us (0.71)
  waiting for transfers between devices: 33 us -> 10.3 us
  local copies, waits for them, and re-layouts: 18.8 us -> 0 us
  Pallas kernels: 32.3 us -> 42.3 us
    ppermute x22 -> x16, waiting for transfers between devices: 33 us -> 10.3 us  [moved(): return lax.ppermute(value, AXES, pairs)]
    unnamed x44 -> x0, local copies, waits for them, and re-layouts: 18.7 us -> none
    pallas_call x6 -> x11, Pallas kernels: 32.3 us -> 42.3 us  [called(): pl.pallas_call(kernel, out_shape=out_shape, in_specs=[SMEM] * len(smem) +...]
    all_to_all x0 -> x1, starting transfers between devices: none -> 4.47 us  [per_device(): lax.all_to_all(panels, 'cols', split_axis=0, concat_axis=0, tiled=True)]
    ppermute x22 -> x16, starting transfers between devices: 22.2 us -> 18 us  [moved(): return lax.ppermute(value, AXES, pairs)]
    reduce_max x1, other arithmetic: 0.09 us -> 1.35 us  [per_device(): jnp.max(jnp.where(names, jnp.arange(nnz, dtype=jnp.int32)[None, :, None],...]
  transfers between devices with their start and end apart: 22 -> 17, of which waited for: 3 -> 8; matrix products, arithmetic and copies ran while one was open for 1% -> 2% of each run, Pallas kernels for 20% -> 41%
where the time goes in v3:
time: 77.2 us; the launch traced here: 76.7 us
  Pallas kernels  42.3 us (55%)
  starting transfers between devices  22.5 us (29%)
  waiting for transfers between devices  10.3 us (13%)
  other arithmetic  1.35 us (2%)
    pallas_call x11, Pallas kernels, called(): pl.pallas_call(kernel, out_shape=out_shape, in_specs=[SMEM] * len(smem) +...  42.3 us
    ppermute x16, starting transfers between devices, moved(): return lax.ppermute(value, AXES, pairs)  18 us
    ppermute x16, waiting for transfers between devices, moved(): return lax.ppermute(value, AXES, pairs)  10.3 us
    all_to_all x1, starting transfers between devices, per_device(): lax.all_to_all(panels, 'cols', split_axis=0, concat_axis=0, tiled=True)  4.47 us
  transfers between devices with their start and end apart: 17, of which 8 were waited for; matrix products, arithmetic and copies ran while one was open for 2% of the time, Pallas kernels for 41%

profile of v3, /device:TPU:0, one launch (start us, length us, event | category | flops | bytes accessed | tf_op | source)
XLA Modules:
  0.0 76.7 jit_solution(7587014885626414843)
XLA Ops:
  0.0 6.1 %project.1 = (bf16[384,512]{1,0:T(8,128)(2,1)}, bf16[384,512]{1,0:T(8,128)(2,1)}, bf16[16,128]{1,0:T(8,128)(2,1)}, bf16[512,1024]{1,0:T(8,128)(2,1)}) custom-call(bf16[4096,128]{1,0:T(8,128)(2,1)} %one_ref.1, bf16[4096,128]{1,0:T(8,128)(2,1)} %two_ref.1, bf16[4096,1024]{1,0:T(8,128)(2,1)} %vectors_ref.5), custom_call_target="tpu_custom_call" | custom-call | flops 1 | bytes 1 | tf_op jit(solution)/shard_map/project/pallas_call | solution.py:39
  6.1 3.0 %collective-permute-start = (bf16[384,512]{1,0:T(8,128)(2,1)}, bf16[384,512]{1,0:T(8,128)(2,1)}, u32[]{:S(2)}, u32[]{:S(2)}) collective-permute-start(bf16[384,512]{1,0:T(8,128)(2,1)} %get-tuple-element.22), channel_id=1, source_target_pairs={{0,4},{1,5},{2,6},{3,7},{4,0},{5,1},{6,2},{7,3},{8,12},{9,13},{10,... | collective-permute-start | bytes 1179656 | tf_op jit(solution)/shard_map/ppermute | solution.py:27
  9.1 0.0 collective-permute-start.2
  9.1 1.5 %collective-permute-done.2.refs_1_ = bf16[16,128]{1,0:T(8,128)(2,1)} collective-permute-done((bf16[16,128]{1,0:T(8,128)(2,1)}, bf16[16,128]{1,0:T(8,128)(2,1)}, u32[]{:S(2)}, u32[]{:S(2)}) %collective-permute-start.2) | collective-permute-done | bytes 4128 | tf_op jit(solution)/shard_map/ppermute | solution.py:27
  10.6 3.0 %collective-permute-start.3 = (bf16[512,1024]{1,0:T(8,128)(2,1)}, bf16[512,1024]{1,0:T(8,128)(2,1)}, u32[]{:S(2)}, u32[]{:S(2)}) collective-permute-start(bf16[512,1024]{1,0:T(8,128)(2,1)} %held.3), channel_id=1, source_target_pairs={{0,4},{2,6},{4,8},{5,1},{6,10},{7,3},{8,12},{9,5},{10,14},{11,7},{... | collective-permute-start | bytes 3145736 | tf_op jit(solution)/shard_map/ppermute | solution.py:27
  13.6 1.3 %select_reduce_fusion.slots_ref = s32[4,20]{1,0:T(4,128)} fusion(s32[4,16]{1,0:T(4,128)} %param.9), kind=kLoop, calls=%fused_computation | loop fusion | flops 3760 | bytes 576 | tf_op jit(solution)/shard_map/reduce_max | solution.py:474
  14.9 8.7 %near_inside.2 = (bf16[1024,1024]{1,0:T(8,128)(2,1)}, bf16[4,2,1024,128]{3,2,1,0:T(8,128)(2,1)}) custom-call(s32[4,20]{1,0:T(4,128)} %select_reduce_fusion.slots_ref, bf16[4,16,256,256]{3,2,1,0:T(8,128)(2,1)} %tiles_ref.5, bf16[4096,1024]{1,0:T(8,128)(2,1)} %vectors_ref.5, bf16[4096,128]{1,0:T(8,128)(2,1)} %refs_0_.1, bf16[4096,128]{1,0:T(8,128)(2,1)} %refs_1_.1, ...), custom_call_target="tpu_custom_call" | custom-call | flops 1 | bytes 1 | tf_op jit(solution)/shard_map/near_inside/pallas_call | solution.py:39
  23.7 4.5 %all-to-all-start = ((bf16[4,2,1024,128]{3,2,1,0:T(8,128)(2,1)}), bf16[4,2,1024,128]{3,2,1,0:T(8,128)(2,1)}, u32[]{:S(2)}, u32[]{:S(2)}) async-start(bf16[4,2,1024,128]{3,2,1,0:T(8,128)(2,1)} %get-tuple-element.28), calls=%async_computation | async-start | bytes 4194304 | tf_op jit(solution)/shard_map/all_to_all | solution.py:493
  28.1 0.9 %collective-permute-done.b_ref = bf16[384,512]{1,0:T(8,128)(2,1)} collective-permute-done((bf16[384,512]{1,0:T(8,128)(2,1)}, bf16[384,512]{1,0:T(8,128)(2,1)}, u32[]{:S(2)}, u32[]{:S(2)}) %collective-permute-start) | collective-permute-done | bytes 393248 | tf_op jit(solution)/shard_map/ppermute | solution.py:27
  29.0 2.0 %summed.2 = (bf16[384,512]{1,0:T(8,128)(2,1)}, bf16[16,128]{1,0:T(8,128)(2,1)}) custom-call(bf16[384,512]{1,0:T(8,128)(2,1)} %get-tuple-element.20.refs_2_.a_ref, bf16[384,512]{1,0:T(8,128)(2,1)} %collective-permute-done.b_ref, bf16[1024,1024]{1,0:T(8,128)(2,1)} %get-tuple-element.21.refs_0_), custom_call_target="tpu_custom_call" | custom-call | flops 1 | bytes 1 | tf_op jit(solution)/shard_map/summed/pallas_call | solution.py:39
  31.1 3.8 %collective-permute-start.1 = (bf16[384,512]{1,0:T(8,128)(2,1)}, bf16[384,512]{1,0:T(8,128)(2,1)}, u32[]{:S(2)}, u32[]{:S(2)}) collective-permute-start(bf16[384,512]{1,0:T(8,128)(2,1)} %get-tuple-element.23.refs_1_.a_ref), channel_id=1, source_target_pairs={{0,8},{1,9},{2,10},{3,11},{4,12},{5,13},{6,14},{7,15},{8,0},{9,1},... | collective-permute-start | bytes 1179656 | tf_op jit(solution)/shard_map/ppermute | solution.py:27
  34.9 8.7 %near_inside.3.refs_1_.sofar_ref = bf16[1024,1024]{1,0:T(8,128)(2,1)} custom-call(s32[4,20]{1,0:T(4,128)} %select_reduce_fusion.slots_ref, bf16[4,16,256,256]{3,2,1,0:T(8,128)(2,1)} %tiles_ref.5, bf16[4096,1024]{1,0:T(8,128)(2,1)} %vectors_ref.5, bf16[1024,1024]{1,0:T(8,128)(2,1)} %get-tuple-element.21.refs_0_, bf16[384,512]{1,0:T(8,128)(2,1)} %get-tuple-element.23.refs_1_.a_ref), custom_call_target="tpu_custom_call" | custom-call | flops 10000000000 | bytes 1 | tf_op jit(solution)/shard_map/near_inside/pallas_call | solution.py:39
  43.6 0.0 collective-permute-done.1.b_ref
  43.6 0.0 collective-permute-done.3.refs_0_
  43.6 1.9 %summed.3 = (bf16[128,512]{1,0:T(8,128)(2,1)}, bf16[256,512]{1,0:T(8,128)(2,1)}, bf16[512,1024]{1,0:T(8,128)(2,1)}) custom-call(bf16[384,512]{1,0:T(8,128)(2,1)} %get-tuple-element.23.refs_1_.a_ref, bf16[384,512]{1,0:T(8,128)(2,1)} %collective-permute-done.1.b_ref, ...), custom_call_target="tpu_custom_call", output_to_operand_aliasing={{2}: (2, {})} | custom-call | flops 1 | bytes 1 | tf_op jit(solution)/shard_map/summed/pallas_call | solution.py:39
  45.5 0.1 collective-permute-start.4
  45.6 1.5 %collective-permute-start.7 = (bf16[256,512]{1,0:T(8,128)(2,1)}, bf16[256,512]{1,0:T(8,128)(2,1)}, u32[]{:S(2)}, u32[]{:S(2)}) collective-permute-start(bf16[256,512]{1,0:T(8,128)(2,1)} %get-tuple-element.27.refs_2_.refs_0_), channel_id=1, source_target_pairs={{0,2},{1,3},{2,0},{3,1},{4,6},{5,7},{6,4},{7,5},{8,10},{9,11},{10,... | collective-permute-start | bytes 786440 | tf_op jit(solution)/shard_map/ppermute | solution.py:27
  47.1 2.7 %collective-permute-start.6 = (bf16[128,512]{1,0:T(8,128)(2,1)}, bf16[128,512]{1,0:T(8,128)(2,1)}, u32[]{:S(2)}, u32[]{:S(2)}) collective-permute-start(bf16[128,512]{1,0:T(8,128)(2,1)} %get-tuple-element.29), channel_id=1, source_target_pairs={{0,16},{1,17},{2,18},{3,19},{4,20},{5,21},{6,22},{7,23},{8,24},{9,... | collective-permute-start | bytes 393224 | tf_op jit(solution)/shard_map/ppermute | solution.py:27
  49.8 0.0 collective-permute-start.5
  49.8 0.0 collective-permute-done.4.refs_1_
  49.8 6.0 %add_halos.1.refs_2_.sofar_ref = bf16[1024,1024]{1,0:T(8,128)(2,1)} custom-call(s32[4,20]{1,0:T(4,128)} %select_reduce_fusion.slots_ref, bf16[1024,1024]{1,0:T(8,128)(2,1)} %near_inside.3.refs_1_.sofar_ref, bf16[4,16,256,256]{3,2,1,0:T(8,128)(2,1)} %tiles_ref.5, bf16[512,1024]{1,0:T(8,128)(2,1)} %get-tuple-element.26.refs_0_, ...), custom_call_target="tpu_custom_call" | custom-call | flops 1 | bytes 1 | tf_op jit(solution)/shard_map/add_halos/pallas_call | solution.py:39
  55.8 0.8 %collective-permute-done.6.refs_0_ = bf16[128,512]{1,0:T(8,128)(2,1)} collective-permute-done((bf16[128,512]{1,0:T(8,128)(2,1)}, bf16[128,512]{1,0:T(8,128)(2,1)}, u32[]{:S(2)}, u32[]{:S(2)}) %collective-permute-start.6) | collective-permute-done | bytes 131104 | tf_op jit(solution)/shard_map/ppermute | solution.py:27
  56.6 2.9 %collective-permute-done.7.refs_1_ = bf16[256,512]{1,0:T(8,128)(2,1)} collective-permute-done((bf16[256,512]{1,0:T(8,128)(2,1)}, bf16[256,512]{1,0:T(8,128)(2,1)}, u32[]{:S(2)}, u32[]{:S(2)}) %collective-permute-start.7) | collective-permute-done | bytes 262176 | tf_op jit(solution)/shard_map/ppermute | solution.py:27
  59.5 0.0 collective-permute-start.8
  59.5 0.4 collective-permute-start.10
  59.9 2.0 %collective-permute-start.11 = (bf16[128,512]{1,0:T(8,128)(2,1)}, bf16[128,512]{1,0:T(8,128)(2,1)}, u32[]{:S(2)}, u32[]{:S(2)}) collective-permute-start(bf16[128,512]{1,0:T(8,128)(2,1)} %get-tuple-element.31.refs_0_), channel_id=1, source_target_pairs={{0,4},{1,5},{2,6},{3,7},{4,0},{5,1},{6,2},{7,3},{8,12},{9,13},{10,... | collective-permute-start | bytes 393224 | tf_op jit(solution)/shard_map/ppermute | solution.py:27
  61.8 1.2 %collective-permute-start.12 = (bf16[128,512]{1,0:T(8,128)(2,1)}, bf16[128,512]{1,0:T(8,128)(2,1)}, u32[]{:S(2)}, u32[]{:S(2)}) collective-permute-start(bf16[128,512]{1,0:T(8,128)(2,1)} %get-tuple-element.31.refs_0_), channel_id=1, source_target_pairs={{0,6},{1,7},{2,4},{3,5},{4,2},{5,3},{6,0},{7,1},{8,14},{9,15},{10,... | collective-permute-start | bytes 393224 | tf_op jit(solution)/shard_map/ppermute | solution.py:27
  63.0 0.0 collective-permute-done.5.refs_1_
  63.0 0.0 collective-permute-start.9
  63.0 0.0 all-to-all-done.panels_ref
  63.0 0.0 collective-permute-done.8.refs_3_
  63.0 4.4 %add_level.2.refs_3_.sofar_ref = bf16[1024,1024]{1,0:T(8,128)(2,1)} custom-call(bf16[1024,1024]{1,0:T(8,128)(2,1)} %add_halos.1.refs_2_.sofar_ref, bf16[4,2,1024,128]{3,2,1,0:T(8,128)(2,1)} %all-to-all-done.panels_ref, bf16[256,512]{1,0:T(8,128)(2,1)} %get-tuple-element.27.refs_2_.refs_0_, bf16[256,512]{1,0:T(8,128)(2,1)} %collective-permute-done.5.refs_1_, ...), custom_call_target="tpu_custom_call" | custom-call | flops 1 | bytes 1 | tf_op jit(solution)/shard_map/add_level/pallas_call | solution.py:39
  67.5 0.0 collective-permute-done.10.refs_0_
  67.5 0.0 collective-permute-done.11.refs_1_
  67.5 2.5 %collective-permute-done.12.refs_2_ = bf16[128,512]{1,0:T(8,128)(2,1)} collective-permute-done((bf16[128,512]{1,0:T(8,128)(2,1)}, bf16[128,512]{1,0:T(8,128)(2,1)}, u32[]{:S(2)}, u32[]{:S(2)}) %collective-permute-start.12) | collective-permute-done | bytes 131104 | tf_op jit(solution)/shard_map/ppermute | solution.py:27
  70.0 0.0 collective-permute-start.13
  70.0 0.5 collective-permute-start.14
  70.5 0.0 collective-permute-start.15
  70.5 0.0 collective-permute-done.9.refs_1_
  70.5 1.2 %collective-permute-done.13.refs_3_ = bf16[128,512]{1,0:T(8,128)(2,1)} collective-permute-done((bf16[128,512]{1,0:T(8,128)(2,1)}, bf16[128,512]{1,0:T(8,128)(2,1)}, u32[]{:S(2)}, u32[]{:S(2)}) %collective-permute-start.13) | collective-permute-done | bytes 131104 | tf_op jit(solution)/shard_map/ppermute | solution.py:27
  71.7 0.2 collective-permute-done.14.refs_5_
  71.8 0.3 collective-permute-done.15.refs_7_
  72.2 4.4 %add_level.3 = bf16[1024,1024]{1,0:T(8,128)(2,1)} custom-call(bf16[1024,1024]{1,0:T(8,128)(2,1)} %add_level.2.refs_3_.sofar_ref, bf16[4,2,1024,128]{3,2,1,0:T(8,128)(2,1)} %all-to-all-done.panels_ref, bf16[128,512]{1,0:T(8,128)(2,1)} %get-tuple-element.31.refs_0_, bf16[128,512]{1,0:T(8,128)(2,1)} %collective-permute-done.9.refs_1_, ...), custom_call_target="tpu_custom_call" | custom-call | flops 1 | bytes 1 | tf_op jit(solution)/shard_map/add_level/pallas_call | solution.py:39
  (3 shorter events, 0.0 us)
Async XLA Ops:
  6.1 22.9 %collective-permute-start = (bf16[384,512]{1,0:T(8,128)(2,1)}, bf16[384,512]{1,0:T(8,128)(2,1)}, u32[]{:S(2)}, u32[]{:S(2)}) collective-permute-start(bf16[384,512]{1,0:T(8,128)(2,1)} %get-tuple-element.22), channel_id=1, source_target_pairs={{0,4},{1,5},{2,6},{3,7},{4,0},{5,1},{6,2},{7,3},{8,12},{9,13},{10,... | collective-permute-start | bytes 1179656 | tf_op jit(solution)/shard_map/ppermute | solution.py:27
  9.1 1.5 %collective-permute-start.2 = (bf16[16,128]{1,0:T(8,128)(2,1)}, bf16[16,128]{1,0:T(8,128)(2,1)}, u32[]{:S(2)}, u32[]{:S(2)}) collective-permute-start(bf16[16,128]{1,0:T(8,128)(2,1)} %get-tuple-element.25), channel_id=1, source_target_pairs={{0,1},{1,0},{2,3},{3,2},{4,5},{5,4},{6,7},{7,6},{8,9},{9,8},{10,11... | collective-permute-start | bytes 12296 | tf_op jit(solution)/shard_map/ppermute | solution.py:27
  10.6 33.0 %collective-permute-start.3 = (bf16[512,1024]{1,0:T(8,128)(2,1)}, bf16[512,1024]{1,0:T(8,128)(2,1)}, u32[]{:S(2)}, u32[]{:S(2)}) collective-permute-start(bf16[512,1024]{1,0:T(8,128)(2,1)} %held.3), channel_id=1, source_target_pairs={{0,4},{2,6},{4,8},{5,1},{6,10},{7,3},{8,12},{9,5},{10,14},{11,7},{... | collective-permute-start | bytes 3145736 | tf_op jit(solution)/shard_map/ppermute | solution.py:27
  23.7 39.4 %all-to-all-start = ((bf16[4,2,1024,128]{3,2,1,0:T(8,128)(2,1)}), bf16[4,2,1024,128]{3,2,1,0:T(8,128)(2,1)}, u32[]{:S(2)}, u32[]{:S(2)}) async-start(bf16[4,2,1024,128]{3,2,1,0:T(8,128)(2,1)} %get-tuple-element.28), calls=%async_computation | async-start | bytes 4194304 | tf_op jit(solution)/shard_map/all_to_all | solution.py:493
  31.1 12.5 %collective-permute-start.1 = (bf16[384,512]{1,0:T(8,128)(2,1)}, bf16[384,512]{1,0:T(8,128)(2,1)}, u32[]{:S(2)}, u32[]{:S(2)}) collective-permute-start(bf16[384,512]{1,0:T(8,128)(2,1)} %get-tuple-element.23.refs_1_.a_ref), channel_id=1, source_target_pairs={{0,8},{1,9},{2,10},{3,11},{4,12},{5,13},{6,14},{7,15},{8,0},{9,1},... | collective-permute-start | bytes 1179656 | tf_op jit(solution)/shard_map/ppermute | solution.py:27
  45.5 4.3 %collective-permute-start.4 = (bf16[512,1024]{1,0:T(8,128)(2,1)}, bf16[512,1024]{1,0:T(8,128)(2,1)}, u32[]{:S(2)}, u32[]{:S(2)}) collective-permute-start(bf16[512,1024]{1,0:T(8,128)(2,1)} %get-tuple-element.26.refs_0_), channel_id=1, source_target_pairs={{0,1},{1,0},{2,3},{3,2},{4,5},{5,4},{6,7},{7,6},{8,9},{9,8},{10,11... | collective-permute-start | bytes 3145736 | tf_op jit(solution)/shard_map/ppermute | solution.py:27
  45.6 13.9 %collective-permute-start.7 = (bf16[256,512]{1,0:T(8,128)(2,1)}, bf16[256,512]{1,0:T(8,128)(2,1)}, u32[]{:S(2)}, u32[]{:S(2)}) collective-permute-start(bf16[256,512]{1,0:T(8,128)(2,1)} %get-tuple-element.27.refs_2_.refs_0_), channel_id=1, source_target_pairs={{0,2},{1,3},{2,0},{3,1},{4,6},{5,7},{6,4},{7,5},{8,10},{9,11},{10,... | collective-permute-start | bytes 786440 | tf_op jit(solution)/shard_map/ppermute | solution.py:27
  47.1 9.5 %collective-permute-start.6 = (bf16[128,512]{1,0:T(8,128)(2,1)}, bf16[128,512]{1,0:T(8,128)(2,1)}, u32[]{:S(2)}, u32[]{:S(2)}) collective-permute-start(bf16[128,512]{1,0:T(8,128)(2,1)} %get-tuple-element.29), channel_id=1, source_target_pairs={{0,16},{1,17},{2,18},{3,19},{4,20},{5,21},{6,22},{7,23},{8,24},{9,... | collective-permute-start | bytes 393224 | tf_op jit(solution)/shard_map/ppermute | solution.py:27
  49.8 13.2 %collective-permute-start.5 = (bf16[256,512]{1,0:T(8,128)(2,1)}, bf16[256,512]{1,0:T(8,128)(2,1)}, u32[]{:S(2)}, u32[]{:S(2)}) collective-permute-start(bf16[256,512]{1,0:T(8,128)(2,1)} %get-tuple-element.27.refs_2_.refs_0_), channel_id=1, source_target_pairs={{0,1},{1,0},{2,3},{3,2},{4,5},{5,4},{6,7},{7,6},{8,9},{9,8},{10,11... | collective-permute-start | bytes 786440 | tf_op jit(solution)/shard_map/ppermute | solution.py:27
  59.5 3.5 %collective-permute-start.8 = (bf16[256,512]{1,0:T(8,128)(2,1)}, bf16[256,512]{1,0:T(8,128)(2,1)}, u32[]{:S(2)}, u32[]{:S(2)}) collective-permute-start(bf16[256,512]{1,0:T(8,128)(2,1)} %get-tuple-element.30.refs_2_), channel_id=1, source_target_pairs={{0,1},{1,0},{2,3},{3,2},{4,5},{5,4},{6,7},{7,6},{8,9},{9,8},{10,11... | collective-permute-start | bytes 786440 | tf_op jit(solution)/shard_map/ppermute | solution.py:27
  59.5 8.0 %collective-permute-start.10 = (bf16[128,512]{1,0:T(8,128)(2,1)}, bf16[128,512]{1,0:T(8,128)(2,1)}, u32[]{:S(2)}, u32[]{:S(2)}) collective-permute-start(bf16[128,512]{1,0:T(8,128)(2,1)} %get-tuple-element.31.refs_0_), channel_id=1, source_target_pairs={{0,2},{1,3},{2,0},{3,1},{4,6},{5,7},{6,4},{7,5},{8,10},{9,11},{10,... | collective-permute-start | bytes 393224 | tf_op jit(solution)/shard_map/ppermute | solution.py:27
  59.9 7.6 %collective-permute-start.11 = (bf16[128,512]{1,0:T(8,128)(2,1)}, bf16[128,512]{1,0:T(8,128)(2,1)}, u32[]{:S(2)}, u32[]{:S(2)}) collective-permute-start(bf16[128,512]{1,0:T(8,128)(2,1)} %get-tuple-element.31.refs_0_), channel_id=1, source_target_pairs={{0,4},{1,5},{2,6},{3,7},{4,0},{5,1},{6,2},{7,3},{8,12},{9,13},{10,... | collective-permute-start | bytes 393224 | tf_op jit(solution)/shard_map/ppermute | solution.py:27
  61.8 8.1 %collective-permute-start.12 = (bf16[128,512]{1,0:T(8,128)(2,1)}, bf16[128,512]{1,0:T(8,128)(2,1)}, u32[]{:S(2)}, u32[]{:S(2)}) collective-permute-start(bf16[128,512]{1,0:T(8,128)(2,1)} %get-tuple-element.31.refs_0_), channel_id=1, source_target_pairs={{0,6},{1,7},{2,4},{3,5},{4,2},{5,3},{6,0},{7,1},{8,14},{9,15},{10,... | collective-permute-start | bytes 393224 | tf_op jit(solution)/shard_map/ppermute | solution.py:27
  63.0 7.5 %collective-permute-start.9 = (bf16[128,512]{1,0:T(8,128)(2,1)}, bf16[128,512]{1,0:T(8,128)(2,1)}, u32[]{:S(2)}, u32[]{:S(2)}) collective-permute-start(bf16[128,512]{1,0:T(8,128)(2,1)} %get-tuple-element.31.refs_0_), channel_id=1, source_target_pairs={{0,1},{1,0},{2,3},{3,2},{4,5},{5,4},{6,7},{7,6},{8,9},{9,8},{10,11... | collective-permute-start | bytes 393224 | tf_op jit(solution)/shard_map/ppermute | solution.py:27
  70.0 1.7 %collective-permute-start.13 = (bf16[128,512]{1,0:T(8,128)(2,1)}, bf16[128,512]{1,0:T(8,128)(2,1)}, u32[]{:S(2)}, u32[]{:S(2)}) collective-permute-start(bf16[128,512]{1,0:T(8,128)(2,1)} %get-tuple-element.32.refs_2_), channel_id=1, source_target_pairs={{0,1},{1,0},{2,3},{3,2},{4,5},{5,4},{6,7},{7,6},{8,9},{9,8},{10,11... | collective-permute-start | bytes 393224 | tf_op jit(solution)/shard_map/ppermute | solution.py:27
  70.0 1.9 %collective-permute-start.14 = (bf16[128,512]{1,0:T(8,128)(2,1)}, bf16[128,512]{1,0:T(8,128)(2,1)}, u32[]{:S(2)}, u32[]{:S(2)}) collective-permute-start(bf16[128,512]{1,0:T(8,128)(2,1)} %get-tuple-element.33.refs_4_), channel_id=1, source_target_pairs={{0,1},{1,0},{2,3},{3,2},{4,5},{5,4},{6,7},{7,6},{8,9},{9,8},{10,11... | collective-permute-start | bytes 393224 | tf_op jit(solution)/shard_map/ppermute | solution.py:27
  70.5 1.7 %collective-permute-start.15 = (bf16[128,512]{1,0:T(8,128)(2,1)}, bf16[128,512]{1,0:T(8,128)(2,1)}, u32[]{:S(2)}, u32[]{:S(2)}) collective-permute-start(bf16[128,512]{1,0:T(8,128)(2,1)} %get-tuple-element.34.refs_6_), channel_id=1, source_target_pairs={{0,1},{1,0},{2,3},{3,2},{4,5},{5,4},{6,7},{7,6},{8,9},{9,8},{10,11... | collective-permute-start | bytes 393224 | tf_op jit(solution)/shard_map/ppermute | solution.py:27

commit v4 on v3

v4 whole, which is shorter than its diff:
```python
import jax
import jax.numpy as jnp
from jax import lax
from jax.experimental import pallas as pl
from jax.experimental.pallas import tpu as pltpu
from jax.sharding import PartitionSpec as P

B = 256
REACH = 2
AXES = ("rows", "cols")
VMEM = 64 * 1024 * 1024
COST_A = 1
COST_B = 1
COST_C = 7000000000
HBM = pl.BlockSpec(memory_space=pltpu.HBM)
SMEM = pl.BlockSpec(memory_space=pltpu.SMEM)


def moved(value, target):
    n_rows, n_cols = lax.axis_size("rows"), lax.axis_size("cols")
    pairs = []
    for row in range(n_rows):
        for col in range(n_cols):
            other = target(row, col)
            if other is not None and 0 <= other[0] < n_rows:
                pairs.append((row * n_cols + col, other[0] * n_cols + other[1]))
    return lax.ppermute(value, AXES, pairs)


def flipped(value, row_bits, col_bits):
    return moved(value, lambda row, col: (row ^ row_bits, col ^ col_bits))


def span(index, size):
    return pl.ds(pl.multiple_of(index * size, size), size)


def called(kernel, name, smem, hbm, after, out_shape, scratch, aliases={}, flops=1):
    return pl.pallas_call(
        kernel,
        out_shape=out_shape,
        in_specs=[SMEM] * len(smem) + [HBM] * (len(hbm) + len(after)),
        out_specs=jax.tree.map(lambda _: HBM, out_shape),
        scratch_shapes=scratch,
        input_output_aliases=aliases,
        compiler_params=pltpu.CompilerParams(vmem_limit_bytes=VMEM),
        cost_estimate=pl.CostEstimate(flops=flops, bytes_accessed=1, transcendentals=0),
        name=name,
    )(*smem, *hbm, *after)


def project(right_one, right_two, vectors):
    depth, rank = right_one.shape
    width = vectors.shape[1]
    half = width // 2
    step = REACH * B
    parts = depth // step

    def kernel(one_ref, two_ref, vectors_ref, send_ref, keep_ref, edge_ref, *scratch):
        rights, block, total, result, right_sems, block_sems, out_sems, edge_sem = scratch
        mine, last_first = lax.axis_index("rows") % 2, lax.axis_index("cols") % 2 == 0
        copies, places = [], []
        for i in range(parts):
            place = span(jnp.where(last_first, parts - 1 - i, i), step)
            places.append(place)
            copies.append(
                [
                    pltpu.make_async_copy(
                        ref.at[place], rights.at[place, pl.ds(level * rank, rank)], right_sems.at[level, i]
                    )
                    for level, ref in enumerate((one_ref, two_ref))
                ]
                + [pltpu.make_async_copy(vectors_ref.at[place], block.at[place], block_sems.at[i])]
            )
            for copy in copies[-1]:
                copy.start()
        edge_copy = pltpu.make_async_copy(block.at[places[0]], edge_ref, edge_sem)
        for i in range(parts):
            for copy in copies[i]:
                copy.wait()
            if i == 0:
                edge_copy.start()
            part = lax.dot_general(
                rights[places[i]], block[places[i]], (((0,), (0,)), ((), ())), preferred_element_type=jnp.float32
            )
            if i == 0:
                total[...] = part
            elif i < parts - 1:
                total[...] += part
            else:
                result[...] = (total[...] + part).astype(jnp.bfloat16)
        outs = []
        for k, (ref, chosen) in enumerate(((send_ref, mine ^ 1), (keep_ref, mine))):
            outs.append(
                pltpu.make_async_copy(
                    result.at[pl.ds(0, rank), span(chosen, half)], ref.at[pl.ds(0, rank)], out_sems.at[k, 0]
                )
            )
            for n in range(2):
                outs.append(
                    pltpu.make_async_copy(
                        result.at[pl.ds(rank, rank), pl.ds(n * half, half)],
                        ref.at[pl.ds((1 + n) * rank, rank)],
                        out_sems.at[k, 1 + n],
                    )
                )
        for copy in outs:
            copy.start()
        for copy in outs:
            copy.wait()
        edge_copy.wait()

    return called(
        kernel,
        "project",
        [],
        [right_one, right_two, vectors],
        (),
        [
            jax.ShapeDtypeStruct((3 * rank, half), jnp.bfloat16),
            jax.ShapeDtypeStruct((3 * rank, half), jnp.bfloat16),
            jax.ShapeDtypeStruct((step, width), jnp.bfloat16),
        ],
        [
            pltpu.VMEM((depth, 2 * rank), jnp.bfloat16),
            pltpu.VMEM((depth, width), jnp.bfloat16),
            pltpu.VMEM((2 * rank, width), jnp.float32),
            pltpu.VMEM((2 * rank, width), jnp.bfloat16),
            pltpu.SemaphoreType.DMA((2, parts)),
            pltpu.SemaphoreType.DMA((parts,)),
            pltpu.SemaphoreType.DMA((2, 3)),
            pltpu.SemaphoreType.DMA,
        ],
    )


def near_field(near_cols, near_tiles, vectors, first, count, sofar=None, halos=(), after=(), flops=1):
    tiles, nnz = near_cols.shape
    rows, width = tiles * B, vectors.shape[1]
    window = vectors.shape[0] // B + 2 * REACH
    half = width // 2
    given = 0 if sofar is None else 1
    inside = count
    if halos:
        count += 2 * REACH
    sizes = []
    while sum(sizes) < inside:
        sizes.append(min((1, 3, 4)[min(len(sizes), 2)], inside - sum(sizes)))
    if inside and sizes[-1] == 1:
        sizes = sizes[:-2] + [sizes[-2] + 1] if len(sizes) > 1 else sizes
    if halos:
        sizes += [REACH, REACH]
    groups = len(sizes)
    begins = [sum(sizes[:g]) for g in range(groups)]

    def kernel(cols_ref, tiles_ref, vectors_ref, *refs):
        sofar_refs, refs = refs[:given], refs[given:]
        halo_refs, refs = refs[: len(halos)], refs[len(halos) + len(after) :]
        out_ref, slots, wide, tall, total, result, tile_sems, tall_sems, sofar_sem, out_sems = refs
        col = lax.axis_index("cols")

        for t in range(tiles):
            for c in range(window):
                slots[t, c] = -1
            for k in range(nnz):
                slots[t, cols_ref[t, k]] = k

        def tile_copy(t, c):
            if c < inside:
                place = first + c + REACH
            else:
                i = c - inside
                before = (i < REACH) == (col % 2 == 1)
                place = jnp.where(before, i % REACH, window - REACH + i % REACH)
            slot = slots[t, place]
            copy = pltpu.make_async_copy(
                tiles_ref.at[t, jnp.maximum(slot, 0)],
                wide.at[pl.ds(t * B, B), pl.ds(c * B, B)],
                tile_sems.at[t, c],
            )
            return slot >= 0, copy

        def tall_copy(g):
            place = pl.ds(begins[g] * B, sizes[g] * B)
            if begins[g] < inside:
                source = vectors_ref.at[pl.ds((first + begins[g]) * B, sizes[g] * B)]
            else:
                source = halo_refs[g - groups]
            return pltpu.make_async_copy(source, tall.at[place], tall_sems.at[g])

        if given:
            sofar_copy = pltpu.make_async_copy(sofar_refs[0], result, sofar_sem)
        for g in range(groups):
            tall_copy(g).start()
            for c in range(begins[g], begins[g] + sizes[g]):
                for t in range(tiles):
                    there, copy = tile_copy(t, c)
                    pl.when(there)(copy.start)

                    @pl.when(jnp.logical_not(there))
                    def _():
                        wide[t * B : (t + 1) * B, c * B : (c + 1) * B] = jnp.zeros((B, B), jnp.bfloat16)

        if given:
            sofar_copy.start()
        outs = []
        for g in range(groups):
            tall_copy(g).wait()
            for c in range(begins[g], begins[g] + sizes[g]):
                for t in range(tiles):
                    there, copy = tile_copy(t, c)
                    pl.when(there)(copy.wait)
            chosen = pl.ds(begins[g] * B, sizes[g] * B)
            if g == groups - 1:
                if given:
                    sofar_copy.wait()
            for n in range(2):
                columns = pl.ds(n * half, half)
                part = jnp.dot(wide[:, chosen], tall[chosen, columns], preferred_element_type=jnp.float32)
                if g > 0:
                    part = total[:, columns] + part
                if g < groups - 1:
                    total[:, columns] = part
                else:
                    if given:
                        part = part + result[:, columns].astype(jnp.float32)
                    result[:, columns] = part.astype(jnp.bfloat16)
                    outs.append(
                        pltpu.make_async_copy(result.at[:, columns], out_ref.at[:, columns], out_sems.at[n])
                    )
                    outs[-1].start()
        for copy in outs:
            copy.wait()

    scratch = [
        pltpu.SMEM((tiles, window), jnp.int32),
        pltpu.VMEM((rows, count * B), jnp.bfloat16),
        pltpu.VMEM((count * B, width), jnp.bfloat16),
        pltpu.VMEM((rows, width), jnp.float32),
        pltpu.VMEM((rows, width), jnp.bfloat16),
        pltpu.SemaphoreType.DMA((tiles, count)),
        pltpu.SemaphoreType.DMA((groups,)),
        pltpu.SemaphoreType.DMA,
        pltpu.SemaphoreType.DMA((2,)),
    ]
    return called(
        kernel,
        "near_field",
        [near_cols],
        [near_tiles, vectors] + ([sofar] if given else []) + [*halos],
        after,
        jax.ShapeDtypeStruct((rows, width), jnp.bfloat16),
        scratch,
        flops=flops,
    )


def packed(lefts, shares, after):
    depth, rank = lefts[0].shape
    rows = depth // shares

    def kernel(one_ref, two_ref, *refs):
        refs = refs[len(after) :]
        out_refs, (block, in_sems, out_sems) = refs[: shares - 1], refs[shares - 1 :]
        col = lax.axis_index("cols")
        ins = [
            [
                pltpu.make_async_copy(
                    ref.at[span(col ^ (d + 1), rows)], block.at[d, level], in_sems.at[d, level]
                )
                for level, ref in enumerate((one_ref, two_ref))
            ]
            for d in range(shares - 1)
        ]
        for copies in ins:
            for copy in copies:
                copy.start()
        outs = []
        for d in range(shares - 1):
            for copy in ins[d]:
                copy.wait()
            outs.append(pltpu.make_async_copy(block.at[d], out_refs[d], out_sems.at[d]))
            outs[-1].start()
        for copy in outs:
            copy.wait()

    return called(
        kernel,
        "packed",
        [],
        [*lefts],
        after,
        [jax.ShapeDtypeStruct((2, rows, rank), jnp.bfloat16)] * (shares - 1),
        [
            pltpu.VMEM((shares - 1, 2, rows, rank), jnp.bfloat16),
            pltpu.SemaphoreType.DMA((shares - 1, 2)),
            pltpu.SemaphoreType.DMA((shares - 1,)),
        ],
    )


def add_levels(sofar, lefts, pieces, coeffs_one, coeffs_two):
    rows, width = sofar.shape
    half = width // 2
    rank = lefts[0].shape[1]
    offsets = len(pieces) + 1
    inner = 2 * offsets * rank

    def kernel(sofar_ref, *refs):
        left_refs, piece_refs, refs = refs[:2], refs[2 : 1 + offsets], refs[1 + offsets :]
        one_refs, refs = refs[: 2 * offsets], refs[2 * offsets :]
        two_refs, refs = refs[:offsets], refs[offsets:]
        out_ref, wide, ranks, result, left_sems, rank_sems, sofar_sems, out_sems = refs
        mine, col = lax.axis_index("rows") % 2, lax.axis_index("cols")
        places = [span(mine ^ n, half) for n in range(2)]
        copies = [[], []]
        for d in range(offsets):
            for level in range(2):
                place = pl.ds((level * offsets + d) * rank, rank)
                source = piece_refs[d - 1].at[level] if d else left_refs[level].at[span(col, rows)]
                copies[0].append(pltpu.make_async_copy(source, wide.at[:, place], left_sems.at[level, d]))
                for n in range(2):
                    source = two_refs[d].at[span(mine ^ n, rank)] if level else one_refs[n * offsets + d]
                    copies[n].append(
                        pltpu.make_async_copy(source, ranks.at[n, place], rank_sems.at[n, level, d])
                    )
        for n in range(2):
            copies[n].append(
                pltpu.make_async_copy(sofar_ref.at[:, places[n]], result.at[n], sofar_sems.at[n])
            )
            for copy in copies[n]:
                copy.start()
        outs = []
        for n in range(2):
            for copy in copies[n]:
                copy.wait()
            part = jnp.dot(wide[...], ranks[n], preferred_element_type=jnp.float32)
            result[n] = (result[n].astype(jnp.float32) + part).astype(jnp.bfloat16)
            outs.append(pltpu.make_async_copy(result.at[n], out_ref.at[:, places[n]], out_sems.at[n]))
            outs[-1].start()
        for copy in outs:
            copy.wait()

    return called(
        kernel,
        "add_levels",
        [],
        [sofar, *lefts, *pieces, *coeffs_one, *coeffs_two],
        (),
        jax.ShapeDtypeStruct((rows, width), jnp.bfloat16),
        [
            pltpu.VMEM((rows, inner), jnp.bfloat16),
            pltpu.VMEM((2, inner, half), jnp.bfloat16),
            pltpu.VMEM((2, rows, half), jnp.bfloat16),
            pltpu.SemaphoreType.DMA((2, offsets)),
            pltpu.SemaphoreType.DMA((2, 2, offsets)),
            pltpu.SemaphoreType.DMA((2,)),
            pltpu.SemaphoreType.DMA((2,)),
        ],
    )


def parted(a, b, top):
    rows, width = b.shape

    def kernel(a_ref, b_ref, sum_ref, rest_ref, mine, theirs, total, sems):
        ins = [
            pltpu.make_async_copy(a_ref.at[pl.ds(0, top)], mine, sems.at[0]),
            pltpu.make_async_copy(b_ref.at[pl.ds(0, top)], theirs.at[pl.ds(0, top)], sems.at[1]),
            pltpu.make_async_copy(
                b_ref.at[pl.ds(top, rows - top)], theirs.at[pl.ds(top, rows - top)], sems.at[2]
            ),
        ]
        for copy in ins:
            copy.start()
        ins[0].wait()
        ins[1].wait()
        total[...] = (mine[...].astype(jnp.float32) + theirs[:top].astype(jnp.float32)).astype(jnp.bfloat16)
        outs = [
            pltpu.make_async_copy(total, sum_ref, sems.at[3]),
            pltpu.make_async_copy(theirs.at[pl.ds(top, rows - top)], rest_ref, sems.at[4]),
        ]
        outs[0].start()
        ins[2].wait()
        outs[1].start()
        for copy in outs:
            copy.wait()

    return called(
        kernel,
        "parted",
        [],
        [a, b],
        (),
        [
            jax.ShapeDtypeStruct((top, width), jnp.bfloat16),
            jax.ShapeDtypeStruct((rows - top, width), jnp.bfloat16),
        ],
        [
            pltpu.VMEM((top, width), jnp.bfloat16),
            pltpu.VMEM((rows, width), jnp.bfloat16),
            pltpu.VMEM((top, width), jnp.bfloat16),
            pltpu.SemaphoreType.DMA((5,)),
        ],
    )


def held(passed, after):
    def kernel(*refs):
        pass

    return called(
        kernel,
        "held",
        [],
        passed,
        after,
        [jax.ShapeDtypeStruct(x.shape, x.dtype) for x in passed],
        [],
        {i: i for i in range(len(passed))},
    )


def per_device(vectors, near_tiles, near_cols, left_one, right_one, left_two, right_two):
    n_rows, n_cols = lax.axis_size("rows"), lax.axis_size("cols")
    bits = n_rows.bit_length() - 1
    col = lax.axis_index("cols")
    depth = vectors.shape[0]
    rank = right_one.shape[1]
    inside = depth // B

    near_args = (near_cols, near_tiles, vectors)
    cuts = [0, inside // 8, 9 * inside // 16, inside]

    def near_part(part, sofar, after, flops):
        first, last = cuts[part : part + 2]
        return near_field(*near_args, first, last - first, sofar, after=after, flops=flops)

    def summed(a, b):
        return (a.astype(jnp.float32) + b.astype(jnp.float32)).astype(jnp.bfloat16)

    send, keep, edge = project(right_one, right_two, vectors)
    arrived = flipped(send, 1, 0)

    pieces = packed((left_one, left_two), n_cols, (keep,))
    pieces = [flipped(piece, 0, offset) for offset, piece in enumerate(pieces, 1)]

    near = near_part(0, None, (keep,), COST_A)
    (keep,) = held([keep], [near])
    both = summed(keep, arrived)
    for bit in range(1, bits - 2):
        both = summed(both, flipped(both, 2**bit, 0))
    arrived = flipped(both, 2 ** (bits - 2), 0)

    (edge,) = held([edge], [both])
    halo = moved(edge, lambda r, c: (r + 1 if c % 2 == 0 else r - 1, c ^ 1))
    near = near_part(1, near, (both,), COST_B)
    both, *pieces[:-1] = held([both, *pieces[:-1]], [near])
    one, two = parted(both, arrived, rank)
    one = flipped(one, 2 ** (bits - 1), 0)
    near = near_part(2, near, (two,), COST_C)

    offsets = range(0, n_cols, 2)
    twos = [two] + [flipped(two, 0, offset) for offset in offsets[1:]]
    one, halo, pieces[-1], *rest = held([one, halo, pieces[-1], *twos[1:]], [near])
    twos = [two] + rest
    ones = [
        one if (other, offset) == (0, 0) else flipped(one, other, offset)
        for other in range(2)
        for offset in offsets
    ]
    near = near_field(*near_args, 0, 0, near, (halo, flipped(halo, 0, 1)))
    ones = [one, *held(ones[1:], [near])]
    coeffs_two = [x for there in twos for x in (there, flipped(there, 0, 1))]
    coeffs_one = [x for there in ones for x in (there, flipped(there, 0, 1))]
    return add_levels(near, (left_one, left_two), pieces, coeffs_one, coeffs_two)


def solution(mesh):
    placed = (
        P("rows", None),
        P(("rows", "cols"), None, None, None),
        P(("rows", "cols"), None),
        P("rows", "cols"),
        P("rows", "cols"),
        P("rows", "cols"),
        P("rows", "cols"),
    )
    return jax.shard_map(
        per_device, mesh=mesh, in_specs=placed, out_specs=P(("rows", "cols"), None), check_vma=False
    )
```

time: 77.2 us -> 68.3 us (0.88)
  waiting for transfers between devices: 10.3 us -> 4.76 us
  starting transfers between devices: 22.5 us -> 18.2 us
    ppermute x16 -> x18, waiting for transfers between devices: 10.3 us -> 4.76 us  [moved(): return lax.ppermute(value, AXES, pairs)]
    all_to_all x1 -> x0, starting transfers between devices: 4.47 us -> none  [per_device(): lax.all_to_all(panels, 'cols', split_axis=0, concat_axis=0, tiled=True)]
    convert_element_type x0 -> x1, other arithmetic: none -> 1.95 us  [summed(): return (a.astype(jnp.float32) + b.astype(jnp.float32)).astype(jnp.bfloat16)]
    reduce_max x1 -> x0, other arithmetic: 1.35 us -> none  [per_device(): jnp.max(jnp.where(names, jnp.arange(nnz, dtype=jnp.int32)[None, :, None],...]
    ppermute x16 -> x18, starting transfers between devices: 18 us -> 18.2 us  [moved(): return lax.ppermute(value, AXES, pairs)]
    pallas_call x11 -> x13, Pallas kernels: 42.3 us -> 42.3 us  [called(): pl.pallas_call(kernel, out_shape=out_shape, in_specs=[SMEM] * len(smem) +...]
  transfers between devices with their start and end apart: 17 -> 18, of which waited for: 8 -> 9; matrix products, arithmetic and copies ran while one was open for 2% -> 3% of each run, Pallas kernels for 41% -> 44%
where the time goes in v4:
time: 68.3 us; the launch traced here: 67.5 us
  Pallas kernels  42.3 us (62%)
  starting transfers between devices  18.2 us (27%)
  waiting for transfers between devices  4.76 us (7%)
  other arithmetic  1.95 us (3%)
    pallas_call x13, Pallas kernels, called(): pl.pallas_call(kernel, out_shape=out_shape, in_specs=[SMEM] * len(smem) +...  42.3 us
    ppermute x18, starting transfers between devices, moved(): return lax.ppermute(value, AXES, pairs)  18.2 us
    ppermute x18, waiting for transfers between devices, moved(): return lax.ppermute(value, AXES, pairs)  4.76 us
    convert_element_type x1, other arithmetic, summed(): return (a.astype(jnp.float32) + b.astype(jnp.float32)).astype(jnp.bfloat16)  1.95 us
  transfers between devices with their start and end apart: 18, of which 9 were waited for; matrix products, arithmetic and copies ran while one was open for 3% of the time, Pallas kernels for 44%

profile of v4, /device:TPU:0, one launch (start us, length us, event | category | flops | bytes accessed | tf_op | source)
XLA Modules:
  0.0 67.5 jit_solution(4457820682137587110)
XLA Ops:
  0.0 6.1 %project.1 = (bf16[384,512]{1,0:T(8,128)(2,1)}, bf16[384,512]{1,0:T(8,128)(2,1)}, bf16[512,1024]{1,0:T(8,128)(2,1)}) custom-call(bf16[4096,128]{1,0:T(8,128)(2,1)} %one_ref.2, bf16[4096,128]{1,0:T(8,128)(2,1)} %two_ref.2, bf16[4096,1024]{1,0:T(8,128)(2,1)} %vectors_ref.9), custom_call_target="tpu_custom_call" | custom-call | flops 1 | bytes 1 | tf_op jit(solution)/shard_map/project/pallas_call | solution.py:39
  6.1 3.0 %collective-permute-start = (bf16[384,512]{1,0:T(8,128)(2,1)}, bf16[384,512]{1,0:T(8,128)(2,1)}, u32[]{:S(2)}, u32[]{:S(2)}) collective-permute-start(bf16[384,512]{1,0:T(8,128)(2,1)} %get-tuple-element.24), channel_id=1, source_target_pairs={{0,4},{1,5},{2,6},{3,7},{4,0},{5,1},{6,2},{7,3},{8,12},{9,13},{10,... | collective-permute-start | bytes 1179656 | tf_op jit(solution)/shard_map/ppermute | solution.py:27
  9.1 2.3 %packed.1 = (bf16[2,1024,128]{2,1,0:T(8,128)(2,1)}, bf16[2,1024,128]{2,1,0:T(8,128)(2,1)}, bf16[2,1024,128]{2,1,0:T(8,128)(2,1)}) custom-call(bf16[4096,128]{1,0:T(8,128)(2,1)} %refs_0_.1, bf16[4096,128]{1,0:T(8,128)(2,1)} %refs_1_.1, bf16[384,512]{1,0:T(8,128)(2,1)} %get-tuple-element.23.refs_0_), custom_call_target="tpu_custom_call" | custom-call | flops 1 | bytes 1 | tf_op jit(solution)/shard_map/packed/pallas_call | solution.py:39
  11.4 0.1 collective-permute-start.1
  11.5 4.4 %near_field.4.refs_1_.refs_0_ = bf16[1024,1024]{1,0:T(8,128)(2,1)} custom-call(s32[4,16]{1,0:T(4,128)} %cols_ref.7, bf16[4,16,256,256]{3,2,1,0:T(8,128)(2,1)} %tiles_ref.7, bf16[4096,1024]{1,0:T(8,128)(2,1)} %vectors_ref.9, bf16[384,512]{1,0:T(8,128)(2,1)} %get-tuple-element.23.refs_0_), custom_call_target="tpu_custom_call" | custom-call | flops 1 | bytes 1 | tf_op jit(solution)/shard_map/near_field/pallas_call | solution.py:39
  15.9 1.6 %collective-permute-start.2 = (bf16[2,1024,128]{2,1,0:T(8,128)(2,1)}, bf16[2,1024,128]{2,1,0:T(8,128)(2,1)}, u32[]{:S(2)}, u32[]{:S(2)}) collective-permute-start(bf16[2,1024,128]{2,1,0:T(8,128)(2,1)} %get-tuple-element.26), channel_id=1, source_target_pairs={{0,2},{1,3},{2,0},{3,1},{4,6},{5,7},{6,4},{7,5},{8,10},{9,11},{10,... | collective-permute-start | bytes 1572872 | tf_op jit(solution)/shard_map/ppermute | solution.py:27
  17.5 1.0 %collective-permute-done = bf16[384,512]{1,0:T(8,128)(2,1)} collective-permute-done((bf16[384,512]{1,0:T(8,128)(2,1)}, bf16[384,512]{1,0:T(8,128)(2,1)}, u32[]{:S(2)}, u32[]{:S(2)}) %collective-permute-start) | collective-permute-done | bytes 393248 | tf_op jit(solution)/shard_map/ppermute | solution.py:27
  18.5 2.0 %add_convert_fusion.refs_1_.refs_0_ = bf16[384,512]{1,0:T(8,128)(2,1)} fusion(bf16[384,512]{1,0:T(8,128)(2,1)} %collective-permute-done, bf16[384,512]{1,0:T(8,128)(2,1)} %held.5), kind=kLoop, calls=%fused_computation | loop fusion | flops 786432 | bytes 1179648 | tf_op jit(solution)/shard_map/convert_element_type | solution.py:440
  20.5 1.8 %collective-permute-start.3 = (bf16[384,512]{1,0:T(8,128)(2,1)}, bf16[384,512]{1,0:T(8,128)(2,1)}, u32[]{:S(2)}, u32[]{:S(2)}) collective-permute-start(bf16[384,512]{1,0:T(8,128)(2,1)} %add_convert_fusion.refs_1_.refs_0_), channel_id=1, source_target_pairs={{0,8},{1,9},{2,10},{3,11},{4,12},{5,13},{6,14},{7,15},{8,0},{9,1},... | collective-permute-start | bytes 1179656 | tf_op jit(solution)/shard_map/ppermute | solution.py:27
  22.3 1.9 %collective-permute-start.5 = (bf16[512,1024]{1,0:T(8,128)(2,1)}, bf16[512,1024]{1,0:T(8,128)(2,1)}, u32[]{:S(2)}, u32[]{:S(2)}) collective-permute-start(bf16[512,1024]{1,0:T(8,128)(2,1)} %held.7), channel_id=1, source_target_pairs={{0,5},{2,7},{4,9},{5,0},{6,11},{7,2},{8,13},{9,4},{10,15},{11,6},{... | collective-permute-start | bytes 3145736 | tf_op jit(solution)/shard_map/ppermute | solution.py:27
  24.2 0.1 collective-permute-start.6
  24.3 7.9 %near_field.5.refs_3_.refs_0_ = bf16[1024,1024]{1,0:T(8,128)(2,1)} custom-call(s32[4,16]{1,0:T(4,128)} %cols_ref.7, bf16[4,16,256,256]{3,2,1,0:T(8,128)(2,1)} %tiles_ref.7, bf16[4096,1024]{1,0:T(8,128)(2,1)} %vectors_ref.9, bf16[1024,1024]{1,0:T(8,128)(2,1)} %near_field.4.refs_1_.refs_0_, bf16[384,512]{1,0:T(8,128)(2,1)} %add_convert_fusion.refs_1_.refs_0_), custom_call_target="tpu_custom_call" | custom-call | flops 1 | bytes 1 | tf_op jit(solution)/shard_map/near_field/pallas_call | solution.py:39
  32.2 0.0 collective-permute-done.1.refs_1_
  32.2 0.0 collective-permute-done.2.refs_2_
  32.2 0.6 collective-permute-done.3.b_ref
  32.9 1.8 %parted.1 = (bf16[128,512]{1,0:T(8,128)(2,1)}, bf16[256,512]{1,0:T(8,128)(2,1)}) custom-call(bf16[384,512]{1,0:T(8,128)(2,1)} %get-tuple-element.27.a_ref, bf16[384,512]{1,0:T(8,128)(2,1)} %collective-permute-done.3.b_ref), custom_call_target="tpu_custom_call" | custom-call | flops 1 | bytes 1 | tf_op jit(solution)/shard_map/parted/pallas_call | solution.py:39
  34.7 1.8 %collective-permute-start.7 = (bf16[256,512]{1,0:T(8,128)(2,1)}, bf16[256,512]{1,0:T(8,128)(2,1)}, u32[]{:S(2)}, u32[]{:S(2)}) collective-permute-start(bf16[256,512]{1,0:T(8,128)(2,1)} %get-tuple-element.28.refs_1_.refs_13_), channel_id=1, source_target_pairs={{0,2},{1,3},{2,0},{3,1},{4,6},{5,7},{6,4},{7,5},{8,10},{9,11},{10,... | collective-permute-start | bytes 786440 | tf_op jit(solution)/shard_map/ppermute | solution.py:27
  36.5 2.6 %collective-permute-start.4 = (bf16[128,512]{1,0:T(8,128)(2,1)}, bf16[128,512]{1,0:T(8,128)(2,1)}, u32[]{:S(2)}, u32[]{:S(2)}) collective-permute-start(bf16[128,512]{1,0:T(8,128)(2,1)} %get-tuple-element.29), channel_id=1, source_target_pairs={{0,16},{1,17},{2,18},{3,19},{4,20},{5,21},{6,22},{7,23},{8,24},{9,... | collective-permute-start | bytes 393224 | tf_op jit(solution)/shard_map/ppermute | solution.py:27
  39.1 7.5 %near_field.6.refs_4_.refs_0_ = bf16[1024,1024]{1,0:T(8,128)(2,1)} custom-call(s32[4,16]{1,0:T(4,128)} %cols_ref.7, bf16[4,16,256,256]{3,2,1,0:T(8,128)(2,1)} %tiles_ref.7, bf16[4096,1024]{1,0:T(8,128)(2,1)} %vectors_ref.9, bf16[1024,1024]{1,0:T(8,128)(2,1)} %near_field.5.refs_3_.refs_0_, bf16[256,512]{1,0:T(8,128)(2,1)} %get-tuple-element.28.refs_1_.refs_13_), custom_call_target="tpu_custom_call" | custom-call | flops 7000000000 | bytes 1 | tf_op jit(solution)/shard_map/near_field/pallas_call | solution.py:39
  46.7 0.0 collective-permute-done.6.refs_2_
  46.7 0.0 collective-permute-done.4.refs_0_
  46.7 0.9 %collective-permute-done.7.refs_3_ = bf16[256,512]{1,0:T(8,128)(2,1)} collective-permute-done((bf16[256,512]{1,0:T(8,128)(2,1)}, bf16[256,512]{1,0:T(8,128)(2,1)}, u32[]{:S(2)}, u32[]{:S(2)}) %collective-permute-start.7) | collective-permute-done | bytes 262176 | tf_op jit(solution)/shard_map/ppermute | solution.py:27
  47.6 0.5 collective-permute-done.5.refs_1_
  48.1 0.0 collective-permute-start.8
  48.1 0.5 collective-permute-start.16
  48.6 1.5 %collective-permute-start.10 = (bf16[128,512]{1,0:T(8,128)(2,1)}, bf16[128,512]{1,0:T(8,128)(2,1)}, u32[]{:S(2)}, u32[]{:S(2)}) collective-permute-start(bf16[128,512]{1,0:T(8,128)(2,1)} %get-tuple-element.36.refs_5_), channel_id=1, source_target_pairs={{0,2},{1,3},{2,0},{3,1},{4,6},{5,7},{6,4},{7,5},{8,10},{9,11},{10,... | collective-permute-start | bytes 393224 | tf_op jit(solution)/shard_map/ppermute | solution.py:27
  50.1 1.8 %collective-permute-start.11 = (bf16[128,512]{1,0:T(8,128)(2,1)}, bf16[128,512]{1,0:T(8,128)(2,1)}, u32[]{:S(2)}, u32[]{:S(2)}) collective-permute-start(bf16[128,512]{1,0:T(8,128)(2,1)} %get-tuple-element.36.refs_5_), channel_id=1, source_target_pairs={{0,4},{1,5},{2,6},{3,7},{4,0},{5,1},{6,2},{7,3},{8,12},{9,13},{10,... | collective-permute-start | bytes 393224 | tf_op jit(solution)/shard_map/ppermute | solution.py:27
  51.9 0.2 collective-permute-start.12
  52.1 0.0 collective-permute-done.8.refs_2_
  52.1 0.0 collective-permute-start.17
  52.1 6.0 %near_field.7.refs_3_.sofar_ref = bf16[1024,1024]{1,0:T(8,128)(2,1)} custom-call(s32[4,16]{1,0:T(4,128)} %cols_ref.7, bf16[4,16,256,256]{3,2,1,0:T(8,128)(2,1)} %tiles_ref.7, bf16[4096,1024]{1,0:T(8,128)(2,1)} %vectors_ref.9, bf16[1024,1024]{1,0:T(8,128)(2,1)} %near_field.6.refs_4_.refs_0_, bf16[512,1024]{1,0:T(8,128)(2,1)} %get-tuple-element.32.refs_1_, ...), custom_call_target="tpu_custom_call" | custom-call | flops 1 | bytes 1 | tf_op jit(solution)/shard_map/near_field/pallas_call | solution.py:39
  58.1 0.0 collective-permute-done.10.refs_0_
  58.1 0.7 %collective-permute-start.9 = (bf16[128,512]{1,0:T(8,128)(2,1)}, bf16[128,512]{1,0:T(8,128)(2,1)}, u32[]{:S(2)}, u32[]{:S(2)}) collective-permute-start(bf16[128,512]{1,0:T(8,128)(2,1)} %get-tuple-element.36.refs_5_), channel_id=1, source_target_pairs={{0,1},{1,0},{2,3},{3,2},{4,5},{5,4},{6,7},{7,6},{8,9},{9,8},{10,11... | collective-permute-start | bytes 393224 | tf_op jit(solution)/shard_map/ppermute | solution.py:27
  58.8 0.0 collective-permute-done.11.refs_1_
  58.9 0.1 collective-permute-done.12.refs_2_
  58.9 0.1 collective-permute-start.13
  59.0 0.5 collective-permute-start.14
  59.4 0.0 collective-permute-done.16.refs_14_
  59.4 0.1 collective-permute-start.15
  59.5 0.7 %collective-permute-done.9.refs_6_ = bf16[128,512]{1,0:T(8,128)(2,1)} collective-permute-done((bf16[128,512]{1,0:T(8,128)(2,1)}, bf16[128,512]{1,0:T(8,128)(2,1)}, u32[]{:S(2)}, u32[]{:S(2)}) %collective-permute-start.9) | collective-permute-done | bytes 131104 | tf_op jit(solution)/shard_map/ppermute | solution.py:27
  60.2 0.0 collective-permute-done.17.refs_16_
  60.2 0.4 collective-permute-done.13.refs_8_
  60.6 0.2 collective-permute-done.14.refs_10_
  60.8 0.3 collective-permute-done.15.refs_12_
  61.1 6.2 %add_levels.1 = bf16[1024,1024]{1,0:T(8,128)(2,1)} custom-call(bf16[1024,1024]{1,0:T(8,128)(2,1)} %near_field.7.refs_3_.sofar_ref, bf16[4096,128]{1,0:T(8,128)(2,1)} %refs_0_.1, bf16[4096,128]{1,0:T(8,128)(2,1)} %refs_1_.1, bf16[2,1024,128]{2,1,0:T(8,128)(2,1)} %get-tuple-element.33.refs_2_, bf16[2,1024,128]{2,1,0:T(8,128)(2,1)} %get-tuple-element.34.refs_3_, ...), custom_call_target="tpu_custom_call" | custom-call | flops 1 | bytes 1 | tf_op jit(solution)/shard_map/add_levels/pallas_call | solution.py:39
  (5 shorter events, 0.0 us)
Async XLA Ops:
  6.1 12.4 %collective-permute-start = (bf16[384,512]{1,0:T(8,128)(2,1)}, bf16[384,512]{1,0:T(8,128)(2,1)}, u32[]{:S(2)}, u32[]{:S(2)}) collective-permute-start(bf16[384,512]{1,0:T(8,128)(2,1)} %get-tuple-element.24), channel_id=1, source_target_pairs={{0,4},{1,5},{2,6},{3,7},{4,0},{5,1},{6,2},{7,3},{8,12},{9,13},{10,... | collective-permute-start | bytes 1179656 | tf_op jit(solution)/shard_map/ppermute | solution.py:27
  11.4 20.8 %collective-permute-start.1 = (bf16[2,1024,128]{2,1,0:T(8,128)(2,1)}, bf16[2,1024,128]{2,1,0:T(8,128)(2,1)}, u32[]{:S(2)}, u32[]{:S(2)}) collective-permute-start(bf16[2,1024,128]{2,1,0:T(8,128)(2,1)} %get-tuple-element.25), channel_id=1, source_target_pairs={{0,1},{1,0},{2,3},{3,2},{4,5},{5,4},{6,7},{7,6},{8,9},{9,8},{10,11... | collective-permute-start | bytes 1572872 | tf_op jit(solution)/shard_map/ppermute | solution.py:27
  15.9 16.3 %collective-permute-start.2 = (bf16[2,1024,128]{2,1,0:T(8,128)(2,1)}, bf16[2,1024,128]{2,1,0:T(8,128)(2,1)}, u32[]{:S(2)}, u32[]{:S(2)}) collective-permute-start(bf16[2,1024,128]{2,1,0:T(8,128)(2,1)} %get-tuple-element.26), channel_id=1, source_target_pairs={{0,2},{1,3},{2,0},{3,1},{4,6},{5,7},{6,4},{7,5},{8,10},{9,11},{10,... | collective-permute-start | bytes 1572872 | tf_op jit(solution)/shard_map/ppermute | solution.py:27
  20.5 12.4 %collective-permute-start.3 = (bf16[384,512]{1,0:T(8,128)(2,1)}, bf16[384,512]{1,0:T(8,128)(2,1)}, u32[]{:S(2)}, u32[]{:S(2)}) collective-permute-start(bf16[384,512]{1,0:T(8,128)(2,1)} %add_convert_fusion.refs_1_.refs_0_), channel_id=1, source_target_pairs={{0,8},{1,9},{2,10},{3,11},{4,12},{5,13},{6,14},{7,15},{8,0},{9,1},... | collective-permute-start | bytes 1179656 | tf_op jit(solution)/shard_map/ppermute | solution.py:27
  22.3 25.8 %collective-permute-start.5 = (bf16[512,1024]{1,0:T(8,128)(2,1)}, bf16[512,1024]{1,0:T(8,128)(2,1)}, u32[]{:S(2)}, u32[]{:S(2)}) collective-permute-start(bf16[512,1024]{1,0:T(8,128)(2,1)} %held.7), channel_id=1, source_target_pairs={{0,5},{2,7},{4,9},{5,0},{6,11},{7,2},{8,13},{9,4},{10,15},{11,6},{... | collective-permute-start | bytes 3145736 | tf_op jit(solution)/shard_map/ppermute | solution.py:27
  24.2 22.4 %collective-permute-start.6 = (bf16[2,1024,128]{2,1,0:T(8,128)(2,1)}, bf16[2,1024,128]{2,1,0:T(8,128)(2,1)}, u32[]{:S(2)}, u32[]{:S(2)}) collective-permute-start(bf16[2,1024,128]{2,1,0:T(8,128)(2,1)} %get-tuple-element.31), channel_id=1, source_target_pairs={{0,3},{1,2},{2,1},{3,0},{4,7},{5,6},{6,5},{7,4},{8,11},{9,10},{10,... | collective-permute-start | bytes 1572872 | tf_op jit(solution)/shard_map/ppermute | solution.py:27
  34.7 12.9 %collective-permute-start.7 = (bf16[256,512]{1,0:T(8,128)(2,1)}, bf16[256,512]{1,0:T(8,128)(2,1)}, u32[]{:S(2)}, u32[]{:S(2)}) collective-permute-start(bf16[256,512]{1,0:T(8,128)(2,1)} %get-tuple-element.28.refs_1_.refs_13_), channel_id=1, source_target_pairs={{0,2},{1,3},{2,0},{3,1},{4,6},{5,7},{6,4},{7,5},{8,10},{9,11},{10,... | collective-permute-start | bytes 786440 | tf_op jit(solution)/shard_map/ppermute | solution.py:27
  36.5 10.2 %collective-permute-start.4 = (bf16[128,512]{1,0:T(8,128)(2,1)}, bf16[128,512]{1,0:T(8,128)(2,1)}, u32[]{:S(2)}, u32[]{:S(2)}) collective-permute-start(bf16[128,512]{1,0:T(8,128)(2,1)} %get-tuple-element.29), channel_id=1, source_target_pairs={{0,16},{1,17},{2,18},{3,19},{4,20},{5,21},{6,22},{7,23},{8,24},{9,... | collective-permute-start | bytes 393224 | tf_op jit(solution)/shard_map/ppermute | solution.py:27
  48.1 4.0 %collective-permute-start.8 = (bf16[512,1024]{1,0:T(8,128)(2,1)}, bf16[512,1024]{1,0:T(8,128)(2,1)}, u32[]{:S(2)}, u32[]{:S(2)}) collective-permute-start(bf16[512,1024]{1,0:T(8,128)(2,1)} %get-tuple-element.32.refs_1_), channel_id=1, source_target_pairs={{0,1},{1,0},{2,3},{3,2},{4,5},{5,4},{6,7},{7,6},{8,9},{9,8},{10,11... | collective-permute-start | bytes 3145736 | tf_op jit(solution)/shard_map/ppermute | solution.py:27
  48.1 11.3 %collective-permute-start.16 = (bf16[256,512]{1,0:T(8,128)(2,1)}, bf16[256,512]{1,0:T(8,128)(2,1)}, u32[]{:S(2)}, u32[]{:S(2)}) collective-permute-start(bf16[256,512]{1,0:T(8,128)(2,1)} %get-tuple-element.28.refs_1_.refs_13_), channel_id=1, source_target_pairs={{0,1},{1,0},{2,3},{3,2},{4,5},{5,4},{6,7},{7,6},{8,9},{9,8},{10,11... | collective-permute-start | bytes 786440 | tf_op jit(solution)/shard_map/ppermute | solution.py:27
  48.6 9.5 %collective-permute-start.10 = (bf16[128,512]{1,0:T(8,128)(2,1)}, bf16[128,512]{1,0:T(8,128)(2,1)}, u32[]{:S(2)}, u32[]{:S(2)}) collective-permute-start(bf16[128,512]{1,0:T(8,128)(2,1)} %get-tuple-element.36.refs_5_), channel_id=1, source_target_pairs={{0,2},{1,3},{2,0},{3,1},{4,6},{5,7},{6,4},{7,5},{8,10},{9,11},{10,... | collective-permute-start | bytes 393224 | tf_op jit(solution)/shard_map/ppermute | solution.py:27
  50.1 8.7 %collective-permute-start.11 = (bf16[128,512]{1,0:T(8,128)(2,1)}, bf16[128,512]{1,0:T(8,128)(2,1)}, u32[]{:S(2)}, u32[]{:S(2)}) collective-permute-start(bf16[128,512]{1,0:T(8,128)(2,1)} %get-tuple-element.36.refs_5_), channel_id=1, source_target_pairs={{0,4},{1,5},{2,6},{3,7},{4,0},{5,1},{6,2},{7,3},{8,12},{9,13},{10,... | collective-permute-start | bytes 393224 | tf_op jit(solution)/shard_map/ppermute | solution.py:27
  51.9 7.0 %collective-permute-start.12 = (bf16[128,512]{1,0:T(8,128)(2,1)}, bf16[128,512]{1,0:T(8,128)(2,1)}, u32[]{:S(2)}, u32[]{:S(2)}) collective-permute-start(bf16[128,512]{1,0:T(8,128)(2,1)} %get-tuple-element.36.refs_5_), channel_id=1, source_target_pairs={{0,6},{1,7},{2,4},{3,5},{4,2},{5,3},{6,0},{7,1},{8,14},{9,15},{10,... | collective-permute-start | bytes 393224 | tf_op jit(solution)/shard_map/ppermute | solution.py:27
  52.1 8.1 %collective-permute-start.17 = (bf16[256,512]{1,0:T(8,128)(2,1)}, bf16[256,512]{1,0:T(8,128)(2,1)}, u32[]{:S(2)}, u32[]{:S(2)}) collective-permute-start(bf16[256,512]{1,0:T(8,128)(2,1)} %get-tuple-element.40.refs_15_), channel_id=1, source_target_pairs={{0,1},{1,0},{2,3},{3,2},{4,5},{5,4},{6,7},{7,6},{8,9},{9,8},{10,11... | collective-permute-start | bytes 786440 | tf_op jit(solution)/shard_map/ppermute | solution.py:27
  58.1 2.1 %collective-permute-start.9 = (bf16[128,512]{1,0:T(8,128)(2,1)}, bf16[128,512]{1,0:T(8,128)(2,1)}, u32[]{:S(2)}, u32[]{:S(2)}) collective-permute-start(bf16[128,512]{1,0:T(8,128)(2,1)} %get-tuple-element.36.refs_5_), channel_id=1, source_target_pairs={{0,1},{1,0},{2,3},{3,2},{4,5},{5,4},{6,7},{7,6},{8,9},{9,8},{10,11... | collective-permute-start | bytes 393224 | tf_op jit(solution)/shard_map/ppermute | solution.py:27
  58.9 1.7 %collective-permute-start.13 = (bf16[128,512]{1,0:T(8,128)(2,1)}, bf16[128,512]{1,0:T(8,128)(2,1)}, u32[]{:S(2)}, u32[]{:S(2)}) collective-permute-start(bf16[128,512]{1,0:T(8,128)(2,1)} %get-tuple-element.37.refs_7_), channel_id=1, source_target_pairs={{0,1},{1,0},{2,3},{3,2},{4,5},{5,4},{6,7},{7,6},{8,9},{9,8},{10,11... | collective-permute-start | bytes 393224 | tf_op jit(solution)/shard_map/ppermute | solution.py:27
  59.0 1.8 %collective-permute-start.14 = (bf16[128,512]{1,0:T(8,128)(2,1)}, bf16[128,512]{1,0:T(8,128)(2,1)}, u32[]{:S(2)}, u32[]{:S(2)}) collective-permute-start(bf16[128,512]{1,0:T(8,128)(2,1)} %get-tuple-element.38.refs_9_), channel_id=1, source_target_pairs={{0,1},{1,0},{2,3},{3,2},{4,5},{5,4},{6,7},{7,6},{8,9},{9,8},{10,11... | collective-permute-start | bytes 393224 | tf_op jit(solution)/shard_map/ppermute | solution.py:27
  59.4 1.7 %collective-permute-start.15 = (bf16[128,512]{1,0:T(8,128)(2,1)}, bf16[128,512]{1,0:T(8,128)(2,1)}, u32[]{:S(2)}, u32[]{:S(2)}) collective-permute-start(bf16[128,512]{1,0:T(8,128)(2,1)} %get-tuple-element.39.refs_11_), channel_id=1, source_target_pairs={{0,1},{1,0},{2,3},{3,2},{4,5},{5,4},{6,7},{7,6},{8,9},{9,8},{10,11... | collective-permute-start | bytes 393224 | tf_op jit(solution)/shard_map/ppermute | solution.py:27

commit v5 on v4

--- a/solution.py
+++ b/solution.py
@@ -11,7 +11,8 @@
 VMEM = 64 * 1024 * 1024
 COST_A = 1
 COST_B = 1
-COST_C = 7000000000
+COST_C = int(7000000000.0)
+COST_D = int(10000000000.0)
 HBM = pl.BlockSpec(memory_space=pltpu.HBM)
 SMEM = pl.BlockSpec(memory_space=pltpu.SMEM)
 
@@ -56,12 +57,12 @@
     step = REACH * B
     parts = depth // step
 
-    def kernel(one_ref, two_ref, vectors_ref, send_ref, keep_ref, edge_ref, *scratch):
-        rights, block, total, result, right_sems, block_sems, out_sems, edge_sem = scratch
-        mine, last_first = lax.axis_index("rows") % 2, lax.axis_index("cols") % 2 == 0
+    def kernel(one_ref, two_ref, vectors_ref, send_ref, keep_ref, *scratch):
+        rights, block, total, result, right_sems, block_sems, out_sems = scratch
+        mine = lax.axis_index("rows") % 2
         copies, places = [], []
         for i in range(parts):
-            place = span(jnp.where(last_first, parts - 1 - i, i), step)
+            place = pl.ds(i * step, step)
             places.append(place)
             copies.append(
                 [
@@ -74,12 +75,9 @@
             )
             for copy in copies[-1]:
                 copy.start()
-        edge_copy = pltpu.make_async_copy(block.at[places[0]], edge_ref, edge_sem)
         for i in range(parts):
             for copy in copies[i]:
                 copy.wait()
-            if i == 0:
-                edge_copy.start()
             part = lax.dot_general(
                 rights[places[i]], block[places[i]], (((0,), (0,)), ((), ())), preferred_element_type=jnp.float32
             )
@@ -108,7 +106,6 @@
             copy.start()
         for copy in outs:
             copy.wait()
-        edge_copy.wait()
 
     return called(
         kernel,
@@ -119,7 +116,6 @@
         [
             jax.ShapeDtypeStruct((3 * rank, half), jnp.bfloat16),
             jax.ShapeDtypeStruct((3 * rank, half), jnp.bfloat16),
-            jax.ShapeDtypeStruct((step, width), jnp.bfloat16),
         ],
         [
             pltpu.VMEM((depth, 2 * rank), jnp.bfloat16),
@@ -129,41 +125,48 @@
             pltpu.SemaphoreType.DMA((2, parts)),
             pltpu.SemaphoreType.DMA((parts,)),
             pltpu.SemaphoreType.DMA((2, 3)),
-            pltpu.SemaphoreType.DMA,
         ],
     )
 
 
-def near_field(near_cols, near_tiles, vectors, first, count, sofar=None, halos=(), after=(), flops=1):
+def near_field(near_cols, near_tiles, vectors, first, count, sofar=None, halos=(), low_rank=None, after=(), flops=1):
     tiles, nnz = near_cols.shape
     rows, width = tiles * B, vectors.shape[1]
+    half = width // 2
     window = vectors.shape[0] // B + 2 * REACH
-    half = width // 2
+    inside = count
     given = 0 if sofar is None else 1
-    inside = count
-    if halos:
-        count += 2 * REACH
     sizes = []
     while sum(sizes) < inside:
         sizes.append(min((1, 3, 4)[min(len(sizes), 2)], inside - sum(sizes)))
-    if inside and sizes[-1] == 1:
-        sizes = sizes[:-2] + [sizes[-2] + 1] if len(sizes) > 1 else sizes
     if halos:
         sizes += [REACH, REACH]
-    groups = len(sizes)
-    begins = [sum(sizes[:g]) for g in range(groups)]
+    count = sum(sizes)
+    near_groups = len(sizes)
+    begins = [sum(sizes[:g]) * B for g in range(near_groups)] + [count * B]
+    level, own, pieces, coeffs = low_rank or (0, None, (), ())
+    rank = own.shape[1] if low_rank else 0
+    offsets = len(pieces) + 1 if low_rank else 0
+    whole = len(coeffs) == offsets
+    depths = [size * B for size in sizes] + ([offsets * rank] if low_rank else [])
+    groups, depth = len(depths), sum(depths)
+    bound = [*halos, *([own, *pieces, *coeffs] if low_rank else [])]
 
     def kernel(cols_ref, tiles_ref, vectors_ref, *refs):
         sofar_refs, refs = refs[:given], refs[given:]
-        halo_refs, refs = refs[: len(halos)], refs[len(halos) + len(after) :]
-        out_ref, slots, wide, tall, total, result, tile_sems, tall_sems, sofar_sem, out_sems = refs
-        col = lax.axis_index("cols")
-
-        for t in range(tiles):
-            for c in range(window):
-                slots[t, c] = -1
-            for k in range(nnz):
-                slots[t, cols_ref[t, k]] = k
+        halo_refs, refs = refs[: len(halos)], refs[len(halos) :]
+        left_refs, refs = refs[:offsets], refs[offsets:]
+        coeff_refs, refs = refs[: len(coeffs)], refs[len(coeffs) + len(after) :]
+        out_ref, slots, wide, tall, total, result, *refs = refs
+        tile_sems, tall_sems, rank_sems, sofar_sem, out_sems = refs
+        mine, col = lax.axis_index("rows") % 2, lax.axis_index("cols")
+
+        if count:
+            for t in range(tiles):
+                for c in range(window):
+                    slots[t, c] = -1
+                for k in range(nnz):
+                    slots[t, cols_ref[t, k]] = k
 
         def tile_copy(t, c):
             if c < inside:
@@ -180,46 +183,66 @@
             )
             return slot >= 0, copy
 
+        def group_tiles(g):
+            return [(t, c) for c in range(begins[g] // B, begins[g] // B + sizes[g]) for t in range(tiles)]
+
         def tall_copy(g):
-            place = pl.ds(begins[g] * B, sizes[g] * B)
-            if begins[g] < inside:
-                source = vectors_ref.at[pl.ds((first + begins[g]) * B, sizes[g] * B)]
+            if begins[g] < inside * B:
+                source = vectors_ref.at[pl.ds(first * B + begins[g], depths[g])]
             else:
-                source = halo_refs[g - groups]
-            return pltpu.make_async_copy(source, tall.at[place], tall_sems.at[g])
-
+                source = halo_refs[g - near_groups]
+            return pltpu.make_async_copy(source, tall.at[pl.ds(begins[g], depths[g])], tall_sems.at[g])
+
+        rank_copies = []
+        for d in range(offsets):
+            source = left_refs[d].at[level] if d else left_refs[0].at[span(col, rows)]
+            place = pl.ds(count * B + d * rank, rank)
+            rank_copies.append(pltpu.make_async_copy(source, wide.at[:, place], rank_sems.at[d, 2]))
+            for n in range(2):
+                if whole:
+                    source, columns = coeff_refs[d].at[pl.ds(n * rank, rank)], pl.ds(n * half, half)
+                else:
+                    source, columns = coeff_refs[n * offsets + d], span(mine ^ n, half)
+                rank_copies.append(pltpu.make_async_copy(source, tall.at[place, columns], rank_sems.at[d, n]))
         if given:
             sofar_copy = pltpu.make_async_copy(sofar_refs[0], result, sofar_sem)
-        for g in range(groups):
+
+        for g in range(near_groups):
             tall_copy(g).start()
-            for c in range(begins[g], begins[g] + sizes[g]):
-                for t in range(tiles):
-                    there, copy = tile_copy(t, c)
-                    pl.when(there)(copy.start)
-
-                    @pl.when(jnp.logical_not(there))
-                    def _():
-                        wide[t * B : (t + 1) * B, c * B : (c + 1) * B] = jnp.zeros((B, B), jnp.bfloat16)
-
+            for t, c in group_tiles(g):
+                there, copy = tile_copy(t, c)
+                pl.when(there)(copy.start)
+
+                @pl.when(jnp.logical_not(there))
+                def _():
+                    wide[t * B : (t + 1) * B, c * B : (c + 1) * B] = jnp.zeros((B, B), jnp.bfloat16)
+
+        for copy in rank_copies:
+            copy.start()
         if given:
             sofar_copy.start()
         outs = []
         for g in range(groups):
-            tall_copy(g).wait()
-            for c in range(begins[g], begins[g] + sizes[g]):
-                for t in range(tiles):
+            last = g == groups - 1
+            if g < near_groups:
+                tall_copy(g).wait()
+                for t, c in group_tiles(g):
                     there, copy = tile_copy(t, c)
                     pl.when(there)(copy.wait)
-            chosen = pl.ds(begins[g] * B, sizes[g] * B)
-            if g == groups - 1:
+            else:
+                for copy in rank_copies:
+                    copy.wait()
+            if last:
                 if given:
                     sofar_copy.wait()
-            for n in range(2):
-                columns = pl.ds(n * half, half)
+            chosen = pl.ds(begins[g], depths[g])
+            cuts = 4 if last else 2
+            for n in range(cuts):
+                columns = pl.ds(n * (width // cuts), width // cuts)
                 part = jnp.dot(wide[:, chosen], tall[chosen, columns], preferred_element_type=jnp.float32)
                 if g > 0:
                     part = total[:, columns] + part
-                if g < groups - 1:
+                if not last:
                     total[:, columns] = part
                 else:
                     if given:
@@ -234,20 +257,21 @@
 
     scratch = [
         pltpu.SMEM((tiles, window), jnp.int32),
-        pltpu.VMEM((rows, count * B), jnp.bfloat16),
-        pltpu.VMEM((count * B, width), jnp.bfloat16),
+        pltpu.VMEM((rows, depth), jnp.bfloat16),
+        pltpu.VMEM((depth, width), jnp.bfloat16),
         pltpu.VMEM((rows, width), jnp.float32),
         pltpu.VMEM((rows, width), jnp.bfloat16),
-        pltpu.SemaphoreType.DMA((tiles, count)),
+        pltpu.SemaphoreType.DMA((tiles, max(count, 1))),
         pltpu.SemaphoreType.DMA((groups,)),
+        pltpu.SemaphoreType.DMA((max(offsets, 1), 3)),
         pltpu.SemaphoreType.DMA,
-        pltpu.SemaphoreType.DMA((2,)),
+        pltpu.SemaphoreType.DMA((4,)),
     ]
     return called(
         kernel,
         "near_field",
         [near_cols],
-        [near_tiles, vectors] + ([sofar] if given else []) + [*halos],
+        [near_tiles, vectors] + ([sofar] if given else []) + bound,
         after,
         jax.ShapeDtypeStruct((rows, width), jnp.bfloat16),
         scratch,
@@ -255,14 +279,19 @@
     )
 
 
-def packed(lefts, shares, after):
+def packed(vectors, lefts, shares, after):
     depth, rank = lefts[0].shape
     rows = depth // shares
 
-    def kernel(one_ref, two_ref, *refs):
+    edge, width = REACH * B, vectors.shape[1]
+
+    def kernel(vectors_ref, one_ref, two_ref, *refs):
         refs = refs[len(after) :]
-        out_refs, (block, in_sems, out_sems) = refs[: shares - 1], refs[shares - 1 :]
+        edge_ref, out_refs, (rows_held, block, edge_sems, in_sems, out_sems) = refs[0], refs[1:shares], refs[shares:]
         col = lax.axis_index("cols")
+        place = span(jnp.where(col % 2 == 0, depth // edge - 1, 0), edge)
+        edge_in = pltpu.make_async_copy(vectors_ref.at[place], rows_held, edge_sems.at[0])
+        edge_out = pltpu.make_async_copy(rows_held, edge_ref, edge_sems.at[1])
         ins = [
             [
                 pltpu.make_async_copy(
@@ -275,12 +304,16 @@
         for copies in ins:
             for copy in copies:
                 copy.start()
+        edge_in.start()
         outs = []
         for d in range(shares - 1):
             for copy in ins[d]:
                 copy.wait()
             outs.append(pltpu.make_async_copy(block.at[d], out_refs[d], out_sems.at[d]))
             outs[-1].start()
+        edge_in.wait()
+        edge_out.start()
+        outs.append(edge_out)
         for copy in outs:
             copy.wait()
 
@@ -288,42 +321,41 @@
         kernel,
         "packed",
         [],
-        [*lefts],
+        [vectors, *lefts],
         after,
-        [jax.ShapeDtypeStruct((2, rows, rank), jnp.bfloat16)] * (shares - 1),
+        [jax.ShapeDtypeStruct((edge, width), jnp.bfloat16)]
+        + [jax.ShapeDtypeStruct((2, rows, rank), jnp.bfloat16)] * (shares - 1),
         [
+            pltpu.VMEM((edge, width), jnp.bfloat16),
             pltpu.VMEM((shares - 1, 2, rows, rank), jnp.bfloat16),
+            pltpu.SemaphoreType.DMA((2,)),
             pltpu.SemaphoreType.DMA((shares - 1, 2)),
             pltpu.SemaphoreType.DMA((shares - 1,)),
         ],
     )
 
 
-def add_levels(sofar, lefts, pieces, coeffs_one, coeffs_two):
+def add_level(sofar, level, own, pieces, coeffs, after=()):
     rows, width = sofar.shape
     half = width // 2
-    rank = lefts[0].shape[1]
+    rank = own.shape[1]
     offsets = len(pieces) + 1
-    inner = 2 * offsets * rank
-
-    def kernel(sofar_ref, *refs):
-        left_refs, piece_refs, refs = refs[:2], refs[2 : 1 + offsets], refs[1 + offsets :]
-        one_refs, refs = refs[: 2 * offsets], refs[2 * offsets :]
-        two_refs, refs = refs[:offsets], refs[offsets:]
-        out_ref, wide, ranks, result, left_sems, rank_sems, sofar_sems, out_sems = refs
-        mine, col = lax.axis_index("rows") % 2, lax.axis_index("cols")
-        places = [span(mine ^ n, half) for n in range(2)]
+    inner = offsets * rank
+
+    def kernel(sofar_ref, own_ref, *refs):
+        piece_refs, refs = refs[: offsets - 1], refs[offsets - 1 :]
+        coeff_refs, refs = refs[:offsets], refs[offsets + len(after) :]
+        out_ref, lefts, ranks, result, left_sems, rank_sems, sofar_sems, out_sems = refs
+        col = lax.axis_index("cols")
+        places = [pl.ds(n * half, half) for n in range(2)]
         copies = [[], []]
         for d in range(offsets):
-            for level in range(2):
-                place = pl.ds((level * offsets + d) * rank, rank)
-                source = piece_refs[d - 1].at[level] if d else left_refs[level].at[span(col, rows)]
-                copies[0].append(pltpu.make_async_copy(source, wide.at[:, place], left_sems.at[level, d]))
-                for n in range(2):
-                    source = two_refs[d].at[span(mine ^ n, rank)] if level else one_refs[n * offsets + d]
-                    copies[n].append(
-                        pltpu.make_async_copy(source, ranks.at[n, place], rank_sems.at[n, level, d])
-                    )
+            place = pl.ds(d * rank, rank)
+            source = piece_refs[d - 1].at[level] if d else own_ref.at[span(col, rows)]
+            copies[0].append(pltpu.make_async_copy(source, lefts.at[:, place], left_sems.at[d]))
+            for n in range(2):
+                source = coeff_refs[d].at[pl.ds(n * rank, rank)]
+                copies[n].append(pltpu.make_async_copy(source, ranks.at[n, place], rank_sems.at[n, d]))
         for n in range(2):
             copies[n].append(
                 pltpu.make_async_copy(sofar_ref.at[:, places[n]], result.at[n], sofar_sems.at[n])
@@ -334,7 +366,7 @@
         for n in range(2):
             for copy in copies[n]:
                 copy.wait()
-            part = jnp.dot(wide[...], ranks[n], preferred_element_type=jnp.float32)
+            part = jnp.dot(lefts[...], ranks[n], preferred_element_type=jnp.float32)
             result[n] = (result[n].astype(jnp.float32) + part).astype(jnp.bfloat16)
             outs.append(pltpu.make_async_copy(result.at[n], out_ref.at[:, places[n]], out_sems.at[n]))
             outs[-1].start()
@@ -343,20 +375,21 @@
 
     return called(
         kernel,
-        "add_levels",
+        "add_level",
         [],
-        [sofar, *lefts, *pieces, *coeffs_one, *coeffs_two],
-        (),
+        [sofar, own, *pieces, *coeffs],
+        after,
         jax.ShapeDtypeStruct((rows, width), jnp.bfloat16),
         [
             pltpu.VMEM((rows, inner), jnp.bfloat16),
             pltpu.VMEM((2, inner, half), jnp.bfloat16),
             pltpu.VMEM((2, rows, half), jnp.bfloat16),
+            pltpu.SemaphoreType.DMA((offsets,)),
             pltpu.SemaphoreType.DMA((2, offsets)),
-            pltpu.SemaphoreType.DMA((2, 2, offsets)),
             pltpu.SemaphoreType.DMA((2,)),
             pltpu.SemaphoreType.DMA((2,)),
         ],
+        flops=COST_D,
     )
 
 
@@ -430,7 +463,7 @@
     inside = depth // B
 
     near_args = (near_cols, near_tiles, vectors)
-    cuts = [0, inside // 8, 9 * inside // 16, inside]
+    cuts = [0, inside // 4, 11 * inside // 16, inside]
 
     def near_part(part, sofar, after, flops):
         first, last = cuts[part : part + 2]
@@ -439,10 +472,10 @@
     def summed(a, b):
         return (a.astype(jnp.float32) + b.astype(jnp.float32)).astype(jnp.bfloat16)
 
-    send, keep, edge = project(right_one, right_two, vectors)
+    send, keep = project(right_one, right_two, vectors)
     arrived = flipped(send, 1, 0)
 
-    pieces = packed((left_one, left_two), n_cols, (keep,))
+    edge, *pieces = packed(vectors, (left_one, left_two), n_cols, (keep,))
     pieces = [flipped(piece, 0, offset) for offset, piece in enumerate(pieces, 1)]
 
     near = near_part(0, None, (keep,), COST_A)
@@ -454,26 +487,29 @@
 
     (edge,) = held([edge], [both])
     halo = moved(edge, lambda r, c: (r + 1 if c % 2 == 0 else r - 1, c ^ 1))
-    near = near_part(1, near, (both,), COST_B)
-    both, *pieces[:-1] = held([both, *pieces[:-1]], [near])
+    near = near_part(1, near, (both, *pieces[1:-1]), COST_B)
+    both, pieces[0] = held([both, pieces[0]], [near])
     one, two = parted(both, arrived, rank)
     one = flipped(one, 2 ** (bits - 1), 0)
     near = near_part(2, near, (two,), COST_C)
 
     offsets = range(0, n_cols, 2)
     twos = [two] + [flipped(two, 0, offset) for offset in offsets[1:]]
-    one, halo, pieces[-1], *rest = held([one, halo, pieces[-1], *twos[1:]], [near])
+    beside = flipped(two, 0, 1)
+    one, pieces[-1], beside, *rest = held([one, pieces[-1], beside, *twos[1:]], [near])
     twos = [two] + rest
     ones = [
         one if (other, offset) == (0, 0) else flipped(one, other, offset)
         for other in range(2)
         for offset in offsets
     ]
-    near = near_field(*near_args, 0, 0, near, (halo, flipped(halo, 0, 1)))
-    ones = [one, *held(ones[1:], [near])]
-    coeffs_two = [x for there in twos for x in (there, flipped(there, 0, 1))]
+    coeffs_two = [two, beside] + [x for there in rest for x in (there, flipped(there, 0, 1))]
+    (halo,) = held([halo], coeffs_two[-1:])
+    halos = (halo, flipped(halo, 0, 1))
+    near = add_level(near, 1, left_two, pieces, coeffs_two, after=(halo,))
+    ones = list(held(ones, [near]))
     coeffs_one = [x for there in ones for x in (there, flipped(there, 0, 1))]
-    return add_levels(near, (left_one, left_two), pieces, coeffs_one, coeffs_two)
+    return near_field(*near_args, 0, 0, near, halos, (0, left_one, pieces, coeffs_one))
 
 
 def solution(mesh):

time: 68.3 us -> 66.7 us (0.977)
  waiting for transfers between devices: 4.76 us -> 3.81 us
  starting transfers between devices: 18.2 us -> 17.4 us
    ppermute x18, waiting for transfers between devices: 4.76 us -> 3.81 us  [moved(): return lax.ppermute(value, AXES, pairs)]
    ppermute x18, starting transfers between devices: 18.2 us -> 17.4 us  [moved(): return lax.ppermute(value, AXES, pairs)]
    pallas_call x13 -> x14, Pallas kernels: 42.3 us -> 42.5 us  [called(): pl.pallas_call(kernel, out_shape=out_shape, in_specs=[SMEM] * len(smem) +...]
  transfers between devices with their start and end apart: 18 -> 18, of which waited for: 9 -> 8; matrix products, arithmetic and copies ran while one was open for 3% -> 3% of each run, Pallas kernels for 44% -> 45%
where the time goes in v5:
time: 66.7 us; the launch traced here: 65.9 us
  Pallas kernels  42.5 us (64%)
  starting transfers between devices  17.4 us (26%)
  waiting for transfers between devices  3.81 us (6%)
  other arithmetic  1.96 us (3%)
    pallas_call x14, Pallas kernels, called(): pl.pallas_call(kernel, out_shape=out_shape, in_specs=[SMEM] * len(smem) +...  42.5 us
    ppermute x18, starting transfers between devices, moved(): return lax.ppermute(value, AXES, pairs)  17.4 us
    ppermute x18, waiting for transfers between devices, moved(): return lax.ppermute(value, AXES, pairs)  3.81 us
    convert_element_type x1, other arithmetic, summed(): return (a.astype(jnp.float32) + b.astype(jnp.float32)).astype(jnp.bfloat16)  1.96 us
  transfers between devices with their start and end apart: 18, of which 8 were waited for; matrix products, arithmetic and copies ran while one was open for 3% of the time, Pallas kernels for 45%

profile of v5, /device:TPU:0, one launch (start us, length us, event | category | flops | bytes accessed | tf_op | source)
XLA Modules:
  0.0 65.9 jit_solution(16465466219269772094)
XLA Ops:
  0.0 5.7 %project.1 = (bf16[384,512]{1,0:T(8,128)(2,1)}, bf16[384,512]{1,0:T(8,128)(2,1)}) custom-call(bf16[4096,128]{1,0:T(8,128)(2,1)} %one_ref.2, bf16[4096,128]{1,0:T(8,128)(2,1)} %two_ref.2, bf16[4096,1024]{1,0:T(8,128)(2,1)} %vectors_ref.11), custom_call_target="tpu_custom_call" | custom-call | flops 1 | bytes 1 | tf_op jit(solution)/shard_map/project/pallas_call | solution.py:40
  5.7 3.0 %collective-permute-start = (bf16[384,512]{1,0:T(8,128)(2,1)}, bf16[384,512]{1,0:T(8,128)(2,1)}, u32[]{:S(2)}, u32[]{:S(2)}) collective-permute-start(bf16[384,512]{1,0:T(8,128)(2,1)} %get-tuple-element.24), channel_id=1, source_target_pairs={{0,4},{1,5},{2,6},{3,7},{4,0},{5,1},{6,2},{7,3},{8,12},{9,13},{10,... | collective-permute-start | bytes 1179656 | tf_op jit(solution)/shard_map/ppermute | solution.py:28
  8.7 2.8 %packed.1 = (bf16[512,1024]{1,0:T(8,128)(2,1)}, bf16[2,1024,128]{2,1,0:T(8,128)(2,1)}, bf16[2,1024,128]{2,1,0:T(8,128)(2,1)}, bf16[2,1024,128]{2,1,0:T(8,128)(2,1)}) custom-call(bf16[4096,1024]{1,0:T(8,128)(2,1)} %vectors_ref.11, bf16[4096,128]{1,0:T(8,128)(2,1)} %refs_3_.1, bf16[4096,128]{1,0:T(8,128)(2,1)} %own_ref.1, ...), custom_call_target="tpu_custom_call" | custom-call | flops 1 | bytes 1 | tf_op jit(solution)/shard_map/packed/pallas_call | solution.py:40
  11.5 1.6 %collective-permute-start.1 = (bf16[2,1024,128]{2,1,0:T(8,128)(2,1)}, bf16[2,1024,128]{2,1,0:T(8,128)(2,1)}, u32[]{:S(2)}, u32[]{:S(2)}) collective-permute-start(bf16[2,1024,128]{2,1,0:T(8,128)(2,1)} %get-tuple-element.25), channel_id=1, source_target_pairs={{0,2},{1,3},{2,0},{3,1},{4,6},{5,7},{6,4},{7,5},{8,10},{9,11},{10,... | collective-permute-start | bytes 1572872 | tf_op jit(solution)/shard_map/ppermute | solution.py:28
  13.1 5.9 %near_field.4.refs_1_.refs_0_ = bf16[1024,1024]{1,0:T(8,128)(2,1)} custom-call(s32[4,16]{1,0:T(4,128)} %cols_ref.7, bf16[4,16,256,256]{3,2,1,0:T(8,128)(2,1)} %tiles_ref.7, bf16[4096,1024]{1,0:T(8,128)(2,1)} %vectors_ref.11, bf16[384,512]{1,0:T(8,128)(2,1)} %get-tuple-element.23.refs_0_), custom_call_target="tpu_custom_call" | custom-call | flops 1 | bytes 1 | tf_op jit(solution)/shard_map/near_field/pallas_call | solution.py:40
  19.0 0.1 collective-permute-start.2
  19.1 0.0 collective-permute-done
  19.1 2.0 %add_convert_fusion.refs_1_.refs_0_ = bf16[384,512]{1,0:T(8,128)(2,1)} fusion(bf16[384,512]{1,0:T(8,128)(2,1)} %collective-permute-done, bf16[384,512]{1,0:T(8,128)(2,1)} %held.6), kind=kLoop, calls=%fused_computation | loop fusion | flops 786432 | bytes 1179648 | tf_op jit(solution)/shard_map/convert_element_type | solution.py:473
  21.0 1.6 %collective-permute-start.3 = (bf16[384,512]{1,0:T(8,128)(2,1)}, bf16[384,512]{1,0:T(8,128)(2,1)}, u32[]{:S(2)}, u32[]{:S(2)}) collective-permute-start(bf16[384,512]{1,0:T(8,128)(2,1)} %add_convert_fusion.refs_1_.refs_0_), channel_id=1, source_target_pairs={{0,8},{1,9},{2,10},{3,11},{4,12},{5,13},{6,14},{7,15},{8,0},{9,1},... | collective-permute-start | bytes 1179656 | tf_op jit(solution)/shard_map/ppermute | solution.py:28
  22.6 2.1 %collective-permute-start.9 = (bf16[512,1024]{1,0:T(8,128)(2,1)}, bf16[512,1024]{1,0:T(8,128)(2,1)}, u32[]{:S(2)}, u32[]{:S(2)}) collective-permute-start(bf16[512,1024]{1,0:T(8,128)(2,1)} %held.9), channel_id=1, source_target_pairs={{0,5},{2,7},{4,9},{5,0},{6,11},{7,2},{8,13},{9,4},{10,15},{11,6},{... | collective-permute-start | bytes 3145736 | tf_op jit(solution)/shard_map/ppermute | solution.py:28
  24.7 0.1 collective-permute-start.5
  24.8 0.5 collective-permute-done.1.refs_2_.refs_1_.refs_5_
  25.3 7.7 %near_field.5.refs_2_.refs_0_ = bf16[1024,1024]{1,0:T(8,128)(2,1)} custom-call(s32[4,16]{1,0:T(4,128)} %cols_ref.7, bf16[4,16,256,256]{3,2,1,0:T(8,128)(2,1)} %tiles_ref.7, bf16[4096,1024]{1,0:T(8,128)(2,1)} %vectors_ref.11, bf16[1024,1024]{1,0:T(8,128)(2,1)} %near_field.4.refs_1_.refs_0_, bf16[384,512]{1,0:T(8,128)(2,1)} %add_convert_fusion.refs_1_.refs_0_, ...), custom_call_target="tpu_custom_call" | custom-call | flops 1 | bytes 1 | tf_op jit(solution)/shard_map/near_field/pallas_call | solution.py:40
  33.0 0.0 collective-permute-done.2.refs_1_
  33.0 0.2 collective-permute-done.3.b_ref
  33.3 1.8 %parted.1 = (bf16[128,512]{1,0:T(8,128)(2,1)}, bf16[256,512]{1,0:T(8,128)(2,1)}) custom-call(bf16[384,512]{1,0:T(8,128)(2,1)} %get-tuple-element.27.a_ref, bf16[384,512]{1,0:T(8,128)(2,1)} %collective-permute-done.3.b_ref), custom_call_target="tpu_custom_call" | custom-call | flops 1 | bytes 1 | tf_op jit(solution)/shard_map/parted/pallas_call | solution.py:40
  35.1 1.5 %collective-permute-start.7 = (bf16[256,512]{1,0:T(8,128)(2,1)}, bf16[256,512]{1,0:T(8,128)(2,1)}, u32[]{:S(2)}, u32[]{:S(2)}) collective-permute-start(bf16[256,512]{1,0:T(8,128)(2,1)} %get-tuple-element.28.refs_1_.refs_3_), channel_id=1, source_target_pairs={{0,2},{1,3},{2,0},{3,1},{4,6},{5,7},{6,4},{7,5},{8,10},{9,11},{10,... | collective-permute-start | bytes 786440 | tf_op jit(solution)/shard_map/ppermute | solution.py:28
  36.6 0.0 collective-permute-start.6
  36.6 2.7 %collective-permute-start.4 = (bf16[128,512]{1,0:T(8,128)(2,1)}, bf16[128,512]{1,0:T(8,128)(2,1)}, u32[]{:S(2)}, u32[]{:S(2)}) collective-permute-start(bf16[128,512]{1,0:T(8,128)(2,1)} %get-tuple-element.30), channel_id=1, source_target_pairs={{0,16},{1,17},{2,18},{3,19},{4,20},{5,21},{6,22},{7,23},{8,24},{9,... | collective-permute-start | bytes 393224 | tf_op jit(solution)/shard_map/ppermute | solution.py:28
  39.3 6.6 %near_field.6.refs_4_.sofar_ref = bf16[1024,1024]{1,0:T(8,128)(2,1)} custom-call(s32[4,16]{1,0:T(4,128)} %cols_ref.7, bf16[4,16,256,256]{3,2,1,0:T(8,128)(2,1)} %tiles_ref.7, bf16[4096,1024]{1,0:T(8,128)(2,1)} %vectors_ref.11, bf16[1024,1024]{1,0:T(8,128)(2,1)} %near_field.5.refs_2_.refs_0_, bf16[256,512]{1,0:T(8,128)(2,1)} %get-tuple-element.28.refs_1_.refs_3_), custom_call_target="tpu_custom_call" | custom-call | flops 7000000000 | bytes 1 | tf_op jit(solution)/shard_map/near_field/pallas_call | solution.py:40
  45.9 0.0 collective-permute-done.5.refs_1_
  46.0 0.0 collective-permute-done.4.refs_0_
  46.0 0.0 collective-permute-done.7.refs_3_
  46.0 0.0 collective-permute-done.6.refs_2_
  46.0 0.2 collective-permute-start.8
  46.2 2.5 %collective-permute-start.13 = (bf16[128,512]{1,0:T(8,128)(2,1)}, bf16[128,512]{1,0:T(8,128)(2,1)}, u32[]{:S(2)}, u32[]{:S(2)}) collective-permute-start(bf16[128,512]{1,0:T(8,128)(2,1)} %get-tuple-element.36.refs_0_), channel_id=1, source_target_pairs={{0,6},{1,7},{2,4},{3,5},{4,2},{5,3},{6,0},{7,1},{8,14},{9,15},{10,... | collective-permute-start | bytes 393224 | tf_op jit(solution)/shard_map/ppermute | solution.py:28
  48.6 0.0 collective-permute-start.12
  48.6 1.1 %collective-permute-start.11 = (bf16[128,512]{1,0:T(8,128)(2,1)}, bf16[128,512]{1,0:T(8,128)(2,1)}, u32[]{:S(2)}, u32[]{:S(2)}) collective-permute-start(bf16[128,512]{1,0:T(8,128)(2,1)} %get-tuple-element.36.refs_0_), channel_id=1, source_target_pairs={{0,2},{1,3},{2,0},{3,1},{4,6},{5,7},{6,4},{7,5},{8,10},{9,11},{10,... | collective-permute-start | bytes 393224 | tf_op jit(solution)/shard_map/ppermute | solution.py:28
  49.7 0.0 collective-permute-done.8.refs_1_.refs_6_
  49.7 0.0 collective-permute-done.9.refs_0_
  49.7 0.0 collective-permute-start.10
  49.7 4.5 %add_level.1.refs_4_.refs_0_ = bf16[1024,1024]{1,0:T(8,128)(2,1)} custom-call(bf16[1024,1024]{1,0:T(8,128)(2,1)} %near_field.6.refs_4_.sofar_ref, bf16[4096,128]{1,0:T(8,128)(2,1)} %own_ref.1, bf16[2,1024,128]{2,1,0:T(8,128)(2,1)} %get-tuple-element.29.refs_0_.refs_4_, bf16[2,1024,128]{2,1,0:T(8,128)(2,1)} %collective-permute-done.1.refs_2_.refs_1_.refs_5_, ...), custom_call_target="tpu_custom_call" | custom-call | flops 10000000000 | bytes 1 | tf_op jit(solution)/shard_map/add_level/pallas_call | solution.py:40
  54.3 0.0 collective-permute-done.13.refs_3_
  54.3 1.2 %collective-permute-done.12.refs_2_ = bf16[128,512]{1,0:T(8,128)(2,1)} collective-permute-done((bf16[128,512]{1,0:T(8,128)(2,1)}, bf16[128,512]{1,0:T(8,128)(2,1)}, u32[]{:S(2)}, u32[]{:S(2)}) %collective-permute-start.12) | collective-permute-done | bytes 131104 | tf_op jit(solution)/shard_map/ppermute | solution.py:28
  55.5 0.5 collective-permute-done.11.refs_1_
  56.0 0.0 collective-permute-start.14
  56.1 0.5 collective-permute-start.15
  56.5 0.0 collective-permute-start.16
  56.6 0.5 collective-permute-start.17
  57.0 0.7 %collective-permute-done.14.refs_8_ = bf16[128,512]{1,0:T(8,128)(2,1)} collective-permute-done((bf16[128,512]{1,0:T(8,128)(2,1)}, bf16[128,512]{1,0:T(8,128)(2,1)}, u32[]{:S(2)}, u32[]{:S(2)}) %collective-permute-start.14) | collective-permute-done | bytes 131104 | tf_op jit(solution)/shard_map/ppermute | solution.py:28
  57.7 0.2 collective-permute-done.15.refs_10_
  57.9 0.3 collective-permute-done.16.refs_12_
  58.2 0.2 collective-permute-done.17.refs_14_
  58.4 0.0 collective-permute-done.10.refs_2_
  58.4 7.4 %near_field.7 = bf16[1024,1024]{1,0:T(8,128)(2,1)} custom-call(s32[4,16]{1,0:T(4,128)} %cols_ref.7, bf16[4,16,256,256]{3,2,1,0:T(8,128)(2,1)} %tiles_ref.7, bf16[4096,1024]{1,0:T(8,128)(2,1)} %vectors_ref.11, bf16[1024,1024]{1,0:T(8,128)(2,1)} %add_level.1.refs_4_.refs_0_, bf16[512,1024]{1,0:T(8,128)(2,1)} %held.10.refs_7_.refs_1_, ...), custom_call_target="tpu_custom_call" | custom-call | flops 1 | bytes 1 | tf_op jit(solution)/shard_map/near_field/pallas_call | solution.py:40
  (6 shorter events, 0.0 us)
Async XLA Ops:
  5.7 13.3 %collective-permute-start = (bf16[384,512]{1,0:T(8,128)(2,1)}, bf16[384,512]{1,0:T(8,128)(2,1)}, u32[]{:S(2)}, u32[]{:S(2)}) collective-permute-start(bf16[384,512]{1,0:T(8,128)(2,1)} %get-tuple-element.24), channel_id=1, source_target_pairs={{0,4},{1,5},{2,6},{3,7},{4,0},{5,1},{6,2},{7,3},{8,12},{9,13},{10,... | collective-permute-start | bytes 1179656 | tf_op jit(solution)/shard_map/ppermute | solution.py:28
  11.5 13.8 %collective-permute-start.1 = (bf16[2,1024,128]{2,1,0:T(8,128)(2,1)}, bf16[2,1024,128]{2,1,0:T(8,128)(2,1)}, u32[]{:S(2)}, u32[]{:S(2)}) collective-permute-start(bf16[2,1024,128]{2,1,0:T(8,128)(2,1)} %get-tuple-element.25), channel_id=1, source_target_pairs={{0,2},{1,3},{2,0},{3,1},{4,6},{5,7},{6,4},{7,5},{8,10},{9,11},{10,... | collective-permute-start | bytes 1572872 | tf_op jit(solution)/shard_map/ppermute | solution.py:28
  19.0 14.1 %collective-permute-start.2 = (bf16[2,1024,128]{2,1,0:T(8,128)(2,1)}, bf16[2,1024,128]{2,1,0:T(8,128)(2,1)}, u32[]{:S(2)}, u32[]{:S(2)}) collective-permute-start(bf16[2,1024,128]{2,1,0:T(8,128)(2,1)} %get-tuple-element.26), channel_id=1, source_target_pairs={{0,1},{1,0},{2,3},{3,2},{4,5},{5,4},{6,7},{7,6},{8,9},{9,8},{10,11... | collective-permute-start | bytes 1572872 | tf_op jit(solution)/shard_map/ppermute | solution.py:28
  21.0 12.2 %collective-permute-start.3 = (bf16[384,512]{1,0:T(8,128)(2,1)}, bf16[384,512]{1,0:T(8,128)(2,1)}, u32[]{:S(2)}, u32[]{:S(2)}) collective-permute-start(bf16[384,512]{1,0:T(8,128)(2,1)} %add_convert_fusion.refs_1_.refs_0_), channel_id=1, source_target_pairs={{0,8},{1,9},{2,10},{3,11},{4,12},{5,13},{6,14},{7,15},{8,0},{9,1},... | collective-permute-start | bytes 1179656 | tf_op jit(solution)/shard_map/ppermute | solution.py:28
  22.6 27.1 %collective-permute-start.9 = (bf16[512,1024]{1,0:T(8,128)(2,1)}, bf16[512,1024]{1,0:T(8,128)(2,1)}, u32[]{:S(2)}, u32[]{:S(2)}) collective-permute-start(bf16[512,1024]{1,0:T(8,128)(2,1)} %held.9), channel_id=1, source_target_pairs={{0,5},{2,7},{4,9},{5,0},{6,11},{7,2},{8,13},{9,4},{10,15},{11,6},{... | collective-permute-start | bytes 3145736 | tf_op jit(solution)/shard_map/ppermute | solution.py:28
  24.7 21.2 %collective-permute-start.5 = (bf16[2,1024,128]{2,1,0:T(8,128)(2,1)}, bf16[2,1024,128]{2,1,0:T(8,128)(2,1)}, u32[]{:S(2)}, u32[]{:S(2)}) collective-permute-start(bf16[2,1024,128]{2,1,0:T(8,128)(2,1)} %get-tuple-element.31), channel_id=1, source_target_pairs={{0,3},{1,2},{2,1},{3,0},{4,7},{5,6},{6,5},{7,4},{8,11},{9,10},{10,... | collective-permute-start | bytes 1572872 | tf_op jit(solution)/shard_map/ppermute | solution.py:28
  35.1 10.9 %collective-permute-start.7 = (bf16[256,512]{1,0:T(8,128)(2,1)}, bf16[256,512]{1,0:T(8,128)(2,1)}, u32[]{:S(2)}, u32[]{:S(2)}) collective-permute-start(bf16[256,512]{1,0:T(8,128)(2,1)} %get-tuple-element.28.refs_1_.refs_3_), channel_id=1, source_target_pairs={{0,2},{1,3},{2,0},{3,1},{4,6},{5,7},{6,4},{7,5},{8,10},{9,11},{10,... | collective-permute-start | bytes 786440 | tf_op jit(solution)/shard_map/ppermute | solution.py:28
  36.6 9.4 %collective-permute-start.6 = (bf16[256,512]{1,0:T(8,128)(2,1)}, bf16[256,512]{1,0:T(8,128)(2,1)}, u32[]{:S(2)}, u32[]{:S(2)}) collective-permute-start(bf16[256,512]{1,0:T(8,128)(2,1)} %get-tuple-element.28.refs_1_.refs_3_), channel_id=1, source_target_pairs={{0,1},{1,0},{2,3},{3,2},{4,5},{5,4},{6,7},{7,6},{8,9},{9,8},{10,11... | collective-permute-start | bytes 786440 | tf_op jit(solution)/shard_map/ppermute | solution.py:28
  36.6 9.4 %collective-permute-start.4 = (bf16[128,512]{1,0:T(8,128)(2,1)}, bf16[128,512]{1,0:T(8,128)(2,1)}, u32[]{:S(2)}, u32[]{:S(2)}) collective-permute-start(bf16[128,512]{1,0:T(8,128)(2,1)} %get-tuple-element.30), channel_id=1, source_target_pairs={{0,16},{1,17},{2,18},{3,19},{4,20},{5,21},{6,22},{7,23},{8,24},{9,... | collective-permute-start | bytes 393224 | tf_op jit(solution)/shard_map/ppermute | solution.py:28
  46.0 3.7 %collective-permute-start.8 = (bf16[256,512]{1,0:T(8,128)(2,1)}, bf16[256,512]{1,0:T(8,128)(2,1)}, u32[]{:S(2)}, u32[]{:S(2)}) collective-permute-start(bf16[256,512]{1,0:T(8,128)(2,1)} %get-tuple-element.34.refs_5_), channel_id=1, source_target_pairs={{0,1},{1,0},{2,3},{3,2},{4,5},{5,4},{6,7},{7,6},{8,9},{9,8},{10,11... | collective-permute-start | bytes 786440 | tf_op jit(solution)/shard_map/ppermute | solution.py:28
  46.2 8.1 %collective-permute-start.13 = (bf16[128,512]{1,0:T(8,128)(2,1)}, bf16[128,512]{1,0:T(8,128)(2,1)}, u32[]{:S(2)}, u32[]{:S(2)}) collective-permute-start(bf16[128,512]{1,0:T(8,128)(2,1)} %get-tuple-element.36.refs_0_), channel_id=1, source_target_pairs={{0,6},{1,7},{2,4},{3,5},{4,2},{5,3},{6,0},{7,1},{8,14},{9,15},{10,... | collective-permute-start | bytes 393224 | tf_op jit(solution)/shard_map/ppermute | solution.py:28
  48.6 6.8 %collective-permute-start.12 = (bf16[128,512]{1,0:T(8,128)(2,1)}, bf16[128,512]{1,0:T(8,128)(2,1)}, u32[]{:S(2)}, u32[]{:S(2)}) collective-permute-start(bf16[128,512]{1,0:T(8,128)(2,1)} %get-tuple-element.36.refs_0_), channel_id=1, source_target_pairs={{0,4},{1,5},{2,6},{3,7},{4,0},{5,1},{6,2},{7,3},{8,12},{9,13},{10,... | collective-permute-start | bytes 393224 | tf_op jit(solution)/shard_map/ppermute | solution.py:28
  48.6 7.4 %collective-permute-start.11 = (bf16[128,512]{1,0:T(8,128)(2,1)}, bf16[128,512]{1,0:T(8,128)(2,1)}, u32[]{:S(2)}, u32[]{:S(2)}) collective-permute-start(bf16[128,512]{1,0:T(8,128)(2,1)} %get-tuple-element.36.refs_0_), channel_id=1, source_target_pairs={{0,2},{1,3},{2,0},{3,1},{4,6},{5,7},{6,4},{7,5},{8,10},{9,11},{10,... | collective-permute-start | bytes 393224 | tf_op jit(solution)/shard_map/ppermute | solution.py:28
  49.7 8.7 %collective-permute-start.10 = (bf16[512,1024]{1,0:T(8,128)(2,1)}, bf16[512,1024]{1,0:T(8,128)(2,1)}, u32[]{:S(2)}, u32[]{:S(2)}) collective-permute-start(bf16[512,1024]{1,0:T(8,128)(2,1)} %held.10.refs_7_.refs_1_), channel_id=1, source_target_pairs={{0,1},{1,0},{2,3},{3,2},{4,5},{5,4},{6,7},{7,6},{8,9},{9,8},{10,11... | collective-permute-start | bytes 3145736 | tf_op jit(solution)/shard_map/ppermute | solution.py:28
  56.0 1.7 %collective-permute-start.14 = (bf16[128,512]{1,0:T(8,128)(2,1)}, bf16[128,512]{1,0:T(8,128)(2,1)}, u32[]{:S(2)}, u32[]{:S(2)}) collective-permute-start(bf16[128,512]{1,0:T(8,128)(2,1)} %get-tuple-element.37.refs_7_), channel_id=1, source_target_pairs={{0,1},{1,0},{2,3},{3,2},{4,5},{5,4},{6,7},{7,6},{8,9},{9,8},{10,11... | collective-permute-start | bytes 393224 | tf_op jit(solution)/shard_map/ppermute | solution.py:28
  56.1 1.8 %collective-permute-start.15 = (bf16[128,512]{1,0:T(8,128)(2,1)}, bf16[128,512]{1,0:T(8,128)(2,1)}, u32[]{:S(2)}, u32[]{:S(2)}) collective-permute-start(bf16[128,512]{1,0:T(8,128)(2,1)} %get-tuple-element.38.refs_9_), channel_id=1, source_target_pairs={{0,1},{1,0},{2,3},{3,2},{4,5},{5,4},{6,7},{7,6},{8,9},{9,8},{10,11... | collective-permute-start | bytes 393224 | tf_op jit(solution)/shard_map/ppermute | solution.py:28
  56.5 1.7 %collective-permute-start.16 = (bf16[128,512]{1,0:T(8,128)(2,1)}, bf16[128,512]{1,0:T(8,128)(2,1)}, u32[]{:S(2)}, u32[]{:S(2)}) collective-permute-start(bf16[128,512]{1,0:T(8,128)(2,1)} %get-tuple-element.39.refs_11_), channel_id=1, source_target_pairs={{0,1},{1,0},{2,3},{3,2},{4,5},{5,4},{6,7},{7,6},{8,9},{9,8},{10,11... | collective-permute-start | bytes 393224 | tf_op jit(solution)/shard_map/ppermute | solution.py:28
  56.6 1.8 %collective-permute-start.17 = (bf16[128,512]{1,0:T(8,128)(2,1)}, bf16[128,512]{1,0:T(8,128)(2,1)}, u32[]{:S(2)}, u32[]{:S(2)}) collective-permute-start(bf16[128,512]{1,0:T(8,128)(2,1)} %get-tuple-element.40.refs_13_), channel_id=1, source_target_pairs={{0,1},{1,0},{2,3},{3,2},{4,5},{5,4},{6,7},{7,6},{8,9},{9,8},{10,11... | collective-permute-start | bytes 393224 | tf_op jit(solution)/shard_map/ppermute | solution.py:28

commit v6 on v5

--- a/solution.py
+++ b/solution.py
@@ -129,7 +129,7 @@
     )
 
 
-def near_field(near_cols, near_tiles, vectors, first, count, sofar=None, halos=(), low_rank=None, after=(), flops=1):
+def near_field(near_cols, near_tiles, vectors, first, count, sofar=None, halos=(), sides=(0, 1), low_rank=None, after=(), flops=1):
     tiles, nnz = near_cols.shape
     rows, width = tiles * B, vectors.shape[1]
     half = width // 2
@@ -140,7 +140,7 @@
     while sum(sizes) < inside:
         sizes.append(min((1, 3, 4)[min(len(sizes), 2)], inside - sum(sizes)))
     if halos:
-        sizes += [REACH, REACH]
+        sizes += [REACH] * len(halos)
     count = sum(sizes)
     near_groups = len(sizes)
     begins = [sum(sizes[:g]) * B for g in range(near_groups)] + [count * B]
@@ -173,7 +173,7 @@
                 place = first + c + REACH
             else:
                 i = c - inside
-                before = (i < REACH) == (col % 2 == 1)
+                before = (sides[i // REACH] == 0) == (col % 2 == 1)
                 place = jnp.where(before, i % REACH, window - REACH + i % REACH)
             slot = slots[t, place]
             copy = pltpu.make_async_copy(
@@ -335,64 +335,6 @@
     )
 
 
-def add_level(sofar, level, own, pieces, coeffs, after=()):
-    rows, width = sofar.shape
-    half = width // 2
-    rank = own.shape[1]
-    offsets = len(pieces) + 1
-    inner = offsets * rank
-
-    def kernel(sofar_ref, own_ref, *refs):
-        piece_refs, refs = refs[: offsets - 1], refs[offsets - 1 :]
-        coeff_refs, refs = refs[:offsets], refs[offsets + len(after) :]
-        out_ref, lefts, ranks, result, left_sems, rank_sems, sofar_sems, out_sems = refs
-        col = lax.axis_index("cols")
-        places = [pl.ds(n * half, half) for n in range(2)]
-        copies = [[], []]
-        for d in range(offsets):
-            place = pl.ds(d * rank, rank)
-            source = piece_refs[d - 1].at[level] if d else own_ref.at[span(col, rows)]
-            copies[0].append(pltpu.make_async_copy(source, lefts.at[:, place], left_sems.at[d]))
-            for n in range(2):
-                source = coeff_refs[d].at[pl.ds(n * rank, rank)]
-                copies[n].append(pltpu.make_async_copy(source, ranks.at[n, place], rank_sems.at[n, d]))
-        for n in range(2):
-            copies[n].append(
-                pltpu.make_async_copy(sofar_ref.at[:, places[n]], result.at[n], sofar_sems.at[n])
-            )
-            for copy in copies[n]:
-                copy.start()
-        outs = []
-        for n in range(2):
-            for copy in copies[n]:
-                copy.wait()
-            part = jnp.dot(lefts[...], ranks[n], preferred_element_type=jnp.float32)
-            result[n] = (result[n].astype(jnp.float32) + part).astype(jnp.bfloat16)
-            outs.append(pltpu.make_async_copy(result.at[n], out_ref.at[:, places[n]], out_sems.at[n]))
-            outs[-1].start()
-        for copy in outs:
-            copy.wait()
-
-    return called(
-        kernel,
-        "add_level",
-        [],
-        [sofar, own, *pieces, *coeffs],
-        after,
-        jax.ShapeDtypeStruct((rows, width), jnp.bfloat16),
-        [
-            pltpu.VMEM((rows, inner), jnp.bfloat16),
-            pltpu.VMEM((2, inner, half), jnp.bfloat16),
-            pltpu.VMEM((2, rows, half), jnp.bfloat16),
-            pltpu.SemaphoreType.DMA((offsets,)),
-            pltpu.SemaphoreType.DMA((2, offsets)),
-            pltpu.SemaphoreType.DMA((2,)),
-            pltpu.SemaphoreType.DMA((2,)),
-        ],
-        flops=COST_D,
-    )
-
-
 def parted(a, b, top):
     rows, width = b.shape
 
@@ -506,10 +448,12 @@
     coeffs_two = [two, beside] + [x for there in rest for x in (there, flipped(there, 0, 1))]
     (halo,) = held([halo], coeffs_two[-1:])
     halos = (halo, flipped(halo, 0, 1))
-    near = add_level(near, 1, left_two, pieces, coeffs_two, after=(halo,))
+    near = near_field(
+        *near_args, 0, 0, near, halos[:1], (0,), (1, left_two, pieces, coeffs_two), flops=COST_D
+    )
     ones = list(held(ones, [near]))
     coeffs_one = [x for there in ones for x in (there, flipped(there, 0, 1))]
-    return near_field(*near_args, 0, 0, near, halos, (0, left_one, pieces, coeffs_one))
+    return near_field(*near_args, 0, 0, near, halos[1:], (1,), (0, left_one, pieces, coeffs_one))
 
 
 def solution(mesh):

time: 66.7 us -> 66 us (0.990)
  waiting for transfers between devices: 3.81 us -> 2.37 us
    ppermute x18, waiting for transfers between devices: 3.81 us -> 2.37 us  [moved(): return lax.ppermute(value, AXES, pairs)]
  transfers between devices with their start and end apart: 18 -> 18, of which waited for: 8 -> 7; matrix products, arithmetic and copies ran while one was open for 3% -> 3% of each run, Pallas kernels for 45% -> 48%
where the time goes in v6:
time: 66 us; the launch traced here: 65.2 us
  Pallas kernels  43 us (65%)
  starting transfers between devices  17.6 us (27%)
  waiting for transfers between devices  2.37 us (4%)
  other arithmetic  1.96 us (3%)
    pallas_call x14, Pallas kernels, called(): pl.pallas_call(kernel, out_shape=out_shape, in_specs=[SMEM] * len(smem) +...  43 us
    ppermute x18, starting transfers between devices, moved(): return lax.ppermute(value, AXES, pairs)  17.6 us
    ppermute x18, waiting for transfers between devices, moved(): return lax.ppermute(value, AXES, pairs)  2.37 us
    convert_element_type x1, other arithmetic, summed(): return (a.astype(jnp.float32) + b.astype(jnp.float32)).astype(jnp.bfloat16)  1.96 us
  transfers between devices with their start and end apart: 18, of which 7 were waited for; matrix products, arithmetic and copies ran while one was open for 3% of the time, Pallas kernels for 48%

profile of v6, /device:TPU:0, one launch (start us, length us, event | category | flops | bytes accessed | tf_op | source)
XLA Modules:
  0.0 65.2 jit_solution(5888503545936480166)
XLA Ops:
  0.0 5.7 %project.1 = (bf16[384,512]{1,0:T(8,128)(2,1)}, bf16[384,512]{1,0:T(8,128)(2,1)}) custom-call(bf16[4096,128]{1,0:T(8,128)(2,1)} %one_ref.2, bf16[4096,128]{1,0:T(8,128)(2,1)} %two_ref.2, bf16[4096,1024]{1,0:T(8,128)(2,1)} %vectors_ref.13), custom_call_target="tpu_custom_call" | custom-call | flops 1 | bytes 1 | tf_op jit(solution)/shard_map/project/pallas_call | solution.py:40
  5.7 3.0 %collective-permute-start = (bf16[384,512]{1,0:T(8,128)(2,1)}, bf16[384,512]{1,0:T(8,128)(2,1)}, u32[]{:S(2)}, u32[]{:S(2)}) collective-permute-start(bf16[384,512]{1,0:T(8,128)(2,1)} %get-tuple-element.24), channel_id=1, source_target_pairs={{0,4},{1,5},{2,6},{3,7},{4,0},{5,1},{6,2},{7,3},{8,12},{9,13},{10,... | collective-permute-start | bytes 1179656 | tf_op jit(solution)/shard_map/ppermute | solution.py:28
  8.7 2.8 %packed.1 = (bf16[512,1024]{1,0:T(8,128)(2,1)}, bf16[2,1024,128]{2,1,0:T(8,128)(2,1)}, bf16[2,1024,128]{2,1,0:T(8,128)(2,1)}, bf16[2,1024,128]{2,1,0:T(8,128)(2,1)}) custom-call(bf16[4096,1024]{1,0:T(8,128)(2,1)} %vectors_ref.13, bf16[4096,128]{1,0:T(8,128)(2,1)} %refs_2_.3, bf16[4096,128]{1,0:T(8,128)(2,1)} %refs_2_.2, ...), custom_call_target="tpu_custom_call" | custom-call | flops 1 | bytes 1 | tf_op jit(solution)/shard_map/packed/pallas_call | solution.py:40
  11.5 1.6 %collective-permute-start.1 = (bf16[2,1024,128]{2,1,0:T(8,128)(2,1)}, bf16[2,1024,128]{2,1,0:T(8,128)(2,1)}, u32[]{:S(2)}, u32[]{:S(2)}) collective-permute-start(bf16[2,1024,128]{2,1,0:T(8,128)(2,1)} %get-tuple-element.25), channel_id=1, source_target_pairs={{0,2},{1,3},{2,0},{3,1},{4,6},{5,7},{6,4},{7,5},{8,10},{9,11},{10,... | collective-permute-start | bytes 1572872 | tf_op jit(solution)/shard_map/ppermute | solution.py:28
  13.1 5.8 %near_field.5.refs_1_.refs_0_ = bf16[1024,1024]{1,0:T(8,128)(2,1)} custom-call(s32[4,16]{1,0:T(4,128)} %cols_ref.9, bf16[4,16,256,256]{3,2,1,0:T(8,128)(2,1)} %tiles_ref.9, bf16[4096,1024]{1,0:T(8,128)(2,1)} %vectors_ref.13, bf16[384,512]{1,0:T(8,128)(2,1)} %get-tuple-element.23.refs_0_), custom_call_target="tpu_custom_call" | custom-call | flops 1 | bytes 1 | tf_op jit(solution)/shard_map/near_field/pallas_call | solution.py:40
  18.9 0.1 collective-permute-start.2
  19.0 0.0 collective-permute-done
  19.0 2.0 %add_convert_fusion.refs_1_.refs_0_ = bf16[384,512]{1,0:T(8,128)(2,1)} fusion(bf16[384,512]{1,0:T(8,128)(2,1)} %collective-permute-done, bf16[384,512]{1,0:T(8,128)(2,1)} %held.6), kind=kLoop, calls=%fused_computation | loop fusion | flops 786432 | bytes 1179648 | tf_op jit(solution)/shard_map/convert_element_type | solution.py:415
  21.0 1.6 %collective-permute-start.3 = (bf16[384,512]{1,0:T(8,128)(2,1)}, bf16[384,512]{1,0:T(8,128)(2,1)}, u32[]{:S(2)}, u32[]{:S(2)}) collective-permute-start(bf16[384,512]{1,0:T(8,128)(2,1)} %add_convert_fusion.refs_1_.refs_0_), channel_id=1, source_target_pairs={{0,8},{1,9},{2,10},{3,11},{4,12},{5,13},{6,14},{7,15},{8,0},{9,1},... | collective-permute-start | bytes 1179656 | tf_op jit(solution)/shard_map/ppermute | solution.py:28
  22.6 2.1 %collective-permute-start.4 = (bf16[512,1024]{1,0:T(8,128)(2,1)}, bf16[512,1024]{1,0:T(8,128)(2,1)}, u32[]{:S(2)}, u32[]{:S(2)}) collective-permute-start(bf16[512,1024]{1,0:T(8,128)(2,1)} %held.8), channel_id=1, source_target_pairs={{0,5},{2,7},{4,9},{5,0},{6,11},{7,2},{8,13},{9,4},{10,15},{11,6},{... | collective-permute-start | bytes 3145736 | tf_op jit(solution)/shard_map/ppermute | solution.py:28
  24.7 0.1 collective-permute-start.6
  24.8 0.5 collective-permute-done.1.refs_2_.refs_4_
  25.3 7.9 %near_field.6.refs_2_.refs_0_ = bf16[1024,1024]{1,0:T(8,128)(2,1)} custom-call(s32[4,16]{1,0:T(4,128)} %cols_ref.9, bf16[4,16,256,256]{3,2,1,0:T(8,128)(2,1)} %tiles_ref.9, bf16[4096,1024]{1,0:T(8,128)(2,1)} %vectors_ref.13, bf16[1024,1024]{1,0:T(8,128)(2,1)} %near_field.5.refs_1_.refs_0_, bf16[384,512]{1,0:T(8,128)(2,1)} %add_convert_fusion.refs_1_.refs_0_, ...), custom_call_target="tpu_custom_call" | custom-call | flops 1 | bytes 1 | tf_op jit(solution)/shard_map/near_field/pallas_call | solution.py:40
  33.2 0.0 collective-permute-done.2.refs_1_
  33.2 0.1 collective-permute-done.3.b_ref
  33.2 1.8 %parted.1 = (bf16[128,512]{1,0:T(8,128)(2,1)}, bf16[256,512]{1,0:T(8,128)(2,1)}) custom-call(bf16[384,512]{1,0:T(8,128)(2,1)} %get-tuple-element.27.a_ref, bf16[384,512]{1,0:T(8,128)(2,1)} %collective-permute-done.3.b_ref), custom_call_target="tpu_custom_call" | custom-call | flops 1 | bytes 1 | tf_op jit(solution)/shard_map/parted/pallas_call | solution.py:40
  35.0 0.3 collective-permute-start.7
  35.4 1.4 %collective-permute-start.8 = (bf16[256,512]{1,0:T(8,128)(2,1)}, bf16[256,512]{1,0:T(8,128)(2,1)}, u32[]{:S(2)}, u32[]{:S(2)}) collective-permute-start(bf16[256,512]{1,0:T(8,128)(2,1)} %get-tuple-element.28.refs_1_.refs_6_), channel_id=1, source_target_pairs={{0,2},{1,3},{2,0},{3,1},{4,6},{5,7},{6,4},{7,5},{8,10},{9,11},{10,... | collective-permute-start | bytes 786440 | tf_op jit(solution)/shard_map/ppermute | solution.py:28
  36.8 2.7 %collective-permute-start.5 = (bf16[128,512]{1,0:T(8,128)(2,1)}, bf16[128,512]{1,0:T(8,128)(2,1)}, u32[]{:S(2)}, u32[]{:S(2)}) collective-permute-start(bf16[128,512]{1,0:T(8,128)(2,1)} %get-tuple-element.30), channel_id=1, source_target_pairs={{0,16},{1,17},{2,18},{3,19},{4,20},{5,21},{6,22},{7,23},{8,24},{9,... | collective-permute-start | bytes 393224 | tf_op jit(solution)/shard_map/ppermute | solution.py:28
  39.5 6.5 %near_field.7.refs_4_.refs_0_ = bf16[1024,1024]{1,0:T(8,128)(2,1)} custom-call(s32[4,16]{1,0:T(4,128)} %cols_ref.9, bf16[4,16,256,256]{3,2,1,0:T(8,128)(2,1)} %tiles_ref.9, bf16[4096,1024]{1,0:T(8,128)(2,1)} %vectors_ref.13, bf16[1024,1024]{1,0:T(8,128)(2,1)} %near_field.6.refs_2_.refs_0_, bf16[256,512]{1,0:T(8,128)(2,1)} %get-tuple-element.28.refs_1_.refs_6_), custom_call_target="tpu_custom_call" | custom-call | flops 7000000000 | bytes 1 | tf_op jit(solution)/shard_map/near_field/pallas_call | solution.py:40
  46.0 0.0 collective-permute-done.6.refs_1_
  46.1 0.0 collective-permute-done.5.refs_0_
  46.1 0.0 collective-permute-done.7.refs_2_
  46.1 0.0 collective-permute-done.8.refs_3_
  46.1 0.1 collective-permute-start.9
  46.2 0.6 collective-permute-start.11
  46.7 2.1 %collective-permute-start.12 = (bf16[128,512]{1,0:T(8,128)(2,1)}, bf16[128,512]{1,0:T(8,128)(2,1)}, u32[]{:S(2)}, u32[]{:S(2)}) collective-permute-start(bf16[128,512]{1,0:T(8,128)(2,1)} %get-tuple-element.36.refs_0_), channel_id=1, source_target_pairs={{0,4},{1,5},{2,6},{3,7},{4,0},{5,1},{6,2},{7,3},{8,12},{9,13},{10,... | collective-permute-start | bytes 393224 | tf_op jit(solution)/shard_map/ppermute | solution.py:28
  48.9 0.8 %collective-permute-start.13 = (bf16[128,512]{1,0:T(8,128)(2,1)}, bf16[128,512]{1,0:T(8,128)(2,1)}, u32[]{:S(2)}, u32[]{:S(2)}) collective-permute-start(bf16[128,512]{1,0:T(8,128)(2,1)} %get-tuple-element.36.refs_0_), channel_id=1, source_target_pairs={{0,6},{1,7},{2,4},{3,5},{4,2},{5,3},{6,0},{7,1},{8,14},{9,15},{10,... | collective-permute-start | bytes 393224 | tf_op jit(solution)/shard_map/ppermute | solution.py:28
  49.7 0.0 collective-permute-done.9.refs_1_.refs_9_
  49.7 0.0 collective-permute-done.4.refs_0_
  49.7 0.0 collective-permute-start.10
  49.7 6.3 %near_field.8.refs_4_.refs_0_ = bf16[1024,1024]{1,0:T(8,128)(2,1)} custom-call(s32[4,16]{1,0:T(4,128)} %cols_ref.9, bf16[4,16,256,256]{3,2,1,0:T(8,128)(2,1)} %tiles_ref.9, bf16[4096,1024]{1,0:T(8,128)(2,1)} %vectors_ref.13, bf16[1024,1024]{1,0:T(8,128)(2,1)} %near_field.7.refs_4_.refs_0_, bf16[512,1024]{1,0:T(8,128)(2,1)} %held.10.refs_1_, ...), custom_call_target="tpu_custom_call" | custom-call | flops 10000000000 | bytes 1 | tf_op jit(solution)/shard_map/near_field/pallas_call | solution.py:40
  56.0 0.0 collective-permute-done.11.refs_1_
  56.0 0.0 collective-permute-done.12.refs_2_
  56.0 0.5 collective-permute-done.13.refs_3_
  56.5 0.1 collective-permute-start.14
  56.6 0.4 collective-permute-start.15
  57.0 0.1 collective-permute-start.16
  57.1 0.4 collective-permute-start.17
  57.5 0.7 %collective-permute-done.14.refs_7_ = bf16[128,512]{1,0:T(8,128)(2,1)} collective-permute-done((bf16[128,512]{1,0:T(8,128)(2,1)}, bf16[128,512]{1,0:T(8,128)(2,1)}, u32[]{:S(2)}, u32[]{:S(2)}) %collective-permute-start.14) | collective-permute-done | bytes 131104 | tf_op jit(solution)/shard_map/ppermute | solution.py:28
  58.2 0.2 collective-permute-done.15.refs_9_
  58.4 0.3 collective-permute-done.16.refs_11_
  58.7 0.2 collective-permute-done.17.refs_13_
  58.9 0.0 collective-permute-done.10.refs_1_
  58.9 6.2 %near_field.9 = bf16[1024,1024]{1,0:T(8,128)(2,1)} custom-call(s32[4,16]{1,0:T(4,128)} %cols_ref.9, bf16[4,16,256,256]{3,2,1,0:T(8,128)(2,1)} %tiles_ref.9, bf16[4096,1024]{1,0:T(8,128)(2,1)} %vectors_ref.13, bf16[1024,1024]{1,0:T(8,128)(2,1)} %near_field.8.refs_4_.refs_0_, bf16[512,1024]{1,0:T(8,128)(2,1)} %collective-permute-done.10.refs_1_, ...), custom_call_target="tpu_custom_call" | custom-call | flops 1 | bytes 1 | tf_op jit(solution)/shard_map/near_field/pallas_call | solution.py:40
  (6 shorter events, 0.0 us)
Async XLA Ops:
  5.7 13.3 %collective-permute-start = (bf16[384,512]{1,0:T(8,128)(2,1)}, bf16[384,512]{1,0:T(8,128)(2,1)}, u32[]{:S(2)}, u32[]{:S(2)}) collective-permute-start(bf16[384,512]{1,0:T(8,128)(2,1)} %get-tuple-element.24), channel_id=1, source_target_pairs={{0,4},{1,5},{2,6},{3,7},{4,0},{5,1},{6,2},{7,3},{8,12},{9,13},{10,... | collective-permute-start | bytes 1179656 | tf_op jit(solution)/shard_map/ppermute | solution.py:28
  11.5 13.8 %collective-permute-start.1 = (bf16[2,1024,128]{2,1,0:T(8,128)(2,1)}, bf16[2,1024,128]{2,1,0:T(8,128)(2,1)}, u32[]{:S(2)}, u32[]{:S(2)}) collective-permute-start(bf16[2,1024,128]{2,1,0:T(8,128)(2,1)} %get-tuple-element.25), channel_id=1, source_target_pairs={{0,2},{1,3},{2,0},{3,1},{4,6},{5,7},{6,4},{7,5},{8,10},{9,11},{10,... | collective-permute-start | bytes 1572872 | tf_op jit(solution)/shard_map/ppermute | solution.py:28
  18.9 14.2 %collective-permute-start.2 = (bf16[2,1024,128]{2,1,0:T(8,128)(2,1)}, bf16[2,1024,128]{2,1,0:T(8,128)(2,1)}, u32[]{:S(2)}, u32[]{:S(2)}) collective-permute-start(bf16[2,1024,128]{2,1,0:T(8,128)(2,1)} %get-tuple-element.26), channel_id=1, source_target_pairs={{0,1},{1,0},{2,3},{3,2},{4,5},{5,4},{6,7},{7,6},{8,9},{9,8},{10,11... | collective-permute-start | bytes 1572872 | tf_op jit(solution)/shard_map/ppermute | solution.py:28
  21.0 12.2 %collective-permute-start.3 = (bf16[384,512]{1,0:T(8,128)(2,1)}, bf16[384,512]{1,0:T(8,128)(2,1)}, u32[]{:S(2)}, u32[]{:S(2)}) collective-permute-start(bf16[384,512]{1,0:T(8,128)(2,1)} %add_convert_fusion.refs_1_.refs_0_), channel_id=1, source_target_pairs={{0,8},{1,9},{2,10},{3,11},{4,12},{5,13},{6,14},{7,15},{8,0},{9,1},... | collective-permute-start | bytes 1179656 | tf_op jit(solution)/shard_map/ppermute | solution.py:28
  22.6 27.1 %collective-permute-start.4 = (bf16[512,1024]{1,0:T(8,128)(2,1)}, bf16[512,1024]{1,0:T(8,128)(2,1)}, u32[]{:S(2)}, u32[]{:S(2)}) collective-permute-start(bf16[512,1024]{1,0:T(8,128)(2,1)} %held.8), channel_id=1, source_target_pairs={{0,5},{2,7},{4,9},{5,0},{6,11},{7,2},{8,13},{9,4},{10,15},{11,6},{... | collective-permute-start | bytes 3145736 | tf_op jit(solution)/shard_map/ppermute | solution.py:28
  24.7 21.3 %collective-permute-start.6 = (bf16[2,1024,128]{2,1,0:T(8,128)(2,1)}, bf16[2,1024,128]{2,1,0:T(8,128)(2,1)}, u32[]{:S(2)}, u32[]{:S(2)}) collective-permute-start(bf16[2,1024,128]{2,1,0:T(8,128)(2,1)} %get-tuple-element.31), channel_id=1, source_target_pairs={{0,3},{1,2},{2,1},{3,0},{4,7},{5,6},{6,5},{7,4},{8,11},{9,10},{10,... | collective-permute-start | bytes 1572872 | tf_op jit(solution)/shard_map/ppermute | solution.py:28
  35.0 11.0 %collective-permute-start.7 = (bf16[256,512]{1,0:T(8,128)(2,1)}, bf16[256,512]{1,0:T(8,128)(2,1)}, u32[]{:S(2)}, u32[]{:S(2)}) collective-permute-start(bf16[256,512]{1,0:T(8,128)(2,1)} %get-tuple-element.28.refs_1_.refs_6_), channel_id=1, source_target_pairs={{0,1},{1,0},{2,3},{3,2},{4,5},{5,4},{6,7},{7,6},{8,9},{9,8},{10,11... | collective-permute-start | bytes 786440 | tf_op jit(solution)/shard_map/ppermute | solution.py:28
  35.4 10.7 %collective-permute-start.8 = (bf16[256,512]{1,0:T(8,128)(2,1)}, bf16[256,512]{1,0:T(8,128)(2,1)}, u32[]{:S(2)}, u32[]{:S(2)}) collective-permute-start(bf16[256,512]{1,0:T(8,128)(2,1)} %get-tuple-element.28.refs_1_.refs_6_), channel_id=1, source_target_pairs={{0,2},{1,3},{2,0},{3,1},{4,6},{5,7},{6,4},{7,5},{8,10},{9,11},{10,... | collective-permute-start | bytes 786440 | tf_op jit(solution)/shard_map/ppermute | solution.py:28
  36.8 9.3 %collective-permute-start.5 = (bf16[128,512]{1,0:T(8,128)(2,1)}, bf16[128,512]{1,0:T(8,128)(2,1)}, u32[]{:S(2)}, u32[]{:S(2)}) collective-permute-start(bf16[128,512]{1,0:T(8,128)(2,1)} %get-tuple-element.30), channel_id=1, source_target_pairs={{0,16},{1,17},{2,18},{3,19},{4,20},{5,21},{6,22},{7,23},{8,24},{9,... | collective-permute-start | bytes 393224 | tf_op jit(solution)/shard_map/ppermute | solution.py:28
  46.1 3.6 %collective-permute-start.9 = (bf16[256,512]{1,0:T(8,128)(2,1)}, bf16[256,512]{1,0:T(8,128)(2,1)}, u32[]{:S(2)}, u32[]{:S(2)}) collective-permute-start(bf16[256,512]{1,0:T(8,128)(2,1)} %get-tuple-element.32.refs_8_), channel_id=1, source_target_pairs={{0,1},{1,0},{2,3},{3,2},{4,5},{5,4},{6,7},{7,6},{8,9},{9,8},{10,11... | collective-permute-start | bytes 786440 | tf_op jit(solution)/shard_map/ppermute | solution.py:28
  46.2 9.8 %collective-permute-start.11 = (bf16[128,512]{1,0:T(8,128)(2,1)}, bf16[128,512]{1,0:T(8,128)(2,1)}, u32[]{:S(2)}, u32[]{:S(2)}) collective-permute-start(bf16[128,512]{1,0:T(8,128)(2,1)} %get-tuple-element.36.refs_0_), channel_id=1, source_target_pairs={{0,2},{1,3},{2,0},{3,1},{4,6},{5,7},{6,4},{7,5},{8,10},{9,11},{10,... | collective-permute-start | bytes 393224 | tf_op jit(solution)/shard_map/ppermute | solution.py:28
  46.7 9.3 %collective-permute-start.12 = (bf16[128,512]{1,0:T(8,128)(2,1)}, bf16[128,512]{1,0:T(8,128)(2,1)}, u32[]{:S(2)}, u32[]{:S(2)}) collective-permute-start(bf16[128,512]{1,0:T(8,128)(2,1)} %get-tuple-element.36.refs_0_), channel_id=1, source_target_pairs={{0,4},{1,5},{2,6},{3,7},{4,0},{5,1},{6,2},{7,3},{8,12},{9,13},{10,... | collective-permute-start | bytes 393224 | tf_op jit(solution)/shard_map/ppermute | solution.py:28
  48.9 7.6 %collective-permute-start.13 = (bf16[128,512]{1,0:T(8,128)(2,1)}, bf16[128,512]{1,0:T(8,128)(2,1)}, u32[]{:S(2)}, u32[]{:S(2)}) collective-permute-start(bf16[128,512]{1,0:T(8,128)(2,1)} %get-tuple-element.36.refs_0_), channel_id=1, source_target_pairs={{0,6},{1,7},{2,4},{3,5},{4,2},{5,3},{6,0},{7,1},{8,14},{9,15},{10,... | collective-permute-start | bytes 393224 | tf_op jit(solution)/shard_map/ppermute | solution.py:28
  49.7 9.2 %collective-permute-start.10 = (bf16[512,1024]{1,0:T(8,128)(2,1)}, bf16[512,1024]{1,0:T(8,128)(2,1)}, u32[]{:S(2)}, u32[]{:S(2)}) collective-permute-start(bf16[512,1024]{1,0:T(8,128)(2,1)} %held.10.refs_1_), channel_id=1, source_target_pairs={{0,1},{1,0},{2,3},{3,2},{4,5},{5,4},{6,7},{7,6},{8,9},{9,8},{10,11... | collective-permute-start | bytes 3145736 | tf_op jit(solution)/shard_map/ppermute | solution.py:28
  56.5 1.7 %collective-permute-start.14 = (bf16[128,512]{1,0:T(8,128)(2,1)}, bf16[128,512]{1,0:T(8,128)(2,1)}, u32[]{:S(2)}, u32[]{:S(2)}) collective-permute-start(bf16[128,512]{1,0:T(8,128)(2,1)} %get-tuple-element.37.refs_6_), channel_id=1, source_target_pairs={{0,1},{1,0},{2,3},{3,2},{4,5},{5,4},{6,7},{7,6},{8,9},{9,8},{10,11... | collective-permute-start | bytes 393224 | tf_op jit(solution)/shard_map/ppermute | solution.py:28
  56.6 1.8 %collective-permute-start.15 = (bf16[128,512]{1,0:T(8,128)(2,1)}, bf16[128,512]{1,0:T(8,128)(2,1)}, u32[]{:S(2)}, u32[]{:S(2)}) collective-permute-start(bf16[128,512]{1,0:T(8,128)(2,1)} %get-tuple-element.38.refs_8_), channel_id=1, source_target_pairs={{0,1},{1,0},{2,3},{3,2},{4,5},{5,4},{6,7},{7,6},{8,9},{9,8},{10,11... | collective-permute-start | bytes 393224 | tf_op jit(solution)/shard_map/ppermute | solution.py:28
  57.0 1.7 %collective-permute-start.16 = (bf16[128,512]{1,0:T(8,128)(2,1)}, bf16[128,512]{1,0:T(8,128)(2,1)}, u32[]{:S(2)}, u32[]{:S(2)}) collective-permute-start(bf16[128,512]{1,0:T(8,128)(2,1)} %get-tuple-element.39.refs_10_), channel_id=1, source_target_pairs={{0,1},{1,0},{2,3},{3,2},{4,5},{5,4},{6,7},{7,6},{8,9},{9,8},{10,11... | collective-permute-start | bytes 393224 | tf_op jit(solution)/shard_map/ppermute | solution.py:28
  57.1 1.8 %collective-permute-start.17 = (bf16[128,512]{1,0:T(8,128)(2,1)}, bf16[128,512]{1,0:T(8,128)(2,1)}, u32[]{:S(2)}, u32[]{:S(2)}) collective-permute-start(bf16[128,512]{1,0:T(8,128)(2,1)} %get-tuple-element.40.refs_12_), channel_id=1, source_target_pairs={{0,1},{1,0},{2,3},{3,2},{4,5},{5,4},{6,7},{7,6},{8,9},{9,8},{10,11... | collective-permute-start | bytes 393224 | tf_op jit(solution)/shard_map/ppermute | solution.py:28

commit v7 on v6

--- a/solution.py
+++ b/solution.py
@@ -405,7 +405,7 @@
     inside = depth // B
 
     near_args = (near_cols, near_tiles, vectors)
-    cuts = [0, inside // 4, 11 * inside // 16, inside]
+    cuts = [0, inside // 4, 5 * inside // 8, inside]
 
     def near_part(part, sofar, after, flops):
         first, last = cuts[part : part + 2]

time: 66 us -> 66 us (level)
  starting transfers between devices: 17.6 us -> 16.9 us
    ppermute x18, starting transfers between devices: 17.6 us -> 16.9 us  [moved(): return lax.ppermute(value, AXES, pairs)]
where the time goes in v7:
time: 66 us; the launch traced here: 65.2 us
  Pallas kernels  43.1 us (65%)
  starting transfers between devices  16.9 us (26%)
  waiting for transfers between devices  2.89 us (4%)
  other arithmetic  1.96 us (3%)
    pallas_call x14, Pallas kernels, called(): pl.pallas_call(kernel, out_shape=out_shape, in_specs=[SMEM] * len(smem) +...  43.1 us
    ppermute x18, starting transfers between devices, moved(): return lax.ppermute(value, AXES, pairs)  16.9 us
    ppermute x18, waiting for transfers between devices, moved(): return lax.ppermute(value, AXES, pairs)  2.89 us
    convert_element_type x1, other arithmetic, summed(): return (a.astype(jnp.float32) + b.astype(jnp.float32)).astype(jnp.bfloat16)  1.96 us
  transfers between devices with their start and end apart: 18, of which 7 were waited for; matrix products, arithmetic and copies ran while one was open for 3% of the time, Pallas kernels for 48%

profile of v7, /device:TPU:0, one launch (start us, length us, event | category | flops | bytes accessed | tf_op | source)
XLA Modules:
  0.0 65.2 jit_solution(434199703533205377)
XLA Ops:
  0.0 5.7 %project.1 = (bf16[384,512]{1,0:T(8,128)(2,1)}, bf16[384,512]{1,0:T(8,128)(2,1)}) custom-call(bf16[4096,128]{1,0:T(8,128)(2,1)} %one_ref.2, bf16[4096,128]{1,0:T(8,128)(2,1)} %two_ref.2, bf16[4096,1024]{1,0:T(8,128)(2,1)} %vectors_ref.13), custom_call_target="tpu_custom_call" | custom-call | flops 1 | bytes 1 | tf_op jit(solution)/shard_map/project/pallas_call | solution.py:40
  5.7 3.0 %collective-permute-start = (bf16[384,512]{1,0:T(8,128)(2,1)}, bf16[384,512]{1,0:T(8,128)(2,1)}, u32[]{:S(2)}, u32[]{:S(2)}) collective-permute-start(bf16[384,512]{1,0:T(8,128)(2,1)} %get-tuple-element.24), channel_id=1, source_target_pairs={{0,4},{1,5},{2,6},{3,7},{4,0},{5,1},{6,2},{7,3},{8,12},{9,13},{10,... | collective-permute-start | bytes 1179656 | tf_op jit(solution)/shard_map/ppermute | solution.py:28
  8.7 2.8 %packed.1 = (bf16[512,1024]{1,0:T(8,128)(2,1)}, bf16[2,1024,128]{2,1,0:T(8,128)(2,1)}, bf16[2,1024,128]{2,1,0:T(8,128)(2,1)}, bf16[2,1024,128]{2,1,0:T(8,128)(2,1)}) custom-call(bf16[4096,1024]{1,0:T(8,128)(2,1)} %vectors_ref.13, bf16[4096,128]{1,0:T(8,128)(2,1)} %refs_2_.3, bf16[4096,128]{1,0:T(8,128)(2,1)} %refs_2_.2, ...), custom_call_target="tpu_custom_call" | custom-call | flops 1 | bytes 1 | tf_op jit(solution)/shard_map/packed/pallas_call | solution.py:40
  11.5 1.6 %collective-permute-start.1 = (bf16[2,1024,128]{2,1,0:T(8,128)(2,1)}, bf16[2,1024,128]{2,1,0:T(8,128)(2,1)}, u32[]{:S(2)}, u32[]{:S(2)}) collective-permute-start(bf16[2,1024,128]{2,1,0:T(8,128)(2,1)} %get-tuple-element.25), channel_id=1, source_target_pairs={{0,2},{1,3},{2,0},{3,1},{4,6},{5,7},{6,4},{7,5},{8,10},{9,11},{10,... | collective-permute-start | bytes 1572872 | tf_op jit(solution)/shard_map/ppermute | solution.py:28
  13.1 5.9 %near_field.5.refs_1_.refs_0_ = bf16[1024,1024]{1,0:T(8,128)(2,1)} custom-call(s32[4,16]{1,0:T(4,128)} %cols_ref.9, bf16[4,16,256,256]{3,2,1,0:T(8,128)(2,1)} %tiles_ref.9, bf16[4096,1024]{1,0:T(8,128)(2,1)} %vectors_ref.13, bf16[384,512]{1,0:T(8,128)(2,1)} %get-tuple-element.23.refs_0_), custom_call_target="tpu_custom_call" | custom-call | flops 1 | bytes 1 | tf_op jit(solution)/shard_map/near_field/pallas_call | solution.py:40
  19.0 0.1 collective-permute-start.2
  19.1 0.0 collective-permute-done
  19.1 2.0 %add_convert_fusion.refs_1_.refs_0_ = bf16[384,512]{1,0:T(8,128)(2,1)} fusion(bf16[384,512]{1,0:T(8,128)(2,1)} %collective-permute-done, bf16[384,512]{1,0:T(8,128)(2,1)} %held.6), kind=kLoop, calls=%fused_computation | loop fusion | flops 786432 | bytes 1179648 | tf_op jit(solution)/shard_map/convert_element_type | solution.py:415
  21.1 1.5 %collective-permute-start.3 = (bf16[384,512]{1,0:T(8,128)(2,1)}, bf16[384,512]{1,0:T(8,128)(2,1)}, u32[]{:S(2)}, u32[]{:S(2)}) collective-permute-start(bf16[384,512]{1,0:T(8,128)(2,1)} %add_convert_fusion.refs_1_.refs_0_), channel_id=1, source_target_pairs={{0,8},{1,9},{2,10},{3,11},{4,12},{5,13},{6,14},{7,15},{8,0},{9,1},... | collective-permute-start | bytes 1179656 | tf_op jit(solution)/shard_map/ppermute | solution.py:28
  22.5 2.2 %collective-permute-start.4 = (bf16[512,1024]{1,0:T(8,128)(2,1)}, bf16[512,1024]{1,0:T(8,128)(2,1)}, u32[]{:S(2)}, u32[]{:S(2)}) collective-permute-start(bf16[512,1024]{1,0:T(8,128)(2,1)} %held.8), channel_id=1, source_target_pairs={{0,5},{2,7},{4,9},{5,0},{6,11},{7,2},{8,13},{9,4},{10,15},{11,6},{... | collective-permute-start | bytes 3145736 | tf_op jit(solution)/shard_map/ppermute | solution.py:28
  24.7 0.1 collective-permute-start.6
  24.8 0.5 collective-permute-done.1.refs_2_.refs_4_
  25.3 7.4 %near_field.6.refs_2_.refs_0_ = bf16[1024,1024]{1,0:T(8,128)(2,1)} custom-call(s32[4,16]{1,0:T(4,128)} %cols_ref.9, bf16[4,16,256,256]{3,2,1,0:T(8,128)(2,1)} %tiles_ref.9, bf16[4096,1024]{1,0:T(8,128)(2,1)} %vectors_ref.13, bf16[1024,1024]{1,0:T(8,128)(2,1)} %near_field.5.refs_1_.refs_0_, bf16[384,512]{1,0:T(8,128)(2,1)} %add_convert_fusion.refs_1_.refs_0_, ...), custom_call_target="tpu_custom_call" | custom-call | flops 1 | bytes 1 | tf_op jit(solution)/shard_map/near_field/pallas_call | solution.py:40
  32.7 0.0 collective-permute-done.2.refs_1_
  32.7 0.6 collective-permute-done.3.b_ref
  33.3 1.8 %parted.1 = (bf16[128,512]{1,0:T(8,128)(2,1)}, bf16[256,512]{1,0:T(8,128)(2,1)}) custom-call(bf16[384,512]{1,0:T(8,128)(2,1)} %get-tuple-element.27.a_ref, bf16[384,512]{1,0:T(8,128)(2,1)} %collective-permute-done.3.b_ref), custom_call_target="tpu_custom_call" | custom-call | flops 1 | bytes 1 | tf_op jit(solution)/shard_map/parted/pallas_call | solution.py:40
  35.1 0.1 collective-permute-start.7
  35.2 1.0 %collective-permute-start.8 = (bf16[256,512]{1,0:T(8,128)(2,1)}, bf16[256,512]{1,0:T(8,128)(2,1)}, u32[]{:S(2)}, u32[]{:S(2)}) collective-permute-start(bf16[256,512]{1,0:T(8,128)(2,1)} %get-tuple-element.28.refs_1_.refs_6_), channel_id=1, source_target_pairs={{0,2},{1,3},{2,0},{3,1},{4,6},{5,7},{6,4},{7,5},{8,10},{9,11},{10,... | collective-permute-start | bytes 786440 | tf_op jit(solution)/shard_map/ppermute | solution.py:28
  36.2 2.8 %collective-permute-start.5 = (bf16[128,512]{1,0:T(8,128)(2,1)}, bf16[128,512]{1,0:T(8,128)(2,1)}, u32[]{:S(2)}, u32[]{:S(2)}) collective-permute-start(bf16[128,512]{1,0:T(8,128)(2,1)} %get-tuple-element.30), channel_id=1, source_target_pairs={{0,16},{1,17},{2,18},{3,19},{4,20},{5,21},{6,22},{7,23},{8,24},{9,... | collective-permute-start | bytes 393224 | tf_op jit(solution)/shard_map/ppermute | solution.py:28
  38.9 7.2 %near_field.7.refs_4_.refs_0_ = bf16[1024,1024]{1,0:T(8,128)(2,1)} custom-call(s32[4,16]{1,0:T(4,128)} %cols_ref.9, bf16[4,16,256,256]{3,2,1,0:T(8,128)(2,1)} %tiles_ref.9, bf16[4096,1024]{1,0:T(8,128)(2,1)} %vectors_ref.13, bf16[1024,1024]{1,0:T(8,128)(2,1)} %near_field.6.refs_2_.refs_0_, bf16[256,512]{1,0:T(8,128)(2,1)} %get-tuple-element.28.refs_1_.refs_6_), custom_call_target="tpu_custom_call" | custom-call | flops 7000000000 | bytes 1 | tf_op jit(solution)/shard_map/near_field/pallas_call | solution.py:40
  46.1 0.0 collective-permute-done.6.refs_1_
  46.1 0.0 collective-permute-done.5.refs_0_
  46.1 0.0 collective-permute-done.7.refs_2_
  46.2 0.0 collective-permute-done.8.refs_3_
  46.2 0.1 collective-permute-start.9
  46.3 1.0 %collective-permute-start.11 = (bf16[128,512]{1,0:T(8,128)(2,1)}, bf16[128,512]{1,0:T(8,128)(2,1)}, u32[]{:S(2)}, u32[]{:S(2)}) collective-permute-start(bf16[128,512]{1,0:T(8,128)(2,1)} %get-tuple-element.36.refs_0_), channel_id=1, source_target_pairs={{0,2},{1,3},{2,0},{3,1},{4,6},{5,7},{6,4},{7,5},{8,10},{9,11},{10,... | collective-permute-start | bytes 393224 | tf_op jit(solution)/shard_map/ppermute | solution.py:28
  47.3 1.3 %collective-permute-start.12 = (bf16[128,512]{1,0:T(8,128)(2,1)}, bf16[128,512]{1,0:T(8,128)(2,1)}, u32[]{:S(2)}, u32[]{:S(2)}) collective-permute-start(bf16[128,512]{1,0:T(8,128)(2,1)} %get-tuple-element.36.refs_0_), channel_id=1, source_target_pairs={{0,4},{1,5},{2,6},{3,7},{4,0},{5,1},{6,2},{7,3},{8,12},{9,13},{10,... | collective-permute-start | bytes 393224 | tf_op jit(solution)/shard_map/ppermute | solution.py:28
  48.6 1.2 %collective-permute-start.13 = (bf16[128,512]{1,0:T(8,128)(2,1)}, bf16[128,512]{1,0:T(8,128)(2,1)}, u32[]{:S(2)}, u32[]{:S(2)}) collective-permute-start(bf16[128,512]{1,0:T(8,128)(2,1)} %get-tuple-element.36.refs_0_), channel_id=1, source_target_pairs={{0,6},{1,7},{2,4},{3,5},{4,2},{5,3},{6,0},{7,1},{8,14},{9,15},{10,... | collective-permute-start | bytes 393224 | tf_op jit(solution)/shard_map/ppermute | solution.py:28
  49.8 0.0 collective-permute-done.9.refs_1_.refs_9_
  49.8 0.0 collective-permute-done.4.refs_0_
  49.8 0.0 collective-permute-start.10
  49.8 6.3 %near_field.8.refs_4_.refs_0_ = bf16[1024,1024]{1,0:T(8,128)(2,1)} custom-call(s32[4,16]{1,0:T(4,128)} %cols_ref.9, bf16[4,16,256,256]{3,2,1,0:T(8,128)(2,1)} %tiles_ref.9, bf16[4096,1024]{1,0:T(8,128)(2,1)} %vectors_ref.13, bf16[1024,1024]{1,0:T(8,128)(2,1)} %near_field.7.refs_4_.refs_0_, bf16[512,1024]{1,0:T(8,128)(2,1)} %held.10.refs_1_, ...), custom_call_target="tpu_custom_call" | custom-call | flops 10000000000 | bytes 1 | tf_op jit(solution)/shard_map/near_field/pallas_call | solution.py:40
  56.1 0.0 collective-permute-done.11.refs_1_
  56.1 0.0 collective-permute-done.12.refs_2_
  56.1 0.4 collective-permute-done.13.refs_3_
  56.5 0.2 collective-permute-start.14
  56.7 0.3 collective-permute-start.15
  57.0 0.2 collective-permute-start.16
  57.2 0.3 collective-permute-start.17
  57.5 0.7 %collective-permute-done.14.refs_7_ = bf16[128,512]{1,0:T(8,128)(2,1)} collective-permute-done((bf16[128,512]{1,0:T(8,128)(2,1)}, bf16[128,512]{1,0:T(8,128)(2,1)}, u32[]{:S(2)}, u32[]{:S(2)}) %collective-permute-start.14) | collective-permute-done | bytes 131104 | tf_op jit(solution)/shard_map/ppermute | solution.py:28
  58.2 0.2 collective-permute-done.15.refs_9_
  58.4 0.3 collective-permute-done.16.refs_11_
  58.7 0.2 collective-permute-done.17.refs_13_
  58.9 0.0 collective-permute-done.10.refs_1_
  58.9 6.1 %near_field.9 = bf16[1024,1024]{1,0:T(8,128)(2,1)} custom-call(s32[4,16]{1,0:T(4,128)} %cols_ref.9, bf16[4,16,256,256]{3,2,1,0:T(8,128)(2,1)} %tiles_ref.9, bf16[4096,1024]{1,0:T(8,128)(2,1)} %vectors_ref.13, bf16[1024,1024]{1,0:T(8,128)(2,1)} %near_field.8.refs_4_.refs_0_, bf16[512,1024]{1,0:T(8,128)(2,1)} %collective-permute-done.10.refs_1_, ...), custom_call_target="tpu_custom_call" | custom-call | flops 1 | bytes 1 | tf_op jit(solution)/shard_map/near_field/pallas_call | solution.py:40
  (6 shorter events, 0.0 us)
Async XLA Ops:
  5.7 13.3 %collective-permute-start = (bf16[384,512]{1,0:T(8,128)(2,1)}, bf16[384,512]{1,0:T(8,128)(2,1)}, u32[]{:S(2)}, u32[]{:S(2)}) collective-permute-start(bf16[384,512]{1,0:T(8,128)(2,1)} %get-tuple-element.24), channel_id=1, source_target_pairs={{0,4},{1,5},{2,6},{3,7},{4,0},{5,1},{6,2},{7,3},{8,12},{9,13},{10,... | collective-permute-start | bytes 1179656 | tf_op jit(solution)/shard_map/ppermute | solution.py:28
  11.5 13.8 %collective-permute-start.1 = (bf16[2,1024,128]{2,1,0:T(8,128)(2,1)}, bf16[2,1024,128]{2,1,0:T(8,128)(2,1)}, u32[]{:S(2)}, u32[]{:S(2)}) collective-permute-start(bf16[2,1024,128]{2,1,0:T(8,128)(2,1)} %get-tuple-element.25), channel_id=1, source_target_pairs={{0,2},{1,3},{2,0},{3,1},{4,6},{5,7},{6,4},{7,5},{8,10},{9,11},{10,... | collective-permute-start | bytes 1572872 | tf_op jit(solution)/shard_map/ppermute | solution.py:28
  19.0 13.7 %collective-permute-start.2 = (bf16[2,1024,128]{2,1,0:T(8,128)(2,1)}, bf16[2,1024,128]{2,1,0:T(8,128)(2,1)}, u32[]{:S(2)}, u32[]{:S(2)}) collective-permute-start(bf16[2,1024,128]{2,1,0:T(8,128)(2,1)} %get-tuple-element.26), channel_id=1, source_target_pairs={{0,1},{1,0},{2,3},{3,2},{4,5},{5,4},{6,7},{7,6},{8,9},{9,8},{10,11... | collective-permute-start | bytes 1572872 | tf_op jit(solution)/shard_map/ppermute | solution.py:28
  21.1 12.2 %collective-permute-start.3 = (bf16[384,512]{1,0:T(8,128)(2,1)}, bf16[384,512]{1,0:T(8,128)(2,1)}, u32[]{:S(2)}, u32[]{:S(2)}) collective-permute-start(bf16[384,512]{1,0:T(8,128)(2,1)} %add_convert_fusion.refs_1_.refs_0_), channel_id=1, source_target_pairs={{0,8},{1,9},{2,10},{3,11},{4,12},{5,13},{6,14},{7,15},{8,0},{9,1},... | collective-permute-start | bytes 1179656 | tf_op jit(solution)/shard_map/ppermute | solution.py:28
  22.5 27.3 %collective-permute-start.4 = (bf16[512,1024]{1,0:T(8,128)(2,1)}, bf16[512,1024]{1,0:T(8,128)(2,1)}, u32[]{:S(2)}, u32[]{:S(2)}) collective-permute-start(bf16[512,1024]{1,0:T(8,128)(2,1)} %held.8), channel_id=1, source_target_pairs={{0,5},{2,7},{4,9},{5,0},{6,11},{7,2},{8,13},{9,4},{10,15},{11,6},{... | collective-permute-start | bytes 3145736 | tf_op jit(solution)/shard_map/ppermute | solution.py:28
  24.7 21.4 %collective-permute-start.6 = (bf16[2,1024,128]{2,1,0:T(8,128)(2,1)}, bf16[2,1024,128]{2,1,0:T(8,128)(2,1)}, u32[]{:S(2)}, u32[]{:S(2)}) collective-permute-start(bf16[2,1024,128]{2,1,0:T(8,128)(2,1)} %get-tuple-element.31), channel_id=1, source_target_pairs={{0,3},{1,2},{2,1},{3,0},{4,7},{5,6},{6,5},{7,4},{8,11},{9,10},{10,... | collective-permute-start | bytes 1572872 | tf_op jit(solution)/shard_map/ppermute | solution.py:28
  35.1 11.0 %collective-permute-start.7 = (bf16[256,512]{1,0:T(8,128)(2,1)}, bf16[256,512]{1,0:T(8,128)(2,1)}, u32[]{:S(2)}, u32[]{:S(2)}) collective-permute-start(bf16[256,512]{1,0:T(8,128)(2,1)} %get-tuple-element.28.refs_1_.refs_6_), channel_id=1, source_target_pairs={{0,1},{1,0},{2,3},{3,2},{4,5},{5,4},{6,7},{7,6},{8,9},{9,8},{10,11... | collective-permute-start | bytes 786440 | tf_op jit(solution)/shard_map/ppermute | solution.py:28
  35.2 11.0 %collective-permute-start.8 = (bf16[256,512]{1,0:T(8,128)(2,1)}, bf16[256,512]{1,0:T(8,128)(2,1)}, u32[]{:S(2)}, u32[]{:S(2)}) collective-permute-start(bf16[256,512]{1,0:T(8,128)(2,1)} %get-tuple-element.28.refs_1_.refs_6_), channel_id=1, source_target_pairs={{0,2},{1,3},{2,0},{3,1},{4,6},{5,7},{6,4},{7,5},{8,10},{9,11},{10,... | collective-permute-start | bytes 786440 | tf_op jit(solution)/shard_map/ppermute | solution.py:28
  36.2 10.0 %collective-permute-start.5 = (bf16[128,512]{1,0:T(8,128)(2,1)}, bf16[128,512]{1,0:T(8,128)(2,1)}, u32[]{:S(2)}, u32[]{:S(2)}) collective-permute-start(bf16[128,512]{1,0:T(8,128)(2,1)} %get-tuple-element.30), channel_id=1, source_target_pairs={{0,16},{1,17},{2,18},{3,19},{4,20},{5,21},{6,22},{7,23},{8,24},{9,... | collective-permute-start | bytes 393224 | tf_op jit(solution)/shard_map/ppermute | solution.py:28
  46.2 3.6 %collective-permute-start.9 = (bf16[256,512]{1,0:T(8,128)(2,1)}, bf16[256,512]{1,0:T(8,128)(2,1)}, u32[]{:S(2)}, u32[]{:S(2)}) collective-permute-start(bf16[256,512]{1,0:T(8,128)(2,1)} %get-tuple-element.32.refs_8_), channel_id=1, source_target_pairs={{0,1},{1,0},{2,3},{3,2},{4,5},{5,4},{6,7},{7,6},{8,9},{9,8},{10,11... | collective-permute-start | bytes 786440 | tf_op jit(solution)/shard_map/ppermute | solution.py:28
  46.3 9.8 %collective-permute-start.11 = (bf16[128,512]{1,0:T(8,128)(2,1)}, bf16[128,512]{1,0:T(8,128)(2,1)}, u32[]{:S(2)}, u32[]{:S(2)}) collective-permute-start(bf16[128,512]{1,0:T(8,128)(2,1)} %get-tuple-element.36.refs_0_), channel_id=1, source_target_pairs={{0,2},{1,3},{2,0},{3,1},{4,6},{5,7},{6,4},{7,5},{8,10},{9,11},{10,... | collective-permute-start | bytes 393224 | tf_op jit(solution)/shard_map/ppermute | solution.py:28
  47.3 8.8 %collective-permute-start.12 = (bf16[128,512]{1,0:T(8,128)(2,1)}, bf16[128,512]{1,0:T(8,128)(2,1)}, u32[]{:S(2)}, u32[]{:S(2)}) collective-permute-start(bf16[128,512]{1,0:T(8,128)(2,1)} %get-tuple-element.36.refs_0_), channel_id=1, source_target_pairs={{0,4},{1,5},{2,6},{3,7},{4,0},{5,1},{6,2},{7,3},{8,12},{9,13},{10,... | collective-permute-start | bytes 393224 | tf_op jit(solution)/shard_map/ppermute | solution.py:28
  48.6 7.9 %collective-permute-start.13 = (bf16[128,512]{1,0:T(8,128)(2,1)}, bf16[128,512]{1,0:T(8,128)(2,1)}, u32[]{:S(2)}, u32[]{:S(2)}) collective-permute-start(bf16[128,512]{1,0:T(8,128)(2,1)} %get-tuple-element.36.refs_0_), channel_id=1, source_target_pairs={{0,6},{1,7},{2,4},{3,5},{4,2},{5,3},{6,0},{7,1},{8,14},{9,15},{10,... | collective-permute-start | bytes 393224 | tf_op jit(solution)/shard_map/ppermute | solution.py:28
  49.8 9.1 %collective-permute-start.10 = (bf16[512,1024]{1,0:T(8,128)(2,1)}, bf16[512,1024]{1,0:T(8,128)(2,1)}, u32[]{:S(2)}, u32[]{:S(2)}) collective-permute-start(bf16[512,1024]{1,0:T(8,128)(2,1)} %held.10.refs_1_), channel_id=1, source_target_pairs={{0,1},{1,0},{2,3},{3,2},{4,5},{5,4},{6,7},{7,6},{8,9},{9,8},{10,11... | collective-permute-start | bytes 3145736 | tf_op jit(solution)/shard_map/ppermute | solution.py:28
  56.5 1.7 %collective-permute-start.14 = (bf16[128,512]{1,0:T(8,128)(2,1)}, bf16[128,512]{1,0:T(8,128)(2,1)}, u32[]{:S(2)}, u32[]{:S(2)}) collective-permute-start(bf16[128,512]{1,0:T(8,128)(2,1)} %get-tuple-element.37.refs_6_), channel_id=1, source_target_pairs={{0,1},{1,0},{2,3},{3,2},{4,5},{5,4},{6,7},{7,6},{8,9},{9,8},{10,11... | collective-permute-start | bytes 393224 | tf_op jit(solution)/shard_map/ppermute | solution.py:28
  56.7 1.7 %collective-permute-start.15 = (bf16[128,512]{1,0:T(8,128)(2,1)}, bf16[128,512]{1,0:T(8,128)(2,1)}, u32[]{:S(2)}, u32[]{:S(2)}) collective-permute-start(bf16[128,512]{1,0:T(8,128)(2,1)} %get-tuple-element.38.refs_8_), channel_id=1, source_target_pairs={{0,1},{1,0},{2,3},{3,2},{4,5},{5,4},{6,7},{7,6},{8,9},{9,8},{10,11... | collective-permute-start | bytes 393224 | tf_op jit(solution)/shard_map/ppermute | solution.py:28
  57.0 1.7 %collective-permute-start.16 = (bf16[128,512]{1,0:T(8,128)(2,1)}, bf16[128,512]{1,0:T(8,128)(2,1)}, u32[]{:S(2)}, u32[]{:S(2)}) collective-permute-start(bf16[128,512]{1,0:T(8,128)(2,1)} %get-tuple-element.39.refs_10_), channel_id=1, source_target_pairs={{0,1},{1,0},{2,3},{3,2},{4,5},{5,4},{6,7},{7,6},{8,9},{9,8},{10,11... | collective-permute-start | bytes 393224 | tf_op jit(solution)/shard_map/ppermute | solution.py:28
  57.2 1.7 %collective-permute-start.17 = (bf16[128,512]{1,0:T(8,128)(2,1)}, bf16[128,512]{1,0:T(8,128)(2,1)}, u32[]{:S(2)}, u32[]{:S(2)}) collective-permute-start(bf16[128,512]{1,0:T(8,128)(2,1)} %get-tuple-element.40.refs_12_), channel_id=1, source_target_pairs={{0,1},{1,0},{2,3},{3,2},{4,5},{5,4},{6,7},{7,6},{8,9},{9,8},{10,11... | collective-permute-start | bytes 393224 | tf_op jit(solution)/shard_map/ppermute | solution.py:28
